TPU v7x, 32 devices: a whole 2x2x4 slice. The times are simulated.
32 devices in a mesh: batch: 4 (over y, x), ctx: 8 (over z, core).
Axes of the slice: x: 2, y: 2, z: 4, core: 2. Of those that a mesh axis runs over, the one named last changes fastest.
Arguments:
- tokens: bfloat16 [4096, 768], P(('batch', 'ctx')), may hold values from -12 to 12
- lengths: int32 [4], P('batch'), may hold values from 897 to 1024
- w_query: bfloat16 [768, 768], P(('batch', 'ctx')), may hold values from -0.21875 to 0.21875
- b_query: bfloat16 [768], P(('batch', 'ctx')), may hold values from -3 to 3
- w_key: bfloat16 [768, 768], P(('batch', 'ctx')), may hold values from -0.21875 to 0.21875
- w_value: bfloat16 [768, 768], P(('batch', 'ctx')), may hold values from -0.21875 to 0.21875
- b_value: bfloat16 [768], P(('batch', 'ctx')), may hold values from -0.1875 to 0.1875
- w_out: bfloat16 [768, 768], P(('batch', 'ctx')), may hold values from -7 to 7
- b_out: bfloat16 [768], P(('batch', 'ctx')), may hold values from -3 to 3
- gain_one: bfloat16 [768], P(('batch', 'ctx')), may hold values from 0.5 to 1.5
- shift_one: bfloat16 [768], P(('batch', 'ctx')), may hold values from -1.75 to 1.75
- w_up: bfloat16 [768, 3072], P(('batch', 'ctx')), may hold values from -0.21875 to 0.21875
- b_up: bfloat16 [3072], P(('batch', 'ctx')), may hold values from -3 to 3
- w_down: bfloat16 [3072, 768], P(('batch', 'ctx')), may hold values from -0.15625 to 0.15625
- b_down: bfloat16 [768], P(('batch', 'ctx')), may hold values from -1.75 to 1.75
- gain_two: bfloat16 [768], P(('batch', 'ctx')), may hold values from 0.5 to 1.5
- shift_two: bfloat16 [768], P(('batch', 'ctx')), may hold values from -3 to 3
- cotangent: bfloat16 [4096, 768], P(('batch', 'ctx')), may hold values from -6 to 6
Outputs:
- output: bfloat16 [4096, 768], P(('batch', 'ctx'))
- grad_tokens: bfloat16 [4096, 768], P(('batch', 'ctx'))
- grad_w_query: float32 [768, 768], P(('batch', 'ctx'))
- grad_b_query: float32 [768], P(('batch', 'ctx'))
- grad_w_key: float32 [768, 768], P(('batch', 'ctx'))
- grad_w_value: float32 [768, 768], P(('batch', 'ctx'))
- grad_b_value: float32 [768], P(('batch', 'ctx'))
- grad_w_out: float32 [768, 768], P(('batch', 'ctx'))
- grad_b_out: float32 [768], P(('batch', 'ctx'))
- grad_gain_one: float32 [768], P(('batch', 'ctx'))
- grad_shift_one: float32 [768], P(('batch', 'ctx'))
- grad_w_up: float32 [768, 3072], P(('batch', 'ctx'))
- grad_b_up: float32 [3072], P(('batch', 'ctx'))
- grad_w_down: float32 [3072, 768], P(('batch', 'ctx'))
- grad_b_down: float32 [768], P(('batch', 'ctx'))
- grad_gain_two: float32 [768], P(('batch', 'ctx'))
- grad_shift_two: float32 [768], P(('batch', 'ctx'))
Inputs may be any that keep to these rules, and one draw needn't show every extreme that they name: `lengths`: valid positions of each sequence; positions from this length on are padding.
All inputs are finite; a program needn't handle non-finite values.
Results may differ from a plain program's by a relative error of at most 0.025.
Values may be sent and summed in bfloat16 or wider, within the bound.
No kernel may reach another device: no remote copies, remote signals or barrier semaphores. Data moves between devices by JAX's collectives and lax.ppermute only.
A program may use at most 128 MiB of HBM per device.

v0:
```python
import jax
import jax.numpy as jnp
from jax import lax
from jax.sharding import PartitionSpec as P

HEADS = 12
HEAD_DIM = 64


epsilon = 1e-06
masked_score = -1e30


def shifted(block, axis, distance):
    devices = range(lax.axis_size(axis))
    route = [((i - distance) % len(devices), i) for i in devices]
    return lax.ppermute(block, axis, route)


def normalize(resid, gain, shift):
    center = resid - jnp.mean(resid, -1, keepdims=True)
    spread = jnp.mean(center * center, -1, keepdims=True)
    return center * lax.rsqrt(spread + epsilon) * gain + shift


def gelu_exact(value):
    return jax.nn.gelu(value, approximate=False)


def head_scores(query_blk, key_blk, owner, length):
    count = key_blk.shape[0]
    raw = jnp.einsum(
        "qhd,khd->hqk",
        query_blk.reshape(-1, HEADS, HEAD_DIM),
        key_blk.reshape(count, HEADS, HEAD_DIM),
        preferred_element_type=jnp.float32,
    )
    position = owner * count + jnp.arange(count, dtype=jnp.int32)
    return jnp.where((position < length)[None, None, :], raw * HEAD_DIM ** (-0.5), masked_score)


def block_grads(query_blk, grad_blk, log_blk, delta_blk, key_blk, value_blk, owner, length):
    rows = query_blk.shape[0]
    count = key_blk.shape[0]
    scores = head_scores(query_blk, key_blk, owner, length)
    probs = jnp.exp(scores - log_blk[:, :, None])
    probs_low = probs.astype(jnp.bfloat16)
    grad_heads = grad_blk.reshape(rows, HEADS, HEAD_DIM)
    query_heads = query_blk.reshape(rows, HEADS, HEAD_DIM)
    key_heads = key_blk.reshape(count, HEADS, HEAD_DIM)
    value_heads = value_blk.reshape(count, HEADS, HEAD_DIM)
    prob_grad = jnp.einsum(
        "qhd,khd->hqk", grad_heads, value_heads, preferred_element_type=jnp.float32
    )
    score_grad = (probs * (prob_grad - delta_blk[:, :, None])).astype(jnp.bfloat16)
    value_term = jnp.einsum(
        "hqk,qhd->khd", probs_low, grad_heads, preferred_element_type=jnp.float32
    )
    key_term = jnp.einsum(
        "hqk,qhd->khd", score_grad, query_heads, preferred_element_type=jnp.float32
    ) * HEAD_DIM ** (-0.5)
    query_term = jnp.einsum(
        "hqk,khd->qhd", score_grad, key_heads, preferred_element_type=jnp.float32
    ) * HEAD_DIM ** (-0.5)
    return (
        query_term.reshape(rows, -1),
        key_term.reshape(count, -1),
        value_term.reshape(count, -1),
    )


def body(
    tokens,
    lengths,
    w_query,
    b_query,
    w_key,
    w_value,
    b_value,
    w_out,
    b_out,
    gain_one,
    shift_one,
    w_up,
    b_up,
    w_down,
    b_down,
    gain_two,
    shift_two,
    cotangent,
):
    cycle = lax.axis_size("ctx")
    place = lax.axis_index("ctx")
    length = lengths[0]
    rows = tokens.shape[0]
    width = tokens.shape[1]
    gathered = (
        lax.all_gather(w_query, ("batch", "ctx"), axis=0, tiled=True),
        lax.all_gather(w_key, ("batch", "ctx"), axis=0, tiled=True),
        lax.all_gather(w_value, ("batch", "ctx"), axis=0, tiled=True),
        lax.all_gather(w_out, ("batch", "ctx"), axis=0, tiled=True),
        lax.all_gather(w_up, ("batch", "ctx"), axis=0, tiled=True),
        lax.all_gather(w_down, ("batch", "ctx"), axis=0, tiled=True),
        lax.all_gather(b_query, ("batch", "ctx"), axis=0, tiled=True),
        lax.all_gather(b_value, ("batch", "ctx"), axis=0, tiled=True),
        lax.all_gather(b_out, ("batch", "ctx"), axis=0, tiled=True),
        lax.all_gather(gain_one, ("batch", "ctx"), axis=0, tiled=True),
        lax.all_gather(shift_one, ("batch", "ctx"), axis=0, tiled=True),
        lax.all_gather(b_up, ("batch", "ctx"), axis=0, tiled=True),
        lax.all_gather(b_down, ("batch", "ctx"), axis=0, tiled=True),
        lax.all_gather(gain_two, ("batch", "ctx"), axis=0, tiled=True),
        lax.all_gather(shift_two, ("batch", "ctx"), axis=0, tiled=True),
    )
    query_full, key_full, value_full, out_full, up_full, down_full = gathered[:6]
    small = [item.astype(jnp.float32) for item in gathered[6:]]
    (
        bias_query,
        bias_value,
        bias_out,
        gain_first,
        shift_first,
        bias_up,
        bias_down,
        gain_second,
        shift_second,
    ) = small
    query_low = (
        jnp.dot(tokens, query_full, preferred_element_type=jnp.float32) + bias_query
    ).astype(jnp.bfloat16)
    key_low = jnp.dot(tokens, key_full, preferred_element_type=jnp.float32).astype(jnp.bfloat16)
    value_low = (
        jnp.dot(tokens, value_full, preferred_element_type=jnp.float32) + bias_value
    ).astype(jnp.bfloat16)
    start_top = jnp.full((HEADS, rows), masked_score, jnp.float32)
    start_total = jnp.zeros((HEADS, rows), jnp.float32)
    start_sum = jnp.zeros((rows, HEADS, HEAD_DIM), jnp.float32)

    def running(state, pair, owner):
        top, total, summed = state
        scores = head_scores(query_low, pair[0], owner, length)
        new_top = jnp.maximum(top, jnp.max(scores, -1))
        factor = jnp.exp(top - new_top)
        expos = jnp.exp(scores - new_top[:, :, None])
        total = total * factor + jnp.sum(expos, -1)
        summed = summed * factor.T[:, :, None] + jnp.einsum(
            "hqk,khd->qhd",
            expos.astype(jnp.bfloat16),
            pair[1].reshape(-1, HEADS, HEAD_DIM),
            preferred_element_type=jnp.float32,
        )
        return (new_top, total, summed)

    def run_step(step, carry):
        pair, state = carry
        state = running(state, pair, (place - step) % cycle)
        pair = shifted((pair[0], pair[1]), "ctx", 1)
        return (pair, state)

    pair, state = lax.fori_loop(
        0, cycle - 1, run_step, ((key_low, value_low), (start_top, start_total, start_sum))
    )
    top, total, summed = running(state, pair, (place + 1) % cycle)
    log_total = top + jnp.log(total)
    attended = (summed / total.T[:, :, None]).reshape(rows, width)
    mixed = attended.astype(jnp.bfloat16)
    projected = jnp.dot(mixed, out_full, preferred_element_type=jnp.float32) + bias_out
    first, first_back = jax.vjp(
        normalize, tokens.astype(jnp.float32) + projected, gain_first, shift_first
    )
    first_low = first.astype(jnp.bfloat16)
    inner = jnp.dot(first_low, up_full, preferred_element_type=jnp.float32) + bias_up
    active, gelu_back = jax.vjp(gelu_exact, inner)
    active_low = active.astype(jnp.bfloat16)
    branch = jnp.dot(active_low, down_full, preferred_element_type=jnp.float32) + bias_down
    result, second_back = jax.vjp(normalize, first + branch, gain_second, shift_second)
    output = result.astype(jnp.bfloat16)
    query_back, key_back, value_back, out_back, up_back, down_back = (
        query_full,
        key_full,
        value_full,
        out_full,
        up_full,
        down_full,
    )
    grad_second, grad_gain_two, grad_shift_two = second_back(cotangent.astype(jnp.float32))
    branch_grad = grad_second.astype(jnp.bfloat16)
    grad_b_down = jnp.sum(branch_grad.astype(jnp.float32), 0)
    grad_w_down = jnp.einsum(
        "tf,td->fd", active_low, branch_grad, preferred_element_type=jnp.float32
    )
    active_grad = jnp.einsum(
        "td,fd->tf", branch_grad, down_back, preferred_element_type=jnp.float32
    )
    inner_grad = gelu_back(active_grad)[0].astype(jnp.bfloat16)
    grad_b_up = jnp.sum(inner_grad.astype(jnp.float32), 0)
    grad_w_up = jnp.einsum("td,tf->df", first_low, inner_grad, preferred_element_type=jnp.float32)
    first_grad = (
        jnp.einsum("tf,df->td", inner_grad, up_back, preferred_element_type=jnp.float32)
        + grad_second
    )
    grad_first, grad_gain_one, grad_shift_one = first_back(first_grad)
    proj_grad = grad_first.astype(jnp.bfloat16)
    grad_b_out = jnp.sum(proj_grad.astype(jnp.float32), 0)
    grad_w_out = jnp.einsum("td,te->de", mixed, proj_grad, preferred_element_type=jnp.float32)
    mixed_grad = jnp.einsum(
        "te,de->td", proj_grad, out_back, preferred_element_type=jnp.float32
    ).astype(jnp.bfloat16)
    delta = jnp.sum(
        (mixed_grad.astype(jnp.float32) * attended).reshape(rows, HEADS, HEAD_DIM), -1
    ).T
    zeros = jnp.zeros((rows, width), jnp.float32)

    def move_key_grads(grads):
        return (
            shifted(grads[0].astype(jnp.bfloat16), "ctx", 1).astype(jnp.float32),
            shifted(grads[1].astype(jnp.bfloat16), "ctx", 1).astype(jnp.float32),
        )

    def key_step(step, carry):
        blocks, grads, query_acc = carry
        query_term, key_term, value_term = block_grads(
            query_low,
            mixed_grad,
            log_total,
            delta,
            blocks[0],
            blocks[1],
            (place - step) % cycle,
            length,
        )
        grads = move_key_grads((grads[0] + key_term, grads[1] + value_term))
        blocks = shifted((blocks[0], blocks[1]), "ctx", 1)
        return (blocks, grads, query_acc + query_term)

    blocks, grads, query_acc = lax.fori_loop(
        0, cycle - 1, key_step, ((key_low, value_low), (zeros, zeros), zeros)
    )
    query_term, key_term, value_term = block_grads(
        query_low, mixed_grad, log_total, delta, blocks[0], blocks[1], (place + 1) % cycle, length
    )
    key_acc, value_acc = move_key_grads((grads[0] + key_term, grads[1] + value_term))
    query_acc = query_acc + query_term
    query_grad = query_acc.astype(jnp.bfloat16)
    key_grad = key_acc.astype(jnp.bfloat16)
    value_grad = value_acc.astype(jnp.bfloat16)
    grad_b_query = jnp.sum(query_grad.astype(jnp.float32), 0)
    grad_b_value = jnp.sum(value_grad.astype(jnp.float32), 0)
    grad_w_query = jnp.einsum("td,te->de", tokens, query_grad, preferred_element_type=jnp.float32)
    grad_w_key = jnp.einsum("td,te->de", tokens, key_grad, preferred_element_type=jnp.float32)
    grad_w_value = jnp.einsum("td,te->de", tokens, value_grad, preferred_element_type=jnp.float32)
    token_grad = grad_first + jnp.einsum(
        "te,de->td", query_grad, query_back, preferred_element_type=jnp.float32
    )
    token_grad = token_grad + jnp.einsum(
        "te,de->td", key_grad, key_back, preferred_element_type=jnp.float32
    )
    token_grad = token_grad + jnp.einsum(
        "te,de->td", value_grad, value_back, preferred_element_type=jnp.float32
    )
    grad_tokens = token_grad.astype(jnp.bfloat16)
    sharded = (
        lax.psum_scatter(grad_w_query, ("batch", "ctx"), scatter_dimension=0, tiled=True),
        lax.psum_scatter(grad_b_query, ("batch", "ctx"), scatter_dimension=0, tiled=True),
        lax.psum_scatter(grad_w_key, ("batch", "ctx"), scatter_dimension=0, tiled=True),
        lax.psum_scatter(grad_w_value, ("batch", "ctx"), scatter_dimension=0, tiled=True),
        lax.psum_scatter(grad_b_value, ("batch", "ctx"), scatter_dimension=0, tiled=True),
        lax.psum_scatter(grad_w_out, ("batch", "ctx"), scatter_dimension=0, tiled=True),
        lax.psum_scatter(grad_b_out, ("batch", "ctx"), scatter_dimension=0, tiled=True),
        lax.psum_scatter(grad_gain_one, ("batch", "ctx"), scatter_dimension=0, tiled=True),
        lax.psum_scatter(grad_shift_one, ("batch", "ctx"), scatter_dimension=0, tiled=True),
        lax.psum_scatter(grad_w_up, ("batch", "ctx"), scatter_dimension=0, tiled=True),
        lax.psum_scatter(grad_b_up, ("batch", "ctx"), scatter_dimension=0, tiled=True),
        lax.psum_scatter(grad_w_down, ("batch", "ctx"), scatter_dimension=0, tiled=True),
        lax.psum_scatter(grad_b_down, ("batch", "ctx"), scatter_dimension=0, tiled=True),
        lax.psum_scatter(grad_gain_two, ("batch", "ctx"), scatter_dimension=0, tiled=True),
        lax.psum_scatter(grad_shift_two, ("batch", "ctx"), scatter_dimension=0, tiled=True),
    )
    return (
        output,
        grad_tokens,
        sharded[0],
        sharded[1],
        sharded[2],
        sharded[3],
        sharded[4],
        sharded[5],
        sharded[6],
        sharded[7],
        sharded[8],
        sharded[9],
        sharded[10],
        sharded[11],
        sharded[12],
        sharded[13],
        sharded[14],
    )


def solution(mesh):
    in_specs = (
        P(("batch", "ctx"), None),
        P("batch"),
        P(("batch", "ctx"), None),
        P(("batch", "ctx")),
        P(("batch", "ctx"), None),
        P(("batch", "ctx"), None),
        P(("batch", "ctx")),
        P(("batch", "ctx"), None),
        P(("batch", "ctx")),
        P(("batch", "ctx")),
        P(("batch", "ctx")),
        P(("batch", "ctx"), None),
        P(("batch", "ctx")),
        P(("batch", "ctx"), None),
        P(("batch", "ctx")),
        P(("batch", "ctx")),
        P(("batch", "ctx")),
        P(("batch", "ctx"), None),
    )
    out_specs = (
        P(("batch", "ctx"), None),
        P(("batch", "ctx"), None),
        P(("batch", "ctx"), None),
        P(("batch", "ctx")),
        P(("batch", "ctx"), None),
        P(("batch", "ctx"), None),
        P(("batch", "ctx")),
        P(("batch", "ctx"), None),
        P(("batch", "ctx")),
        P(("batch", "ctx")),
        P(("batch", "ctx")),
        P(("batch", "ctx"), None),
        P(("batch", "ctx")),
        P(("batch", "ctx"), None),
        P(("batch", "ctx")),
        P(("batch", "ctx")),
        P(("batch", "ctx")),
    )
    return jax.shard_map(body, mesh=mesh, in_specs=in_specs, out_specs=out_specs, check_vma=False)
```

profile of v0, /device:TPU:0, one launch (start us, length us, event | category | flops | bytes accessed | tf_op | source)
XLA Modules:
  0.0 1192.6 jit_solution(15248548266345240938)
XLA Ops:
  18.8 42.6 %all-reduce.19 = (bf16[3072]{0:T(1024)(128)(2,1)S(1)}, bf16[768]{0:T(1024)(128)(2,1)S(1)}, bf16[768]{0:T(1024)(128)(2,1)S(1)}, bf16[768]{0:T(1024)(128)(2,1)S(1)...) all-reduce(bf16[3072]{0:T(1024)(128)(2,1)S(1)} %dynamic-update-slic, ...), channel_id=1, replica_groups=mesh['batch'=4,'ctx'=8] {'batch','ctx'}, use_global_device_ids=true, to_apply=%add.5 | all-reduce | flops 9216 | bytes 36864
  64.0 4.2 all-gather.7.cloned.1.call-done
  68.2 1.7 convolution_convert_fusion.1
  70.1 54.4 %all-gather.9.cloned.1.call-done = bf16[768,768]{1,0:T(8,128)(2,1)} async-done(((bf16[24,768]{1,0:T(8,128)(2,1)}), bf16[768,768]{1,0:T(8,128)(2,1)}) %all-gather.9.cloned.1.call-update) | async-done | bytes 1179664 | tf_op jit(solution)/shard_map/all_gather | solution.py:100
  124.5 1.6 fusion.35
  126.3 54.4 %all-gather.11.cloned.1.call-done = bf16[768,768]{1,0:T(8,128)(2,1)} async-done(((bf16[24,768]{1,0:T(8,128)(2,1)}), bf16[768,768]{1,0:T(8,128)(2,1)}) %all-gather.11.cloned.1.call-update) | async-done | bytes 1179664 | tf_op jit(solution)/shard_map/all_gather | solution.py:98
  180.7 1.6 fusion.36
  182.4 66.4 %while.48 = (s32[]{:T(128)}, bf16[128,768]{0,1:T(8,128)(2,1)S(1)}, bf16[128,768]{0,1:T(8,128)(2,1)S(1)}, f32[12,128]{1,0:T(8,128)S(1)}, f32[12,128]{1,0:T(8,128)...) while((s32[]{:T(128)}, bf16[128,768]{0,1:T(8,128)(2,1)S(1)}, ...), condition=%wide.region_3.4_spmd.clone, body=%wide.region_0.3_spmd.clone.sunk | while | flops 52012304 | bytes 6193774 | solution.py:159
  184.7 4.7 collective-permute-done
  189.4 2.1 collective-permute-done.1
  193.2 5.6 collective-permute-done
  198.7 2.3 collective-permute-done.1
  202.7 5.3 collective-permute-done
  208.0 2.1 collective-permute-done.1
  211.7 5.9 collective-permute-done
  217.7 2.5 collective-permute-done.1
  221.8 5.3 collective-permute-done
  227.1 2.3 collective-permute-done.1
  231.1 6.4 collective-permute-done
  237.5 2.3 collective-permute-done.1
  241.4 5.3 collective-permute-done
  246.7 2.1 collective-permute-done.1
  250.4 1.7 fusion.67
  252.9 52.4 %all-gather.15.cloned.1.call-done = bf16[768,3072]{1,0:T(8,128)(2,1)} async-done(((bf16[24,3072]{1,0:T(8,128)(2,1)}), bf16[768,3072]{1,0:T(8,128)(2,1)}) %all-gather.15.cloned.1.call-update) | async-done | bytes 4718608 | tf_op jit(solution)/shard_map/all_gather | solution.py:102
  305.3 8.4 multiply_convert_fusion
  313.7 57.0 %all-gather.17.cloned.1.call-done = bf16[3072,768]{1,0:T(8,128)(2,1)} async-done(((bf16[96,768]{1,0:T(8,128)(2,1)}), bf16[3072,768]{1,0:T(8,128)(2,1)}) %all-gather.17.cloned.1.call-update) | async-done | bytes 4718608 | tf_op jit(solution)/shard_map/all_gather | solution.py:103
  370.7 3.4 fusion.68
  376.8 2.5 convert_reduce_fusion
  379.3 2.4 multiply_reduce_fusion
  384.4 101.4 %while.49 = (s32[]{:T(128)}, bf16[128,768]{0,1:T(8,128)(2,1)S(1)}, bf16[128,768]{0,1:T(8,128)(2,1)S(1)}, f32[128,768]{0,1:T(8,128)S(1)}, f32[128,768]{0,1:T(8,12...) while((s32[]{:T(128)}, bf16[128,768]{0,1:T(8,128)(2,1)S(1)}, ...), condition=%wide.region_16.17_spmd.clone, body=%wide.region_15.16_spmd.clone.sunk | while | flops 128385296 | bytes 14365398 | solution.py:235
  385.0 1.8 collective-permute-start.3
  391.1 5.2 collective-permute-done.4
  396.3 2.2 collective-permute-done.5
  403.7 7.0 collective-permute-done.4
  410.7 2.2 collective-permute-done.5
  417.4 7.6 collective-permute-done.4
  425.1 2.2 collective-permute-done.5
  431.8 7.6 collective-permute-done.4
  439.4 2.2 collective-permute-done.5
  446.2 7.6 collective-permute-done.4
  453.8 2.2 collective-permute-done.5
  460.6 7.6 collective-permute-done.4
  468.2 2.2 collective-permute-done.5
  475.0 7.6 collective-permute-done.4
  482.6 2.2 collective-permute-done.5
  487.7 1.9 convolution_bitcast_fusion.3
  489.6 3.1 copy.107
  493.7 1.9 fusion.51
  496.2 6.9 collective-permute-done.6
  503.0 1.9 convolution_bitcast_fusion.2
  504.9 3.2 copy.109
  509.7 6.9 collective-permute-done.7
  516.6 1.9 convolution_bitcast_fusion.1
  518.5 3.1 copy.111
  522.7 5.2 fusion.58
  529.1 5.1 fusion.70
  535.5 1.3 convolution_add_fusion.2
  537.0 37.9 %all-reduce.18 = (f32[768]{0:T(1024)S(1)}, f32[768]{0:T(1024)S(1)}, f32[768]{0:T(1024)S(1)}, f32[768]{0:T(1024)S(1)}, f32[768]{0:T(1024)S(1)}, /*index=5*/f32[30...) all-reduce(f32[768]{0:T(1024)S(1)} %get-tuple-element.800, ...), channel_id=3, replica_groups=mesh['batch'=4,'ctx'=8] {'batch','ctx'}, use_global_device_ids=true, to_apply=%region_19.20.clone | all-reduce | flops 9216 | bytes 73728
  582.0 7.4 reduce-scatter.19.cloned.1.call-done
  589.4 104.8 %reduce-scatter.13.cloned.1.call-done = f32[24,768]{1,0:T(8,128)} async-done(((f32[768,768]{1,0:T(8,128)}), f32[24,768]{1,0:T(8,128)}) %reduce-scatter.13.cloned.1.call-update) | async-done | bytes 73744 | tf_op jit(solution)/shard_map/reduce_scatter | solution.py:267
  694.2 103.9 %reduce-scatter.21.cloned.1.call-done = f32[24,768]{1,0:T(8,128)} async-done(((f32[768,768]{1,0:T(8,128)}), f32[24,768]{1,0:T(8,128)}) %reduce-scatter.21.cloned.1.call-update) | async-done | bytes 73744
  798.1 104.7 %reduce-scatter.23.cloned.1.call-done = f32[24,768]{1,0:T(8,128)} async-done(((f32[768,768]{1,0:T(8,128)}), f32[24,768]{1,0:T(8,128)}) %reduce-scatter.23.cloned.1.call-update) | async-done | bytes 73744
  902.8 141.1 %reduce-scatter.15.cloned.1.call-done = f32[24,3072]{1,0:T(8,128)} async-done(((f32[768,3072]{1,0:T(8,128)}), f32[24,3072]{1,0:T(8,128)}) %reduce-scatter.15.cloned.1.call-update) | async-done | bytes 294928 | tf_op jit(solution)/shard_map/reduce_scatter | solution.py:271
  1043.9 141.8 %reduce-scatter.17.cloned.1.call-done = f32[96,768]{1,0:T(8,128)} async-done(((f32[3072,768]{1,0:T(8,128)}), f32[96,768]{1,0:T(8,128)}) %reduce-scatter.17.cloned.1.call-update) | async-done | bytes 294928 | tf_op jit(solution)/shard_map/reduce_scatter | solution.py:273
  (410 shorter events, 81.5 us)
Async XLA Ops:
  7.2 117.3 %copy-start = (bf16[128,768]{1,0:T(8,128)(2,1)S(1)}, bf16[128,768]{1,0:T(8,128)(2,1)}, u32[]{:S(2)}) copy-start(bf16[128,768]{1,0:T(8,128)(2,1)} %param.22) | copy-start | bytes 589828
  7.2 61.0 %all-gather.7.cloned.1.call-start = ((), (), s32[]{:S(2)}) async-start(), calls=%async_computation.6 | async-start | bytes 1216512 | tf_op jit(solution)/shard_map/all_gather | solution.py:99
  7.9 116.6 %all-gather.9.cloned.1.call-start = ((), (), s32[]{:S(2)}) async-start(), calls=%async_computation.7 | async-start | bytes 1216512 | tf_op jit(solution)/shard_map/all_gather | solution.py:100
  8.7 172.0 %all-gather.11.cloned.1.call-start = ((), (), s32[]{:S(2)}) async-start(), calls=%async_computation.8 | async-start | bytes 1216512 | tf_op jit(solution)/shard_map/all_gather | solution.py:98
  9.4 240.9 %all-gather.13.cloned.1.call-start = ((), (), s32[]{:S(2)}) async-start(), calls=%async_computation.9 | async-start | bytes 1216512 | tf_op jit(solution)/shard_map/all_gather | solution.py:101
  10.0 295.3 %all-gather.15.cloned.1.call-start = ((), (), s32[]{:S(2)}) async-start(), calls=%async_computation.10 | async-start | bytes 4866048 | tf_op jit(solution)/shard_map/all_gather | solution.py:102
  10.6 360.1 %all-gather.17.cloned.1.call-start = ((), (), s32[]{:S(2)}) async-start(), calls=%async_computation.11 | async-start | bytes 4866048 | tf_op jit(solution)/shard_map/all_gather | solution.py:103
  11.2 578.2 %reduce-scatter.19.cloned.1.call-start = ((), (), s32[]{:S(2)}) async-start(), calls=%async_computation.15 | async-start | bytes 2433024
  63.9 184.8 %copy-start.35 = (pred[128]{0:T(512)(128)(4,1)}, pred[128]{0:T(512)(128)(4,1)S(1)}, u32[]{:S(2)}) copy-start(pred[128]{0:T(512)(128)(4,1)S(1)} %add_compare_fusion.2) | copy-start | bytes 388
  182.5 6.9 collective-permute-start
  182.8 8.7 collective-permute-start.1
  191.5 7.2 collective-permute-start
  191.6 9.4 collective-permute-start.1
  201.0 6.9 collective-permute-start
  201.1 9.0 collective-permute-start.1
  210.1 7.5 collective-permute-start
  210.2 10.0 collective-permute-start.1
  220.2 6.9 collective-permute-start
  220.3 9.1 collective-permute-start.1
  229.4 8.0 collective-permute-start
  229.5 10.2 collective-permute-start.1
  239.7 6.9 collective-permute-start
  239.8 9.0 collective-permute-start.1
  252.1 129.5 %copy-start.21 = (f32[128]{0:T(128)}, f32[128]{0:T(128)S(1)}, u32[]{:S(2)}) copy-start(f32[128]{0:T(128)S(1)} %broadcast_multiply_fusion.1) | copy-start | bytes 1540
  313.7 60.4 %copy-start.5 = (bf16[128,3072]{1,0:T(8,128)(2,1)}, bf16[128,3072]{1,0:T(8,128)(2,1)S(1)}, u32[]{:S(2)}) copy-start(bf16[128,3072]{1,0:T(8,128)(2,1)S(1)} %get-tuple-element.806) | copy-start | bytes 2359300
  370.7 6.0 slice-start
  384.7 14.8 %collective-permute-start.2 = (bf16[128,768]{0,1:T(8,128)(2,1)S(1)}, bf16[128,768]{0,1:T(8,128)(2,1)S(1)}, u32[]{:S(2)}, u32[]{:S(2)}) collective-permute-start(bf16[128,768]{0,1:T(8,128)(2,1)S(1)} %copy.147), channel_id=1, source_target_pairs={{7,0},{0,1},{1,2},{2,3},{3,4},{4,5},{5,6},{6,7},{15,8},{8,9},{9,10... | collective-permute-start | bytes 589832 | tf_op jit(solution)/shard_map/while/body/eval_jaxpr/ppermute | solution.py:17
  385.0 14.4 %collective-permute-start.3 = (bf16[128,768]{0,1:T(8,128)(2,1)S(1)}, bf16[128,768]{0,1:T(8,128)(2,1)S(1)}, u32[]{:S(2)}, u32[]{:S(2)}) collective-permute-start(bf16[128,768]{0,1:T(8,128)(2,1)S(1)} %copy.148), channel_id=1, source_target_pairs={{7,0},{0,1},{1,2},{2,3},{3,4},{4,5},{5,6},{6,7},{15,8},{8,9},{9,10... | collective-permute-start | bytes 589832 | tf_op jit(solution)/shard_map/while/body/eval_jaxpr/ppermute | solution.py:17
  389.3 6.9 collective-permute-start.4
  389.9 8.5 collective-permute-start.5
  399.5 14.3 %collective-permute-start.2 = (bf16[128,768]{0,1:T(8,128)(2,1)S(1)}, bf16[128,768]{0,1:T(8,128)(2,1)S(1)}, u32[]{:S(2)}, u32[]{:S(2)}) collective-permute-start(bf16[128,768]{0,1:T(8,128)(2,1)S(1)} %copy.147), channel_id=1, source_target_pairs={{7,0},{0,1},{1,2},{2,3},{3,4},{4,5},{5,6},{6,7},{15,8},{8,9},{9,10... | collective-permute-start | bytes 589832 | tf_op jit(solution)/shard_map/while/body/eval_jaxpr/ppermute | solution.py:17
  399.6 14.3 %collective-permute-start.3 = (bf16[128,768]{0,1:T(8,128)(2,1)S(1)}, bf16[128,768]{0,1:T(8,128)(2,1)S(1)}, u32[]{:S(2)}, u32[]{:S(2)}) collective-permute-start(bf16[128,768]{0,1:T(8,128)(2,1)S(1)} %copy.148), channel_id=1, source_target_pairs={{7,0},{0,1},{1,2},{2,3},{3,4},{4,5},{5,6},{6,7},{15,8},{8,9},{9,10... | collective-permute-start | bytes 589832 | tf_op jit(solution)/shard_map/while/body/eval_jaxpr/ppermute | solution.py:17
  402.2 8.5 collective-permute-start.4
  402.5 10.3 collective-permute-start.5
  413.9 14.3 %collective-permute-start.2 = (bf16[128,768]{0,1:T(8,128)(2,1)S(1)}, bf16[128,768]{0,1:T(8,128)(2,1)S(1)}, u32[]{:S(2)}, u32[]{:S(2)}) collective-permute-start(bf16[128,768]{0,1:T(8,128)(2,1)S(1)} %copy.147), channel_id=1, source_target_pairs={{7,0},{0,1},{1,2},{2,3},{3,4},{4,5},{5,6},{6,7},{15,8},{8,9},{9,10... | collective-permute-start | bytes 589832 | tf_op jit(solution)/shard_map/while/body/eval_jaxpr/ppermute | solution.py:17
  414.0 14.3 %collective-permute-start.3 = (bf16[128,768]{0,1:T(8,128)(2,1)S(1)}, bf16[128,768]{0,1:T(8,128)(2,1)S(1)}, u32[]{:S(2)}, u32[]{:S(2)}) collective-permute-start(bf16[128,768]{0,1:T(8,128)(2,1)S(1)} %copy.148), channel_id=1, source_target_pairs={{7,0},{0,1},{1,2},{2,3},{3,4},{4,5},{5,6},{6,7},{15,8},{8,9},{9,10... | collective-permute-start | bytes 589832 | tf_op jit(solution)/shard_map/while/body/eval_jaxpr/ppermute | solution.py:17
  416.6 8.5 collective-permute-start.4
  416.9 10.3 collective-permute-start.5
  428.3 14.3 %collective-permute-start.2 = (bf16[128,768]{0,1:T(8,128)(2,1)S(1)}, bf16[128,768]{0,1:T(8,128)(2,1)S(1)}, u32[]{:S(2)}, u32[]{:S(2)}) collective-permute-start(bf16[128,768]{0,1:T(8,128)(2,1)S(1)} %copy.147), channel_id=1, source_target_pairs={{7,0},{0,1},{1,2},{2,3},{3,4},{4,5},{5,6},{6,7},{15,8},{8,9},{9,10... | collective-permute-start | bytes 589832 | tf_op jit(solution)/shard_map/while/body/eval_jaxpr/ppermute | solution.py:17
  428.3 14.3 %collective-permute-start.3 = (bf16[128,768]{0,1:T(8,128)(2,1)S(1)}, bf16[128,768]{0,1:T(8,128)(2,1)S(1)}, u32[]{:S(2)}, u32[]{:S(2)}) collective-permute-start(bf16[128,768]{0,1:T(8,128)(2,1)S(1)} %copy.148), channel_id=1, source_target_pairs={{7,0},{0,1},{1,2},{2,3},{3,4},{4,5},{5,6},{6,7},{15,8},{8,9},{9,10... | collective-permute-start | bytes 589832 | tf_op jit(solution)/shard_map/while/body/eval_jaxpr/ppermute | solution.py:17
  431.0 8.5 collective-permute-start.4
  431.3 10.3 collective-permute-start.5
  442.6 14.3 %collective-permute-start.2 = (bf16[128,768]{0,1:T(8,128)(2,1)S(1)}, bf16[128,768]{0,1:T(8,128)(2,1)S(1)}, u32[]{:S(2)}, u32[]{:S(2)}) collective-permute-start(bf16[128,768]{0,1:T(8,128)(2,1)S(1)} %copy.147), channel_id=1, source_target_pairs={{7,0},{0,1},{1,2},{2,3},{3,4},{4,5},{5,6},{6,7},{15,8},{8,9},{9,10... | collective-permute-start | bytes 589832 | tf_op jit(solution)/shard_map/while/body/eval_jaxpr/ppermute | solution.py:17
  442.7 14.3 %collective-permute-start.3 = (bf16[128,768]{0,1:T(8,128)(2,1)S(1)}, bf16[128,768]{0,1:T(8,128)(2,1)S(1)}, u32[]{:S(2)}, u32[]{:S(2)}) collective-permute-start(bf16[128,768]{0,1:T(8,128)(2,1)S(1)} %copy.148), channel_id=1, source_target_pairs={{7,0},{0,1},{1,2},{2,3},{3,4},{4,5},{5,6},{6,7},{15,8},{8,9},{9,10... | collective-permute-start | bytes 589832 | tf_op jit(solution)/shard_map/while/body/eval_jaxpr/ppermute | solution.py:17
  445.3 8.5 collective-permute-start.4
  445.7 10.3 collective-permute-start.5
  457.0 14.3 %collective-permute-start.2 = (bf16[128,768]{0,1:T(8,128)(2,1)S(1)}, bf16[128,768]{0,1:T(8,128)(2,1)S(1)}, u32[]{:S(2)}, u32[]{:S(2)}) collective-permute-start(bf16[128,768]{0,1:T(8,128)(2,1)S(1)} %copy.147), channel_id=1, source_target_pairs={{7,0},{0,1},{1,2},{2,3},{3,4},{4,5},{5,6},{6,7},{15,8},{8,9},{9,10... | collective-permute-start | bytes 589832 | tf_op jit(solution)/shard_map/while/body/eval_jaxpr/ppermute | solution.py:17
  457.1 14.3 %collective-permute-start.3 = (bf16[128,768]{0,1:T(8,128)(2,1)S(1)}, bf16[128,768]{0,1:T(8,128)(2,1)S(1)}, u32[]{:S(2)}, u32[]{:S(2)}) collective-permute-start(bf16[128,768]{0,1:T(8,128)(2,1)S(1)} %copy.148), channel_id=1, source_target_pairs={{7,0},{0,1},{1,2},{2,3},{3,4},{4,5},{5,6},{6,7},{15,8},{8,9},{9,10... | collective-permute-start | bytes 589832 | tf_op jit(solution)/shard_map/while/body/eval_jaxpr/ppermute | solution.py:17
  459.7 8.5 collective-permute-start.4
  460.1 10.3 collective-permute-start.5
  471.4 14.3 %collective-permute-start.2 = (bf16[128,768]{0,1:T(8,128)(2,1)S(1)}, bf16[128,768]{0,1:T(8,128)(2,1)S(1)}, u32[]{:S(2)}, u32[]{:S(2)}) collective-permute-start(bf16[128,768]{0,1:T(8,128)(2,1)S(1)} %copy.147), channel_id=1, source_target_pairs={{7,0},{0,1},{1,2},{2,3},{3,4},{4,5},{5,6},{6,7},{15,8},{8,9},{9,10... | collective-permute-start | bytes 589832 | tf_op jit(solution)/shard_map/while/body/eval_jaxpr/ppermute | solution.py:17
  471.5 14.3 %collective-permute-start.3 = (bf16[128,768]{0,1:T(8,128)(2,1)S(1)}, bf16[128,768]{0,1:T(8,128)(2,1)S(1)}, u32[]{:S(2)}, u32[]{:S(2)}) collective-permute-start(bf16[128,768]{0,1:T(8,128)(2,1)S(1)} %copy.148), channel_id=1, source_target_pairs={{7,0},{0,1},{1,2},{2,3},{3,4},{4,5},{5,6},{6,7},{15,8},{8,9},{9,10... | collective-permute-start | bytes 589832 | tf_op jit(solution)/shard_map/while/body/eval_jaxpr/ppermute | solution.py:17
  474.1 8.5 collective-permute-start.4
  474.5 10.3 collective-permute-start.5
  492.7 201.5 %reduce-scatter.13.cloned.1.call-start = ((), (), s32[]{:S(2)}) async-start(), calls=%async_computation.12 | async-start | bytes 2433024 | tf_op jit(solution)/shard_map/reduce_scatter | solution.py:267
  495.6 302.5 %reduce-scatter.21.cloned.1.call-start = ((), (), s32[]{:S(2)}) async-start(), calls=%async_computation.16 | async-start | bytes 2433024
  496.1 6.9 collective-permute-start.6
  508.1 394.7 %reduce-scatter.23.cloned.1.call-start = ((), (), s32[]{:S(2)}) async-start(), calls=%async_computation.17 | async-start | bytes 2433024
  509.7 6.9 collective-permute-start.7
  521.6 522.3 %reduce-scatter.15.cloned.1.call-start = ((), (), s32[]{:S(2)}) async-start(), calls=%async_computation.13 | async-start | bytes 9732096 | tf_op jit(solution)/shard_map/reduce_scatter | solution.py:271
  527.9 657.8 %reduce-scatter.17.cloned.1.call-start = ((), (), s32[]{:S(2)}) async-start(), calls=%async_computation.14 | async-start | bytes 9732096 | tf_op jit(solution)/shard_map/reduce_scatter | solution.py:273
  534.2 46.0 %copy-start.2 = (bf16[768,768]{1,0:T(8,128)(2,1)S(1)}, bf16[768,768]{1,0:T(8,128)(2,1)}, u32[]{:S(2)}) copy-start(bf16[768,768]{1,0:T(8,128)(2,1)} %all-gather.9.cloned.1.call-done) | copy-start | bytes 3538948
  536.8 44.0 %copy-start.1 = (bf16[768,768]{1,0:T(8,128)(2,1)S(1)}, bf16[768,768]{1,0:T(8,128)(2,1)}, u32[]{:S(2)}) copy-start(bf16[768,768]{1,0:T(8,128)(2,1)} %all-gather.7.cloned.1.call-done) | copy-start | bytes 3538948
  536.8 44.0 %copy-start.17 = (f32[128,768]{1,0:T(8,128)S(1)}, f32[128,768]{1,0:T(8,128)}, u32[]{:S(2)}) copy-start(f32[128,768]{1,0:T(8,128)} %convolution_add_fusion.2) | copy-start | bytes 1179652
  (36 other events, 79.4 us)
Sparse Core Ops, SparseCore 0:
  11.1 57.0 all-gather.6
  71.2 53.2 all-gather.8
  127.5 53.1 all-gather.10
  183.5 57.9 all-gather.12
  244.4 60.8 all-gather.14
  308.2 62.4 all-gather.16
  492.8 96.5 reduce-scatter.18
  596.1 98.0 reduce-scatter.12
  700.1 98.0 reduce-scatter.20
  804.7 98.0 reduce-scatter.22
  909.3 134.5 reduce-scatter.14
  1051.3 134.4 reduce-scatter.16
where the time goes:
time: 1190 us
  waiting for transfers between devices  963 us (81%)
  blocking collectives  80.6 us (7%)
  matrix products  68.3 us (6%)
  local copies, waits for them, and re-layouts  30 us (3%)
  other arithmetic  25.6 us (2%)
  between operations  15.6 us (1%)
    unnamed x15, waiting for transfers between devices  220 us
    reduce_scatter x1, waiting for transfers between devices, body(): lax.psum_scatter(grad_w_down, ('batch', 'ctx'), scatter_dimension=0, tile...  142 us
    reduce_scatter x1, waiting for transfers between devices, body(): lax.psum_scatter(grad_w_up, ('batch', 'ctx'), scatter_dimension=0, tiled=...  141 us
    ppermute x44, waiting for transfers between devices, shifted(): return lax.ppermute(block, axis, route)  133 us
    reduce_scatter x1, waiting for transfers between devices, body(): lax.psum_scatter(grad_w_out, ('batch', 'ctx'), scatter_dimension=0, tiled...  105 us
    unnamed x2, blocking collectives  80.6 us
    all_gather x1, waiting for transfers between devices, body(): lax.all_gather(w_down, ('batch', 'ctx'), axis=0, tiled=True)  57 us
    all_gather x1, waiting for transfers between devices, body(): lax.all_gather(w_value, ('batch', 'ctx'), axis=0, tiled=True)  54.4 us
  transfers between devices with their start and end apart: 56, of which 41 were waited for; matrix products, arithmetic and copies ran while one was open for 8% of the time, Pallas kernels for 0%

commit v1 on v0

--- a/solution.py
+++ b/solution.py
@@ -1,6 +1,11 @@
+import functools
+import math
+
 import jax
 import jax.numpy as jnp
 from jax import lax
+from jax.experimental import pallas as pl
+from jax.experimental.pallas import tpu as pltpu
 from jax.sharding import PartitionSpec as P
 
 HEADS = 12
@@ -296,6 +301,481 @@
     )
 
 
+def normal_parts(resid):
+    center = resid - jnp.mean(resid, -1, keepdims=True)
+    spread = jnp.mean(center * center, -1, keepdims=True)
+    scale = lax.rsqrt(spread + epsilon)
+    return center * scale, scale
+
+
+def normal_back(hat, scale, grad):
+    inner = jnp.mean(grad * hat, -1, keepdims=True)
+    return scale * (grad - jnp.mean(grad, -1, keepdims=True) - hat * inner)
+
+
+def dot(left, right, dims=((1,), (0,))):
+    return lax.dot_general(left, right, (dims, ((), ())), preferred_element_type=jnp.float32)
+
+
+def head_rows(block, head, extra):
+    row = lax.broadcasted_iota(jnp.int32, block.shape, 0)
+    keep = (row >= head * HEAD_DIM) & (row < (head + 1) * HEAD_DIM)
+    if extra:
+        keep = keep | (row >= extra)
+    return jnp.where(keep, block, jnp.zeros_like(block))
+
+
+def head_lanes(block, head):
+    lane = lax.broadcasted_iota(jnp.int32, block.shape, 1)
+    keep = (lane >= head * HEAD_DIM) & (lane < (head + 1) * HEAD_DIM)
+    return jnp.where(keep, block, jnp.zeros_like(block))
+
+
+def attend_kernel(heads, query_t, key, value_t, att_ref, mixed_ref, log_ref):
+    width = heads * HEAD_DIM
+    pieces = mixed_ref.shape[0]
+    span = mixed_ref.shape[2]
+    logs = []
+    for head in range(heads):
+        scores = dot(key[...], head_rows(query_t[...], head, width))
+        top = jnp.max(scores, 0, keepdims=True)
+        expos = jnp.exp(scores - top)
+        total = jnp.sum(expos, 0, keepdims=True)
+        rows = slice(head * HEAD_DIM, (head + 1) * HEAD_DIM)
+        summed = dot(value_t[rows, :], expos.astype(jnp.bfloat16)) / total
+        att_ref[rows, :] = summed
+        low = summed.astype(jnp.bfloat16)
+        for piece in range(pieces):
+            mixed_ref[piece, rows, :] = low[:, piece * span : (piece + 1) * span]
+        logs.append(top + jnp.log(total))
+    for head in range(heads):
+        log_ref[head : head + 1, :] = logs[head]
+
+
+def attend_back_kernel(
+    heads,
+    query_t,
+    query,
+    key,
+    key_t,
+    value,
+    grad_t,
+    grad,
+    att,
+    log,
+    query_grad,
+    key_grad,
+    value_grad,
+):
+    width = heads * HEAD_DIM
+
+    @pl.when(pl.program_id(0) == 0)
+    def _():
+        key_grad[...] = jnp.zeros_like(key_grad)
+        value_grad[...] = jnp.zeros_like(value_grad)
+
+    turned = []
+    for head in range(heads):
+        rows = slice(head * HEAD_DIM, (head + 1) * HEAD_DIM)
+        scores = dot(key[...], head_rows(query_t[...], head, width))
+        probs = jnp.exp(scores - log[head : head + 1, :])
+        prob_grad = dot(value[...], head_rows(grad_t[...], head, 0))
+        delta = jnp.sum(grad_t[rows, :].astype(jnp.float32) * att[rows, :], 0, keepdims=True)
+        score_grad = (probs * (prob_grad - delta)).astype(jnp.bfloat16)
+        turned.append(dot(key_t[rows, :], score_grad))
+        key_grad[...] += dot(score_grad, head_lanes(query[...], head))
+        value_grad[...] += dot(probs.astype(jnp.bfloat16), head_lanes(grad[...], head))
+    gathered = jnp.concatenate(turned, 0) * HEAD_DIM ** (-0.5)
+    query_grad[...] = jnp.transpose(gathered).astype(jnp.bfloat16)
+
+
+def attend(heads, query_t, key, value_t, span):
+    count = query_t.shape[1]
+    keys = key.shape[0]
+    width = heads * HEAD_DIM
+    pieces = 2 if (count // span) % 2 == 0 else 1
+    step = pieces * span
+    return pl.pallas_call(
+        functools.partial(attend_kernel, heads),
+        grid=(count // step,),
+        in_specs=[
+            pl.BlockSpec((query_t.shape[0], step), lambda i: (0, i)),
+            pl.BlockSpec(key.shape, lambda i: (0, 0)),
+            pl.BlockSpec(value_t.shape, lambda i: (0, 0)),
+        ],
+        out_specs=[
+            pl.BlockSpec((width, step), lambda i: (0, i)),
+            pl.BlockSpec((pieces, width, span), lambda i: (i, 0, 0)),
+            pl.BlockSpec((heads, step), lambda i: (0, i)),
+        ],
+        out_shape=[
+            jax.ShapeDtypeStruct((width, count), jnp.float32),
+            jax.ShapeDtypeStruct((count // span, width, span), jnp.bfloat16),
+            jax.ShapeDtypeStruct((heads, count), jnp.float32),
+        ],
+        compiler_params=pltpu.CompilerParams(vmem_limit_bytes=40 * 2**20),
+        cost_estimate=pl.CostEstimate(
+            flops=4 * heads * count * keys * 256,
+            bytes_accessed=4 * keys * 256 * 2,
+            transcendentals=heads * count * keys,
+        ),
+        name="attend",
+    )(query_t, key, value_t)
+
+
+def attend_back(heads, span, query_t, query, key, key_t, value, grad_t, grad, att, log):
+    count = query_t.shape[1]
+    keys = key.shape[0]
+    width = heads * HEAD_DIM
+    pieces = 2 if (count // span) % 2 == 0 else 1
+    step = pieces * span
+
+    def lanes(block):
+        return pl.BlockSpec((block.shape[0], step), lambda i: (0, i))
+
+    def rows(block):
+        return pl.BlockSpec((step, block.shape[1]), lambda i: (i, 0))
+
+    def whole(block):
+        return pl.BlockSpec(block.shape, lambda i: (0, 0))
+
+    return pl.pallas_call(
+        functools.partial(attend_back_kernel, heads),
+        grid=(count // step,),
+        in_specs=[
+            lanes(query_t),
+            rows(query),
+            whole(key),
+            whole(key_t),
+            whole(value),
+            lanes(grad_t),
+            rows(grad),
+            lanes(att),
+            lanes(log),
+        ],
+        out_specs=[
+            pl.BlockSpec((step, width), lambda i: (i, 0)),
+            pl.BlockSpec((keys, width), lambda i: (0, 0)),
+            pl.BlockSpec((keys, width), lambda i: (0, 0)),
+        ],
+        out_shape=[
+            jax.ShapeDtypeStruct((count, width), jnp.bfloat16),
+            jax.ShapeDtypeStruct((keys, width), jnp.float32),
+            jax.ShapeDtypeStruct((keys, width), jnp.float32),
+        ],
+        compiler_params=pltpu.CompilerParams(vmem_limit_bytes=40 * 2**20),
+        cost_estimate=pl.CostEstimate(
+            flops=10 * heads * count * keys * 256,
+            bytes_accessed=8 * keys * 256 * 2,
+            transcendentals=heads * count * keys,
+        ),
+        name="attend_back",
+    )(query_t, query, key, key_t, value, grad_t, grad, att, log)
+
+
+def pick(blocks, index, axis=0):
+    return lax.dynamic_index_in_dim(blocks, index, axis, keepdims=False)
+
+
+def ordered(found, me):
+    count = len(found)
+    rising = [found[count - 1 - i] for i in range(count)]
+    twice = jnp.stack(rising + rising[:-1], 0)
+    return lax.dynamic_slice_in_dim(twice, count - 1 - me, count, 0)
+
+
+def layer_split(
+    tokens,
+    lengths,
+    w_query,
+    b_query,
+    w_key,
+    w_value,
+    b_value,
+    w_out,
+    b_out,
+    gain_one,
+    shift_one,
+    w_up,
+    b_up,
+    w_down,
+    b_down,
+    gain_two,
+    shift_two,
+    cotangent,
+):
+    f32, low = jnp.float32, jnp.bfloat16
+    teams = lax.axis_size("batch")
+    chips = lax.axis_size("ctx") // 2
+    team = lax.axis_index("batch")
+    place = lax.axis_index("ctx")
+    chip, core = place // 2, place % 2
+    rows, width = tokens.shape
+    part = w_query.shape[0]
+    hidden = w_up.shape[1]
+    quarter = hidden // teams
+    heads = HEADS // chips
+    group = heads * HEAD_DIM
+    length = lengths[0]
+
+    def to_chip(block, distance):
+        route = [(i, (i // 2 + distance) % chips * 2 + i % 2) for i in range(2 * chips)]
+        return lax.ppermute(block, "ctx", route)
+
+    def to_core(block):
+        return lax.ppermute(block, "ctx", [(i, i ^ 1) for i in range(2 * chips)])
+
+    def to_team(block, distance):
+        return lax.ppermute(block, "batch", [(i, (i + distance) % teams) for i in range(teams)])
+
+    def from_chips(block):
+        return [block] + [to_chip(block, d) for d in range(1, chips)]
+
+    def from_teams(block):
+        return [block] + [to_team(block, d) for d in range(1, teams)]
+
+    def swap_chips(blocks, axis=0):
+        return [pick(blocks, chip, axis)] + [
+            to_chip(pick(blocks, (chip + d) % chips, axis), d) for d in range(1, chips)
+        ]
+
+    def swap_teams(blocks, axis=0):
+        return [pick(blocks, team, axis)] + [
+            to_team(pick(blocks, (team + d) % teams, axis), d) for d in range(1, teams)
+        ]
+
+    def both_cores(block, axis):
+        other = to_core(block)
+        first = jnp.where(core == 0, block, other)
+        second = jnp.where(core == 0, other, block)
+        return jnp.stack([first, second], axis)
+
+    def total(blocks):
+        result = blocks[0].astype(f32)
+        for block in blocks[1:]:
+            result = result + block.astype(f32)
+        return result
+
+    def return_teams(blocks):
+        return total(
+            [blocks[0]] + [to_team(blocks[d].astype(low), -d) for d in range(1, teams)]
+        )
+
+    vectors = (
+        b_query,
+        b_value,
+        b_out,
+        gain_one,
+        shift_one,
+        b_down,
+        gain_two,
+        shift_two,
+        b_up,
+    )
+    short = jnp.concatenate(vectors)
+    held = -(-(part + 1) // 16) * 16
+    by_group = jnp.concatenate(
+        [item.reshape(part, chips, group) for item in (w_query, w_key, w_value)], 2
+    ).transpose(1, 0, 2)
+    short_row = jnp.pad(short, (0, 3 * group - short.shape[0]))
+    packed = jnp.concatenate(
+        [
+            by_group,
+            jnp.broadcast_to(short_row, (chips, 1, 3 * group)),
+            jnp.zeros((chips, held - part - 1, 3 * group), low),
+        ],
+        1,
+    )
+    mine_rel = from_chips(tokens)
+    packed = ordered(swap_chips(packed), chip)
+    packed = ordered(from_teams(packed), team)
+    packed = both_cores(packed, 2)
+    w_heads = packed[:, :, :, :part].reshape(width, 3 * group)
+    shorts = packed[:, :, :, part].reshape(teams * chips * 2, 3 * group)
+
+    def vector(index, size):
+        return shorts[:, index * part : index * part + size].reshape(-1).astype(f32)
+
+    bias_query, bias_value, bias_out, gain_first, shift_first = [vector(i, part) for i in range(5)]
+    bias_down, gain_second, shift_second = [vector(i, part) for i in range(5, 8)]
+    bias_up = vector(8, b_up.shape[0])
+    bias_up = lax.dynamic_slice_in_dim(bias_up, team * quarter, quarter)
+    bias_query = lax.dynamic_slice_in_dim(bias_query, chip * group, group)
+    bias_value = lax.dynamic_slice_in_dim(bias_value, chip * group, group)
+
+    other_rel = [to_core(block) for block in mine_rel]
+    mine = jnp.concatenate(mine_rel, 0)
+    every = jnp.concatenate(mine_rel + other_rel, 0)
+    starts = [((chip - d) % chips * 2 + core) * rows for d in range(chips)]
+    starts = starts + [((chip - d) % chips * 2 + 1 - core) * rows for d in range(chips)]
+    position = jnp.concatenate([start + jnp.arange(rows) for start in starts])
+
+    up_blocks = ordered(swap_teams(w_up.reshape(part, teams, quarter), 1), team)
+    up_blocks = ordered(from_chips(up_blocks), chip)
+    up_blocks = both_cores(up_blocks, 2)
+    up_part = up_blocks.transpose(1, 0, 2, 3, 4).reshape(width, quarter)
+    down_blocks = ordered(from_chips(w_down), chip)
+    down_part = both_cores(down_blocks, 1).reshape(quarter, width)
+    out_blocks = ordered(from_chips(w_out), chip)
+    out_blocks = ordered(from_teams(out_blocks), team)
+    out_full = both_cores(out_blocks, 2).reshape(width, width)
+
+    w_q, w_k, w_v = w_heads[:, :group], w_heads[:, group : 2 * group], w_heads[:, 2 * group :]
+    scale = HEAD_DIM ** (-0.5)
+    nt, tn = ((0,), (1,)), ((0,), (0,))
+    query = ((dot(mine, w_q) + bias_query).astype(low) * scale).astype(low)
+    query_t = ((dot(w_q, mine, nt) + bias_query[:, None]).astype(low) * scale).astype(low)
+    key = dot(every, w_k).astype(low)
+    key_t = dot(w_k, every, nt).astype(low)
+    value = (dot(every, w_v) + bias_value).astype(low)
+    value_t = (dot(w_v, every, nt) + bias_value[:, None]).astype(low)
+    hide = jnp.where(position < length, 0.0, masked_score).astype(low)
+    spare = 256 - group % 256
+    key_wide = jnp.concatenate(
+        [key, hide[:, None], jnp.zeros((key.shape[0], spare - 1), low)], 1
+    )
+    query_wide = jnp.concatenate(
+        [query_t, jnp.ones((1, mine.shape[0]), low), jnp.zeros((spare - 1, mine.shape[0]), low)], 0
+    )
+    attended, mixed_out, log_total = attend(heads, query_wide, key_wide, value_t, rows)
+
+    back = [mixed_out[0]] + [to_chip(mixed_out[d], -d) for d in range(1, chips)]
+    twice = jnp.stack(back + back[:-1], 0)
+    mixed_t = lax.dynamic_slice_in_dim(twice, (chips - chip) % chips, chips, 0)
+    mixed_t = mixed_t.reshape(width, rows)
+    projected = dot(mixed_t, out_full, tn) + bias_out
+    hat_one, scale_one = normal_parts(tokens.astype(f32) + projected)
+    first = hat_one * gain_first + shift_first
+    first_low = first.astype(low)
+
+    wide = jnp.concatenate(from_teams(first_low), 0)
+    inner = dot(wide, up_part) + bias_up
+    cdf = 0.5 * (1.0 + lax.erf(inner * 2.0**-0.5))
+    slope = cdf + inner * (jnp.exp(-0.5 * inner * inner) * (2.0 * math.pi) ** -0.5)
+    active_low = (inner * cdf).astype(low)
+    active_low, slope = lax.optimization_barrier((active_low, slope))
+    branch_part = dot(active_low, down_part)
+    branch = return_teams(branch_part.reshape(teams, rows, width)) + bias_down
+    hat_two, scale_two = normal_parts(first + branch)
+    output = (hat_two * gain_second + shift_second).astype(low)
+    grad_out = cotangent.astype(f32)
+    grad_gain_two = jnp.sum(grad_out * hat_two, 0)
+    grad_shift_two = jnp.sum(grad_out, 0)
+    grad_second = normal_back(hat_two, scale_two, grad_out * gain_second)
+    branch_grad = grad_second.astype(low)
+    grad_b_down = jnp.sum(branch_grad.astype(f32), 0)
+    wide_grad = jnp.concatenate(from_teams(branch_grad), 0)
+    active_grad = dot(wide_grad, down_part, ((1,), (1,)))
+    inner_grad = (active_grad * slope).astype(low)
+    first_part = dot(inner_grad, up_part, ((1,), (1,)))
+    first_grad = return_teams(first_part.reshape(teams, rows, width)) + grad_second
+    grad_b_up = jnp.sum(inner_grad.astype(f32), 0)
+    grad_down = dot(active_low, wide_grad, tn)
+    grad_up = dot(wide, inner_grad, tn)
+
+    grad_gain_one = jnp.sum(first_grad * hat_one, 0)
+    grad_shift_one = jnp.sum(first_grad, 0)
+    grad_first = normal_back(hat_one, scale_one, first_grad * gain_first)
+    proj_grad = grad_first.astype(low)
+    grad_b_out = jnp.sum(proj_grad.astype(f32), 0)
+    mixed_grad_t = dot(out_full, proj_grad, ((1,), (1,))).astype(low)
+    grad_out_w = dot(mixed_t, proj_grad)
+
+    come = swap_chips(mixed_grad_t.reshape(chips, group, rows))
+    grad_t = jnp.concatenate(come, 1)
+    grad_rows = grad_t.T
+    query_grad, key_sum, value_sum = attend_back(
+        heads,
+        rows,
+        query_wide,
+        query,
+        key_wide,
+        key_t,
+        value,
+        grad_t,
+        grad_rows,
+        attended,
+        log_total,
+    )
+    half = mine.shape[0]
+    pair = jnp.concatenate([key_sum, value_sum], 1)
+    pair = pair[:half] + to_core(pair[half:].astype(low)).astype(f32)
+    grads = jnp.concatenate([query_grad, pair.astype(low)], 1)
+    token_part = dot(grads, w_heads, ((1,), (1,))).reshape(chips, rows, width)
+    token_grad = grad_first + total(
+        [token_part[0]] + [to_chip(token_part[d].astype(low), -d) for d in range(1, chips)]
+    )
+    grad_tokens = token_grad.astype(low)
+    grad_heads = dot(mine, grads, tn)
+
+    def cores_sum(terms, axis):
+        away = to_core(pick(terms, 1 - core, axis).astype(low))
+        return pick(terms, core, axis).astype(f32) + away.astype(f32)
+
+    down_sum = cores_sum(grad_down.reshape(chips, 2, -1, width), 1).astype(low)
+    out_down = total(swap_chips(down_sum))
+    up_sum = cores_sum(grad_up.reshape(teams, chips, 2, part, quarter), 2).astype(low)
+    up_sum = total(swap_chips(up_sum, 1)).astype(low)
+    out_up = ordered(swap_teams(up_sum), team).transpose(1, 0, 2).reshape(part, hidden).astype(f32)
+    out_sum = cores_sum(grad_out_w.reshape(teams, chips, 2, part, width), 2).astype(low)
+    out_sum = total(swap_teams(out_sum)).astype(low)
+    out_out = total(swap_chips(out_sum))
+
+    def spread(piece, index, whole):
+        return lax.dynamic_update_slice_in_dim(
+            jnp.zeros((whole,), f32), piece, index * piece.shape[0], 0
+        )
+
+    grads_low = grads.astype(f32)
+    grad_b_query = spread(jnp.sum(grads_low[:, :group], 0), chip, width)
+    grad_b_value = spread(jnp.sum(grads_low[:, 2 * group :], 0), chip, width)
+    grad_b_up = spread(grad_b_up, team, hidden)
+    small = (
+        grad_b_query,
+        grad_b_value,
+        grad_b_out,
+        grad_gain_one,
+        grad_shift_one,
+        grad_b_down,
+        grad_gain_two,
+        grad_shift_two,
+        grad_b_up,
+    )
+    small = jnp.concatenate([item.reshape(teams, chips, 2, 1, -1) for item in small], -1)
+    small = jnp.pad(small, ((0, 0),) * 4 + ((0, 3 * group - small.shape[-1]),))
+    blank = jnp.zeros((teams, chips, 2, held - part - 1, 3 * group), f32)
+    terms = jnp.concatenate(
+        [grad_heads.reshape(teams, chips, 2, part, 3 * group), small, blank], 3
+    )
+    terms = cores_sum(terms, 2).astype(low)
+    terms = total(swap_teams(terms)).astype(low)
+    found = ordered(swap_chips(terms), chip)
+    matrices = found[:, :part].transpose(1, 0, 2).reshape(part, chips, 3, group).astype(f32)
+    out_query, out_key, out_value = [matrices[:, :, i].reshape(part, width) for i in range(3)]
+    vector_sum = jnp.sum(found[:, part].astype(f32), 0)
+    vec = [vector_sum[i * part : (i + 1) * part] for i in range(8)]
+    out_b_up = vector_sum[8 * part : 8 * part + b_up.shape[0]]
+    return (
+        output,
+        grad_tokens,
+        out_query,
+        vec[0],
+        out_key,
+        out_value,
+        vec[1],
+        out_out,
+        vec[2],
+        vec[3],
+        vec[4],
+        out_up,
+        out_b_up,
+        out_down,
+        vec[5],
+        vec[6],
+        vec[7],
+    )
+
+
 def solution(mesh):
     in_specs = (
         P(("batch", "ctx"), None),
@@ -336,4 +816,7 @@
         P(("batch", "ctx")),
         P(("batch", "ctx")),
     )
-    return jax.shard_map(body, mesh=mesh, in_specs=in_specs, out_specs=out_specs, check_vma=False)
+    places = mesh.shape["ctx"]
+    whole_heads = places % 2 == 0 and HEADS % (places // 2) == 0
+    step = layer_split if whole_heads else body
+    return jax.shard_map(step, mesh=mesh, in_specs=in_specs, out_specs=out_specs, check_vma=False)

time: 1190 us -> 322 us (0.27)
  waiting for transfers between devices: 963 us -> 93.3 us
  starting transfers between devices: 7.16 us -> 97.7 us
  blocking collectives: 80.6 us -> 0 us
  matrix products: 68.3 us -> 22.9 us
  local copies, waits for them, and re-layouts: 30 us -> 66.8 us
  between operations: 15.6 us -> 3.43 us
    reduce_scatter x3 -> x0, waiting for transfers between devices: 388 us -> none  [the longest x1 142 us: body(): lax.psum_scatter(grad_w_down, ('batch', 'ctx'), scatter_dimension=0, tile...]
    all_gather x6 -> x0, waiting for transfers between devices: 223 us -> none  [the longest x1 57 us: body(): lax.all_gather(w_down, ('batch', 'ctx'), axis=0, tiled=True)]
    unnamed x15 -> x0, waiting for transfers between devices: 220 us -> none
    ppermute x44 -> x79, starting transfers between devices: 6.69 us -> 97.7 us  [the longest x36 57.8 us: to_chip(): return lax.ppermute(block, 'ctx', route)]
    unnamed x2 -> x0, blocking collectives: 80.6 us -> none
    dot_general x74 -> x17, matrix products: 68.3 us -> 22.9 us  [dot(): lax.dot_general(left, right, (dims, ((), ())), preferred_element_type=jnp...]
    ppermute x44 -> x79, waiting for transfers between devices: 133 us -> 93.3 us  [the longest x30 59.5 us: to_team(): lax.ppermute(block, 'batch', [(i, (i + distance) % teams) for i in range(...]
    unnamed x124 -> x192, local copies, waits for them, and re-layouts: 29.3 us -> 20.3 us
  transfers between devices with their start and end apart: 56 -> 79, of which waited for: 41 -> 34; matrix products, arithmetic and copies ran while one was open for 8% -> 27% of each run, Pallas kernels for 0% -> 3%
where the time goes in v1:
time: 322 us; the launch traced here: 316 us
  starting transfers between devices  97.7 us (30%)
  waiting for transfers between devices  93.3 us (29%)
  local copies, waits for them, and re-layouts  66.8 us (21%)
  matrix products  22.9 us (7%)
  other arithmetic  22.2 us (7%)
  Pallas kernels  9.64 us (3%)
  between operations  3.43 us (1%)
    ppermute x30, waiting for transfers between devices, to_team(): lax.ppermute(block, 'batch', [(i, (i + distance) % teams) for i in range(...  59.5 us
    ppermute x36, starting transfers between devices, to_chip(): return lax.ppermute(block, 'ctx', route)  57.8 us
    ppermute x30, starting transfers between devices, to_team(): lax.ppermute(block, 'batch', [(i, (i + distance) % teams) for i in range(...  37.8 us
    ppermute x36, waiting for transfers between devices, to_chip(): return lax.ppermute(block, 'ctx', route)  32.3 us
    dot_general x17, matrix products, dot(): lax.dot_general(left, right, (dims, ((), ())), preferred_element_type=jnp...  22.9 us
    unnamed x192, local copies, waits for them, and re-layouts  20.3 us
    reshape x9, local copies, waits for them, and re-layouts, layer_split(): item.reshape(teams, chips, 2, 1, -1)  7.04 us
  transfers between devices with their start and end apart: 79, of which 34 were waited for; matrix products, arithmetic and copies ran while one was open for 27% of the time, Pallas kernels for 3%

profile of v1, /device:TPU:0, one launch (start us, length us, event | category | flops | bytes accessed | tf_op | source)
XLA Modules:
  0.0 315.9 jit_solution(4095153320588247265)
XLA Ops:
  0.7 4.1 %collective-permute-start.18 = (bf16[24,768]{1,0:T(8,128)(2,1)}, bf16[24,768]{1,0:T(8,128)(2,1)S(1)}, u32[]{:S(2)}, u32[]{:S(2)}) collective-permute-start(bf16[24,768]{1,0:T(8,128)(2,1)} %param.25), channel_id=1, source_target_pairs={{0,4},{1,5},{2,6},{3,7},{4,0},{5,1},{6,2},{7,3},{8,12},{9,13},{10,... | collective-permute-start | bytes 110600 | tf_op jit(solution)/shard_map/ppermute | solution.py:523
  7.8 2.9 collective-permute-start.34
  16.0 6.1 %concatenate.69 = bf16[288]{0:T(512)(128)(2,1)S(1)} concatenate(bf16[24]{0:T(256)(128)(2,1)} %param.21, bf16[24]{0:T(256)(128)(2,1)} %param.24, bf16[24]{0:T(256)(128)(2,1)} %param.26, bf16[24]{0:T(256)(128)(2,1)} %param.27, bf16[24]{0:T(256)(128)(2,1)} %param.28, bf16[24]{0:T(256)(128)(2,1)} %param.32, bf16[24]{0:T(256)(128)(2,1)} %param.33, bf16[24]{0:T(256)(128)(2,1)} %param.34, ...), dimensions={0} | concatenate | bytes 1152 | tf_op jit(solution)/shard_map/concatenate | solution.py:575
  30.9 2.4 collective-permute-start.27
  36.5 1.8 collective-permute-done.28
  42.9 2.1 collective-permute-start.36
  45.1 1.8 collective-permute-start.9
  47.7 1.9 stack.209
  49.7 2.1 collective-permute-start.7
  51.9 2.0 collective-permute-start.3
  56.8 1.8 collective-permute-done.3
  58.6 1.6 collective-permute-start.20
  60.2 3.8 %collective-permute-done.20 = bf16[4,24,768]{2,1,0:T(8,128)(2,1)S(1)} collective-permute-done((bf16[4,24,768]{2,1,0:T(8,128)(2,1)S(1)}, bf16[4,24,768]{2,1,0:T(8,128)(2,1)S(1)}, u32[]{:S(2)}, u32[]{:S(2)}) %collective-permute-start.20) | collective-permute-done | bytes 147488 | tf_op jit(solution)/shard_map/ppermute | solution.py:529
  64.0 5.9 %collective-permute-start.30 = (bf16[4,24,768]{2,1,0:T(8,128)(2,1)S(1)}, bf16[4,24,768]{2,1,0:T(8,128)(2,1)S(1)}, u32[]{:S(2)}, u32[]{:S(2)}) collective-permute-start(bf16[4,24,768]{2,1,0:T(8,128)(2,1)S(1)} %copy-done.41), channel_id=1, source_target_pairs={{0,6},{1,7},{2,0},{3,1},{4,2},{5,3},{6,4},{7,5},{8,14},{9,15},{10,... | collective-permute-start | bytes 442376 | tf_op jit(solution)/shard_map/ppermute | solution.py:523
  70.0 2.7 collective-permute-done.30
  74.1 3.6 %collective-permute-done.21 = bf16[4,24,768]{2,1,0:T(8,128)(2,1)S(1)} collective-permute-done((bf16[4,24,768]{2,1,0:T(8,128)(2,1)S(1)}, bf16[4,24,768]{2,1,0:T(8,128)(2,1)S(1)}, u32[]{:S(2)}, u32[]{:S(2)}) %collective-permute-start.21) | collective-permute-done | bytes 147488 | tf_op jit(solution)/shard_map/ppermute | solution.py:529
  78.7 5.1 %collective-permute-done.22 = bf16[4,24,768]{2,1,0:T(8,128)(2,1)S(1)} collective-permute-done((bf16[4,24,768]{2,1,0:T(8,128)(2,1)S(1)}, bf16[4,24,768]{2,1,0:T(8,128)(2,1)S(1)}, u32[]{:S(2)}, u32[]{:S(2)}) %collective-permute-start.22) | collective-permute-done | bytes 147488 | tf_op jit(solution)/shard_map/ppermute | solution.py:529
  83.8 2.7 collective-permute-start.31
  86.5 5.2 %collective-permute-done.31 = bf16[4,24,768]{2,1,0:T(8,128)(2,1)S(1)} collective-permute-done((bf16[4,24,768]{2,1,0:T(8,128)(2,1)S(1)}, bf16[4,24,768]{2,1,0:T(8,128)(2,1)S(1)}, u32[]{:S(2)}, u32[]{:S(2)}) %collective-permute-start.31) | collective-permute-done | bytes 147488 | tf_op jit(solution)/shard_map/ppermute | solution.py:523
  92.2 6.4 %collective-permute-done.32 = bf16[4,24,768]{2,1,0:T(8,128)(2,1)S(1)} collective-permute-done((bf16[4,24,768]{2,1,0:T(8,128)(2,1)S(1)}, bf16[4,24,768]{2,1,0:T(8,128)(2,1)S(1)}, u32[]{:S(2)}, u32[]{:S(2)}) %collective-permute-start.32) | collective-permute-done | bytes 147488 | tf_op jit(solution)/shard_map/ppermute | solution.py:523
  100.2 3.8 %collective-permute-done.4 = bf16[4,32,576]{2,0,1:T(4,128)(2,1)S(1)} collective-permute-done((bf16[4,32,576]{2,0,1:T(4,128)(2,1)S(1)}, bf16[4,32,576]{2,0,1:T(4,128)(2,1)S(1)}, u32[]{:S(2)}, u32[]{:S(2)}) %collective-permute-start.4) | collective-permute-done | bytes 147488 | tf_op jit(solution)/shard_map/ppermute | solution.py:529
  104.0 1.7 collective-permute-start.5
  105.8 4.5 %collective-permute-done.5 = bf16[4,32,576]{2,0,1:T(4,128)(2,1)S(1)} collective-permute-done((bf16[4,32,576]{2,0,1:T(4,128)(2,1)S(1)}, bf16[4,32,576]{2,0,1:T(4,128)(2,1)S(1)}, u32[]{:S(2)}, u32[]{:S(2)}) %collective-permute-start.5) | collective-permute-done | bytes 147488 | tf_op jit(solution)/shard_map/ppermute | solution.py:529
  123.6 2.2 fusion.8.value_t
  127.1 4.3 %attend.1 = (f32[192,512]{1,0:T(8,128)S(1)}, bf16[4,192,128]{2,1,0:T(8,128)(2,1)S(1)}, f32[3,512]{1,0:T(4,128)S(1)}) custom-call(bf16[256,512]{1,0:T(8,128)(2,1)S(1)} %maximum_maximum_fusion.1.query_t, bf16[1024,256]{1,0:T(8,128)(2,1)S(1)} %maximum_maximum_fusion.key, bf16[192,1024]{1,0:T(8,128)(2,1)S(1)} %fusion.8.value_t), custom_call_target="tpu_custom_call" | custom-call | flops 1610612736 | bytes 2097152 | tf_op jit(solution)/shard_map/attend/pallas_call | solution.py:398
  140.2 6.2 %collective-permute-done.15 = bf16[192,128]{1,0:T(8,128)(2,1)S(1)} collective-permute-done((bf16[192,128]{1,0:T(8,128)(2,1)S(1)}, bf16[192,128]{1,0:T(8,128)(2,1)S(1)}, u32[]{:S(2)}, u32[]{:S(2)}) %collective-permute-start.15) | collective-permute-done | bytes 49184 | tf_op jit(solution)/shard_map/ppermute | solution.py:523
  146.6 1.8 fusion.93
  150.6 1.7 collective-permute-start.24
  152.9 3.7 %collective-permute-done.26 = bf16[128,768]{1,0:T(8,128)(2,1)S(1)} collective-permute-done((bf16[128,768]{1,0:T(8,128)(2,1)S(1)}, bf16[128,768]{1,0:T(8,128)(2,1)S(1)}, u32[]{:S(2)}, u32[]{:S(2)}) %collective-permute-start.26) | collective-permute-done | bytes 196640 | tf_op jit(solution)/shard_map/ppermute | solution.py:529
  156.6 2.3 collective-permute-done.25
  159.7 2.8 fusion.5
  165.7 1.7 collective-permute-start.39
  168.4 2.5 collective-permute-done.38
  170.9 3.1 collective-permute-done.40
  182.2 2.6 collective-permute-done.43
  184.8 3.1 collective-permute-done.42
  187.9 3.8 %convert_reduce_fusion = (f32[768]{0:T(1024)S(1)}, bf16[512,768]{1,0:T(8,128)(2,1)}) fusion(f32[512,768]{1,0:T(8,128)} %get-tuple-element.27, bf16[768,768]{1,0:T(8,128)(2,1)} %bitcast.323, bf16[128,768]{1,0:T(8,128)(2,1)} %collective-permute-done.43, bf16[128,768]{1,0:T(8,128)(2,1)} %collective-permute-done.42, ...), kind=kOutput, calls=%fused_computation.12 | convolution fusion | flops 608697600 | bytes 4328448 | tf_op jit(solution)/shard_map/dot_general | solution.py:317
  192.7 2.2 fusion.67
  198.2 1.8 collective-permute-start.46
  202.3 3.5 %collective-permute-done.44 = bf16[128,768]{1,0:T(8,128)(2,1)S(1)} collective-permute-done((bf16[128,768]{1,0:T(8,128)(2,1)S(1)}, bf16[128,768]{1,0:T(8,128)(2,1)S(1)}, u32[]{:S(2)}, u32[]{:S(2)}) %collective-permute-start.44) | collective-permute-done | bytes 196640 | tf_op jit(solution)/shard_map/ppermute | solution.py:529
  205.8 2.6 collective-permute-done.46
  220.4 5.3 %attend_back.1 = (bf16[512,192]{1,0:T(8,128)(2,1)S(1)}, f32[1024,192]{1,0:T(8,128)S(1)}, f32[1024,192]{1,0:T(8,128)S(1)}) custom-call(bf16[256,512]{1,0:T(8,128)(2,1)S(1)} %maximum_maximum_fusion.1.query_t, bf16[512,192]{1,0:T(8,128)(2,1)S(1)} %fusion.15.query, bf16[1024,256]{1,0:T(8,128)(2,1)S(1)} %maximum_maximum_fusion.key, ...), custom_call_target="tpu_custom_call" | custom-call | flops 4026531840 | bytes 4194304 | tf_op jit(solution)/shard_map/attend_back/pallas_call | solution.py:442
  229.5 1.9 collective-permute-start.76
  233.9 3.7 %collective-permute-start.71 = (bf16[4,24,768]{2,1,0:T(8,128)(2,1)}, bf16[4,24,768]{2,1,0:T(8,128)(2,1)}, u32[]{:S(2)}, u32[]{:S(2)}) collective-permute-start(bf16[4,24,768]{2,1,0:T(8,128)(2,1)} %get-tuple-element.76), channel_id=1, source_target_pairs={{0,6},{1,7},{2,0},{3,1},{4,2},{5,3},{6,4},{7,5},{8,14},{9,15},{10,... | collective-permute-start | bytes 442376 | tf_op jit(solution)/shard_map/ppermute | solution.py:523
  239.8 1.7 fusion.96
  248.9 1.9 concatenate.89
  253.9 2.0 collective-permute-start.77
  257.2 1.7 collective-permute-start.51
  259.0 3.9 %collective-permute-start.53 = (bf16[128,768]{1,0:T(8,128)(2,1)S(1)}, bf16[128,768]{1,0:T(8,128)(2,1)S(1)}, u32[]{:S(2)}, u32[]{:S(2)}) collective-permute-start(bf16[128,768]{1,0:T(8,128)(2,1)S(1)} %get-tuple-element.61), channel_id=1, source_target_pairs={{0,2},{1,3},{2,4},{3,5},{4,6},{5,7},{6,0},{7,1},{8,10},{9,11},{10,... | collective-permute-start | bytes 589832 | tf_op jit(solution)/shard_map/ppermute | solution.py:523
  262.9 4.8 %collective-permute-done.77 = bf16[96,768]{1,0:T(8,128)(2,1)S(1)} collective-permute-done((bf16[96,768]{1,0:T(8,128)(2,1)S(1)}, bf16[96,768]{1,0:T(8,128)(2,1)S(1)}, u32[]{:S(2)}, u32[]{:S(2)}) %collective-permute-start.77) | collective-permute-done | bytes 147488 | tf_op jit(solution)/shard_map/ppermute | solution.py:523
  268.3 1.8 fusion.55
  271.6 1.6 collective-permute-start.73
  273.2 2.4 collective-permute-done.73
  276.6 4.2 %collective-permute-done.74 = bf16[24,768]{1,0:T(8,128)(2,1)S(1)} collective-permute-done((bf16[24,768]{1,0:T(8,128)(2,1)S(1)}, bf16[24,768]{1,0:T(8,128)(2,1)S(1)}, u32[]{:S(2)}, u32[]{:S(2)}) %collective-permute-start.74) | collective-permute-done | bytes 36896 | tf_op jit(solution)/shard_map/ppermute | solution.py:529
  283.0 2.9 collective-permute-start.64
  285.9 1.6 collective-permute-start.63
  287.5 2.0 collective-permute-done.52
  290.6 2.9 collective-permute-start.57
  293.5 1.6 collective-permute-start.56
  295.2 3.5 %collective-permute-start.65 = (bf16[24,768]{1,0:T(8,128)(2,1)S(1)}, bf16[24,768]{1,0:T(8,128)(2,1)S(1)}, u32[]{:S(2)}, u32[]{:S(2)}) collective-permute-start(bf16[24,768]{1,0:T(8,128)(2,1)S(1)} %get-tuple-element.113), channel_id=1, source_target_pairs={{0,2},{1,3},{2,4},{3,5},{4,6},{5,7},{6,0},{7,1},{8,10},{9,11},{10,... | collective-permute-start | bytes 110600 | tf_op jit(solution)/shard_map/ppermute | solution.py:523
  300.4 2.9 collective-permute-start.58
  304.6 1.8 collective-permute-start.60
  306.3 1.8 collective-permute-start.59
  308.1 3.2 %collective-permute-done.59 = bf16[32,576]{1,0:T(8,128)(2,1)S(1)} collective-permute-done((bf16[32,576]{1,0:T(8,128)(2,1)S(1)}, bf16[32,576]{1,0:T(8,128)(2,1)S(1)}, u32[]{:S(2)}, u32[]{:S(2)}) %collective-permute-start.59) | collective-permute-done | bytes 36896 | tf_op jit(solution)/shard_map/ppermute | solution.py:523
  (463 shorter events, 123.5 us)
Async XLA Ops:
  0.7 33.5 %collective-permute-start.18 = (bf16[24,768]{1,0:T(8,128)(2,1)}, bf16[24,768]{1,0:T(8,128)(2,1)S(1)}, u32[]{:S(2)}, u32[]{:S(2)}) collective-permute-start(bf16[24,768]{1,0:T(8,128)(2,1)} %param.25), channel_id=1, source_target_pairs={{0,4},{1,5},{2,6},{3,7},{4,0},{5,1},{6,2},{7,3},{8,12},{9,13},{10,... | collective-permute-start | bytes 110600 | tf_op jit(solution)/shard_map/ppermute | solution.py:523
  4.8 25.5 %collective-permute-start.17 = (bf16[24,768]{1,0:T(8,128)(2,1)}, bf16[24,768]{1,0:T(8,128)(2,1)S(1)}, u32[]{:S(2)}, u32[]{:S(2)}) collective-permute-start(bf16[24,768]{1,0:T(8,128)(2,1)} %param.25), channel_id=1, source_target_pairs={{0,6},{1,7},{2,0},{3,1},{4,2},{5,3},{6,4},{7,5},{8,14},{9,15},{10,... | collective-permute-start | bytes 110600 | tf_op jit(solution)/shard_map/ppermute | solution.py:523
  6.1 28.5 %collective-permute-start.19 = (bf16[24,768]{1,0:T(8,128)(2,1)}, bf16[24,768]{1,0:T(8,128)(2,1)S(1)}, u32[]{:S(2)}, u32[]{:S(2)}) collective-permute-start(bf16[24,768]{1,0:T(8,128)(2,1)} %param.25), channel_id=1, source_target_pairs={{0,2},{1,3},{2,4},{3,5},{4,6},{5,7},{6,0},{7,1},{8,10},{9,11},{10,... | collective-permute-start | bytes 110600 | tf_op jit(solution)/shard_map/ppermute | solution.py:523
  6.8 45.0 %collective-permute-start.35 = (bf16[96,768]{1,0:T(8,128)(2,1)}, bf16[96,768]{1,0:T(8,128)(2,1)S(1)}, u32[]{:S(2)}, u32[]{:S(2)}) collective-permute-start(bf16[96,768]{1,0:T(8,128)(2,1)} %param.31), channel_id=1, source_target_pairs={{0,4},{1,5},{2,6},{3,7},{4,0},{5,1},{6,2},{7,3},{8,12},{9,13},{10,... | collective-permute-start | bytes 442376 | tf_op jit(solution)/shard_map/ppermute | solution.py:523
  7.8 41.9 %collective-permute-start.34 = (bf16[96,768]{1,0:T(8,128)(2,1)}, bf16[96,768]{1,0:T(8,128)(2,1)S(1)}, u32[]{:S(2)}, u32[]{:S(2)}) collective-permute-start(bf16[96,768]{1,0:T(8,128)(2,1)} %param.31), channel_id=1, source_target_pairs={{0,6},{1,7},{2,0},{3,1},{4,2},{5,3},{6,4},{7,5},{8,14},{9,15},{10,... | collective-permute-start | bytes 442376 | tf_op jit(solution)/shard_map/ppermute | solution.py:523
  36.0 6.9 %collective-permute-start = (bf16[32,576]{1,0:T(8,128)(2,1)}, bf16[32,576]{1,0:T(8,128)(2,1)S(1)}, u32[]{:S(2)}, u32[]{:S(2)}) collective-permute-start(bf16[32,576]{1,0:T(8,128)(2,1)} %bitcast.308), channel_id=1, source_target_pairs={{0,6},{1,7},{2,0},{3,1},{4,2},{5,3},{6,4},{7,5},{8,14},{9,15},{10,... | collective-permute-start | bytes 110600 | tf_op jit(solution)/shard_map/ppermute | solution.py:523
  38.3 6.8 %collective-permute-start.1 = (bf16[32,576]{1,0:T(8,128)(2,1)}, bf16[32,576]{1,0:T(8,128)(2,1)S(1)}, u32[]{:S(2)}, u32[]{:S(2)}) collective-permute-start(bf16[32,576]{1,0:T(8,128)(2,1)} %bitcast.349), channel_id=1, source_target_pairs={{0,4},{1,5},{2,6},{3,7},{4,0},{5,1},{6,2},{7,3},{8,12},{9,13},{10,... | collective-permute-start | bytes 110600 | tf_op jit(solution)/shard_map/ppermute | solution.py:523
  39.7 7.2 %collective-permute-start.2 = (bf16[32,576]{1,0:T(8,128)(2,1)}, bf16[32,576]{1,0:T(8,128)(2,1)S(1)}, u32[]{:S(2)}, u32[]{:S(2)}) collective-permute-start(bf16[32,576]{1,0:T(8,128)(2,1)} %bitcast.348), channel_id=1, source_target_pairs={{0,2},{1,3},{2,4},{3,5},{4,6},{5,7},{6,0},{7,1},{8,10},{9,11},{10,... | collective-permute-start | bytes 110600 | tf_op jit(solution)/shard_map/ppermute | solution.py:523
  42.9 9.0 %collective-permute-start.36 = (bf16[96,768]{1,0:T(8,128)(2,1)}, bf16[96,768]{1,0:T(8,128)(2,1)}, u32[]{:S(2)}, u32[]{:S(2)}) collective-permute-start(bf16[96,768]{1,0:T(8,128)(2,1)} %param.31), channel_id=1, source_target_pairs={{0,2},{1,3},{2,4},{3,5},{4,6},{5,7},{6,0},{7,1},{8,10},{9,11},{10,... | collective-permute-start | bytes 442376 | tf_op jit(solution)/shard_map/ppermute | solution.py:523
  45.1 69.6 %collective-permute-start.9 = (bf16[128,768]{1,0:T(8,128)(2,1)S(1)}, bf16[128,768]{1,0:T(8,128)(2,1)}, u32[]{:S(2)}, u32[]{:S(2)}) collective-permute-start(bf16[128,768]{1,0:T(8,128)(2,1)S(1)} %copy-done.31), channel_id=1, source_target_pairs={{0,6},{1,7},{2,0},{3,1},{4,2},{5,3},{6,4},{7,5},{8,14},{9,15},{10,... | collective-permute-start | bytes 589832 | tf_op jit(solution)/shard_map/ppermute | solution.py:523
  47.0 66.7 %collective-permute-start.8 = (bf16[128,768]{1,0:T(8,128)(2,1)S(1)}, bf16[128,768]{1,0:T(8,128)(2,1)}, u32[]{:S(2)}, u32[]{:S(2)}) collective-permute-start(bf16[128,768]{1,0:T(8,128)(2,1)S(1)} %copy-done.31), channel_id=1, source_target_pairs={{0,4},{1,5},{2,6},{3,7},{4,0},{5,1},{6,2},{7,3},{8,12},{9,13},{10,... | collective-permute-start | bytes 589832 | tf_op jit(solution)/shard_map/ppermute | solution.py:523
  49.7 63.4 %collective-permute-start.7 = (bf16[128,768]{1,0:T(8,128)(2,1)S(1)}, bf16[128,768]{1,0:T(8,128)(2,1)S(1)}, u32[]{:S(2)}, u32[]{:S(2)}) collective-permute-start(bf16[128,768]{1,0:T(8,128)(2,1)S(1)} %copy-done.31), channel_id=1, source_target_pairs={{0,2},{1,3},{2,4},{3,5},{4,6},{5,7},{6,0},{7,1},{8,10},{9,11},{10,... | collective-permute-start | bytes 589832 | tf_op jit(solution)/shard_map/ppermute | solution.py:523
  51.8 64.5 %collective-permute-start.10 = (bf16[128,768]{1,0:T(8,128)(2,1)S(1)}, bf16[128,768]{1,0:T(8,128)(2,1)S(1)}, u32[]{:S(2)}, u32[]{:S(2)}) collective-permute-start(bf16[128,768]{1,0:T(8,128)(2,1)S(1)} %copy-done.31), channel_id=1, source_target_pairs={{0,1},{1,0},{2,3},{3,2},{4,5},{5,4},{6,7},{7,6},{8,9},{9,8},{10,11... | collective-permute-start | bytes 589832 | tf_op jit(solution)/shard_map/ppermute | solution.py:526
  51.9 6.6 %collective-permute-start.3 = (bf16[4,32,576]{2,0,1:T(4,128)(2,1)S(1)}, bf16[4,32,576]{2,0,1:T(4,128)(2,1)S(1)}, u32[]{:S(2)}, u32[]{:S(2)}) collective-permute-start(bf16[4,32,576]{2,0,1:T(4,128)(2,1)S(1)} %constant_dynamic-slice_fusion.16), channel_id=1, source_target_pairs={{0,24},{8,0},{16,8},{24,16},{1,25},{9,1},{17,9},{25,17},{2,26},{10... | collective-permute-start | bytes 442376 | tf_op jit(solution)/shard_map/ppermute | solution.py:529
  58.6 5.5 %collective-permute-start.20 = (bf16[4,24,768]{2,1,0:T(8,128)(2,1)S(1)}, bf16[4,24,768]{2,1,0:T(8,128)(2,1)S(1)}, u32[]{:S(2)}, u32[]{:S(2)}) collective-permute-start(bf16[4,24,768]{2,1,0:T(8,128)(2,1)S(1)} %copy-done.42), channel_id=1, source_target_pairs={{0,24},{8,0},{16,8},{24,16},{1,25},{9,1},{17,9},{25,17},{2,26},{10... | collective-permute-start | bytes 442376 | tf_op jit(solution)/shard_map/ppermute | solution.py:529
  64.0 8.6 %collective-permute-start.30 = (bf16[4,24,768]{2,1,0:T(8,128)(2,1)S(1)}, bf16[4,24,768]{2,1,0:T(8,128)(2,1)S(1)}, u32[]{:S(2)}, u32[]{:S(2)}) collective-permute-start(bf16[4,24,768]{2,1,0:T(8,128)(2,1)S(1)} %copy-done.41), channel_id=1, source_target_pairs={{0,6},{1,7},{2,0},{3,1},{4,2},{5,3},{6,4},{7,5},{8,14},{9,15},{10,... | collective-permute-start | bytes 442376 | tf_op jit(solution)/shard_map/ppermute | solution.py:523
  77.8 6.0 %collective-permute-start.22 = (bf16[4,24,768]{2,1,0:T(8,128)(2,1)S(1)}, bf16[4,24,768]{2,1,0:T(8,128)(2,1)S(1)}, u32[]{:S(2)}, u32[]{:S(2)}) collective-permute-start(bf16[4,24,768]{2,1,0:T(8,128)(2,1)S(1)} %copy-done.42), channel_id=1, source_target_pairs={{0,8},{8,16},{16,24},{24,0},{1,9},{9,17},{17,25},{25,1},{2,10},{10... | collective-permute-start | bytes 442376 | tf_op jit(solution)/shard_map/ppermute | solution.py:529
  83.8 7.9 %collective-permute-start.31 = (bf16[4,24,768]{2,1,0:T(8,128)(2,1)S(1)}, bf16[4,24,768]{2,1,0:T(8,128)(2,1)S(1)}, u32[]{:S(2)}, u32[]{:S(2)}) collective-permute-start(bf16[4,24,768]{2,1,0:T(8,128)(2,1)S(1)} %copy-done.41), channel_id=1, source_target_pairs={{0,4},{1,5},{2,6},{3,7},{4,0},{5,1},{6,2},{7,3},{8,12},{9,13},{10,... | collective-permute-start | bytes 442376 | tf_op jit(solution)/shard_map/ppermute | solution.py:523
  91.7 6.9 %collective-permute-start.32 = (bf16[4,24,768]{2,1,0:T(8,128)(2,1)S(1)}, bf16[4,24,768]{2,1,0:T(8,128)(2,1)S(1)}, u32[]{:S(2)}, u32[]{:S(2)}) collective-permute-start(bf16[4,24,768]{2,1,0:T(8,128)(2,1)S(1)} %copy-done.41), channel_id=1, source_target_pairs={{0,2},{1,3},{2,4},{3,5},{4,6},{5,7},{6,0},{7,1},{8,10},{9,11},{10,... | collective-permute-start | bytes 442376 | tf_op jit(solution)/shard_map/ppermute | solution.py:523
  104.0 6.4 %collective-permute-start.5 = (bf16[4,32,576]{2,0,1:T(4,128)(2,1)S(1)}, bf16[4,32,576]{2,0,1:T(4,128)(2,1)S(1)}, u32[]{:S(2)}, u32[]{:S(2)}) collective-permute-start(bf16[4,32,576]{2,0,1:T(4,128)(2,1)S(1)} %constant_dynamic-slice_fusion.16), channel_id=1, source_target_pairs={{0,8},{8,16},{16,24},{24,0},{1,9},{9,17},{17,25},{25,1},{2,10},{10... | collective-permute-start | bytes 442376 | tf_op jit(solution)/shard_map/ppermute | solution.py:529
  110.4 7.9 %collective-permute-start.37 = (bf16[4,96,768]{2,1,0:T(8,128)(2,1)S(1)}, bf16[4,96,768]{2,1,0:T(8,128)(2,1)S(1)}, u32[]{:S(2)}, u32[]{:S(2)}) collective-permute-start(bf16[4,96,768]{2,1,0:T(8,128)(2,1)S(1)} %constant_dynamic-slice_fusion.5), channel_id=1, source_target_pairs={{0,1},{1,0},{2,3},{3,2},{4,5},{5,4},{6,7},{7,6},{8,9},{9,8},{10,11... | collective-permute-start | bytes 1769480 | tf_op jit(solution)/shard_map/ppermute | solution.py:526
  113.1 20.5 %collective-permute-start.23 = (bf16[4,4,24,768]{3,2,1,0:T(8,128)(2,1)}, bf16[4,4,24,768]{3,2,1,0:T(8,128)(2,1)}, u32[]{:S(2)}, u32[]{:S(2)}) collective-permute-start(bf16[4,4,24,768]{3,2,1,0:T(8,128)(2,1)} %constant_dynamic-slice_fusion.12), channel_id=1, source_target_pairs={{0,1},{1,0},{2,3},{3,2},{4,5},{5,4},{6,7},{7,6},{8,9},{9,8},{10,11... | collective-permute-start | bytes 1769480 | tf_op jit(solution)/shard_map/ppermute | solution.py:526
  113.7 22.3 %collective-permute-start.33 = (bf16[4,4,24,768]{3,2,1,0:T(8,128)(2,1)}, bf16[4,4,24,768]{3,2,1,0:T(8,128)(2,1)}, u32[]{:S(2)}, u32[]{:S(2)}) collective-permute-start(bf16[4,4,24,768]{3,2,1,0:T(8,128)(2,1)} %constant_dynamic-slice_fusion.6), channel_id=1, source_target_pairs={{0,1},{1,0},{2,3},{3,2},{4,5},{5,4},{6,7},{7,6},{8,9},{9,8},{10,11... | collective-permute-start | bytes 1769480 | tf_op jit(solution)/shard_map/ppermute | solution.py:526
  132.1 8.1 %collective-permute-start.14 = (bf16[192,128]{1,0:T(8,128)(2,1)}, bf16[192,128]{1,0:T(8,128)(2,1)S(1)}, u32[]{:S(2)}, u32[]{:S(2)}) collective-permute-start(bf16[192,128]{1,0:T(8,128)(2,1)} %get-tuple-element.94), channel_id=1, source_target_pairs={{0,6},{1,7},{2,0},{3,1},{4,2},{5,3},{6,4},{7,5},{8,14},{9,15},{10,... | collective-permute-start | bytes 147464 | tf_op jit(solution)/shard_map/ppermute | solution.py:523
  139.5 7.0 %collective-permute-start.16 = (bf16[192,128]{1,0:T(8,128)(2,1)S(1)}, bf16[192,128]{1,0:T(8,128)(2,1)S(1)}, u32[]{:S(2)}, u32[]{:S(2)}) collective-permute-start(bf16[192,128]{1,0:T(8,128)(2,1)S(1)} %copy-done.47), channel_id=1, source_target_pairs={{0,2},{1,3},{2,4},{3,5},{4,6},{5,7},{6,0},{7,1},{8,10},{9,11},{10,... | collective-permute-start | bytes 147464 | tf_op jit(solution)/shard_map/ppermute | solution.py:523
  140.0 6.4 %collective-permute-start.15 = (bf16[192,128]{1,0:T(8,128)(2,1)S(1)}, bf16[192,128]{1,0:T(8,128)(2,1)S(1)}, u32[]{:S(2)}, u32[]{:S(2)}) collective-permute-start(bf16[192,128]{1,0:T(8,128)(2,1)S(1)} %copy-done.48), channel_id=1, source_target_pairs={{0,4},{1,5},{2,6},{3,7},{4,0},{5,1},{6,2},{7,3},{8,12},{9,13},{10,... | collective-permute-start | bytes 147464 | tf_op jit(solution)/shard_map/ppermute | solution.py:523
  148.8 7.8 %collective-permute-start.26 = (bf16[128,768]{1,0:T(8,128)(2,1)S(1)}, bf16[128,768]{1,0:T(8,128)(2,1)S(1)}, u32[]{:S(2)}, u32[]{:S(2)}) collective-permute-start(bf16[128,768]{1,0:T(8,128)(2,1)S(1)} %fusion.44), channel_id=1, source_target_pairs={{0,24},{8,0},{16,8},{24,16},{1,25},{9,1},{17,9},{25,17},{2,26},{10... | collective-permute-start | bytes 589832 | tf_op jit(solution)/shard_map/ppermute | solution.py:529
  149.3 9.6 %collective-permute-start.25 = (bf16[128,768]{1,0:T(8,128)(2,1)S(1)}, bf16[128,768]{1,0:T(8,128)(2,1)S(1)}, u32[]{:S(2)}, u32[]{:S(2)}) collective-permute-start(bf16[128,768]{1,0:T(8,128)(2,1)S(1)} %fusion.44), channel_id=1, source_target_pairs={{0,16},{8,24},{16,0},{24,8},{1,17},{9,25},{17,1},{25,9},{2,18},{10... | collective-permute-start | bytes 589832 | tf_op jit(solution)/shard_map/ppermute | solution.py:529
  150.6 9.1 %collective-permute-start.24 = (bf16[128,768]{1,0:T(8,128)(2,1)S(1)}, bf16[128,768]{1,0:T(8,128)(2,1)S(1)}, u32[]{:S(2)}, u32[]{:S(2)}) collective-permute-start(bf16[128,768]{1,0:T(8,128)(2,1)S(1)} %fusion.44), channel_id=1, source_target_pairs={{0,8},{8,16},{16,24},{24,0},{1,9},{9,17},{17,25},{25,1},{2,10},{10... | collective-permute-start | bytes 589832 | tf_op jit(solution)/shard_map/ppermute | solution.py:529
  163.4 7.4 %collective-permute-start.38 = (bf16[128,768]{1,0:T(8,128)(2,1)S(1)}, bf16[128,768]{1,0:T(8,128)(2,1)S(1)}, u32[]{:S(2)}, u32[]{:S(2)}) collective-permute-start(bf16[128,768]{1,0:T(8,128)(2,1)S(1)} %get-tuple-element.66), channel_id=1, source_target_pairs={{0,24},{8,0},{16,8},{24,16},{1,25},{9,1},{17,9},{25,17},{2,26},{10... | collective-permute-start | bytes 589832 | tf_op jit(solution)/shard_map/ppermute | solution.py:529
  165.0 9.0 %collective-permute-start.40 = (bf16[128,768]{1,0:T(8,128)(2,1)S(1)}, bf16[128,768]{1,0:T(8,128)(2,1)S(1)}, u32[]{:S(2)}, u32[]{:S(2)}) collective-permute-start(bf16[128,768]{1,0:T(8,128)(2,1)S(1)} %get-tuple-element.67), channel_id=1, source_target_pairs={{0,8},{8,16},{16,24},{24,0},{1,9},{9,17},{17,25},{25,1},{2,10},{10... | collective-permute-start | bytes 589832 | tf_op jit(solution)/shard_map/ppermute | solution.py:529
  165.7 9.4 %collective-permute-start.39 = (bf16[128,768]{1,0:T(8,128)(2,1)S(1)}, bf16[128,768]{1,0:T(8,128)(2,1)S(1)}, u32[]{:S(2)}, u32[]{:S(2)}) collective-permute-start(bf16[128,768]{1,0:T(8,128)(2,1)S(1)} %get-tuple-element.68), channel_id=1, source_target_pairs={{0,16},{8,24},{16,0},{24,8},{1,17},{9,25},{17,1},{25,9},{2,18},{10... | collective-permute-start | bytes 589832 | tf_op jit(solution)/shard_map/ppermute | solution.py:529
  176.7 8.0 %collective-permute-start.43 = (bf16[128,768]{1,0:T(8,128)(2,1)}, bf16[128,768]{1,0:T(8,128)(2,1)}, u32[]{:S(2)}, u32[]{:S(2)}) collective-permute-start(bf16[128,768]{1,0:T(8,128)(2,1)} %get-tuple-element.44), channel_id=1, source_target_pairs={{0,24},{8,0},{16,8},{24,16},{1,25},{9,1},{17,9},{25,17},{2,26},{10... | collective-permute-start | bytes 589832 | tf_op jit(solution)/shard_map/ppermute | solution.py:529
  177.7 10.3 %collective-permute-start.42 = (bf16[128,768]{1,0:T(8,128)(2,1)}, bf16[128,768]{1,0:T(8,128)(2,1)}, u32[]{:S(2)}, u32[]{:S(2)}) collective-permute-start(bf16[128,768]{1,0:T(8,128)(2,1)} %get-tuple-element.44), channel_id=1, source_target_pairs={{0,16},{8,24},{16,0},{24,8},{1,17},{9,25},{17,1},{25,9},{2,18},{10... | collective-permute-start | bytes 589832 | tf_op jit(solution)/shard_map/ppermute | solution.py:529
  178.2 9.7 %collective-permute-start.41 = (bf16[128,768]{1,0:T(8,128)(2,1)}, bf16[128,768]{1,0:T(8,128)(2,1)}, u32[]{:S(2)}, u32[]{:S(2)}) collective-permute-start(bf16[128,768]{1,0:T(8,128)(2,1)} %get-tuple-element.44), channel_id=1, source_target_pairs={{0,8},{8,16},{16,24},{24,0},{1,9},{9,17},{17,25},{25,1},{2,10},{10... | collective-permute-start | bytes 589832 | tf_op jit(solution)/shard_map/ppermute | solution.py:529
  195.8 30.2 %collective-permute-start.75 = (bf16[4,96,768]{2,1,0:T(8,128)(2,1)}, bf16[4,96,768]{2,1,0:T(8,128)(2,1)}, u32[]{:S(2)}, u32[]{:S(2)}) collective-permute-start(bf16[4,96,768]{2,1,0:T(8,128)(2,1)} %fusion.25), channel_id=1, source_target_pairs={{0,1},{1,0},{2,3},{3,2},{4,5},{5,4},{6,7},{7,6},{8,9},{9,8},{10,11... | collective-permute-start | bytes 1769480 | tf_op jit(solution)/shard_map/ppermute | solution.py:526
  197.9 7.9 %collective-permute-start.44 = (bf16[128,768]{1,0:T(8,128)(2,1)S(1)}, bf16[128,768]{1,0:T(8,128)(2,1)S(1)}, u32[]{:S(2)}, u32[]{:S(2)}) collective-permute-start(bf16[128,768]{1,0:T(8,128)(2,1)S(1)} %get-tuple-element.63), channel_id=1, source_target_pairs={{0,24},{8,0},{16,8},{24,16},{1,25},{9,1},{17,9},{25,17},{2,26},{10... | collective-permute-start | bytes 589832 | tf_op jit(solution)/shard_map/ppermute | solution.py:529
  198.2 10.2 %collective-permute-start.46 = (bf16[128,768]{1,0:T(8,128)(2,1)S(1)}, bf16[128,768]{1,0:T(8,128)(2,1)S(1)}, u32[]{:S(2)}, u32[]{:S(2)}) collective-permute-start(bf16[128,768]{1,0:T(8,128)(2,1)S(1)} %get-tuple-element.64), channel_id=1, source_target_pairs={{0,8},{8,16},{16,24},{24,0},{1,9},{9,17},{17,25},{25,1},{2,10},{10... | collective-permute-start | bytes 589832 | tf_op jit(solution)/shard_map/ppermute | solution.py:529
  200.0 9.8 %collective-permute-start.45 = (bf16[128,768]{1,0:T(8,128)(2,1)S(1)}, bf16[128,768]{1,0:T(8,128)(2,1)S(1)}, u32[]{:S(2)}, u32[]{:S(2)}) collective-permute-start(bf16[128,768]{1,0:T(8,128)(2,1)S(1)} %get-tuple-element.65), channel_id=1, source_target_pairs={{0,16},{8,24},{16,0},{24,8},{1,17},{9,25},{17,1},{25,9},{2,18},{10... | collective-permute-start | bytes 589832 | tf_op jit(solution)/shard_map/ppermute | solution.py:529
  202.3 29.1 %collective-permute-start.68 = (bf16[4,4,24,768]{3,2,1,0:T(8,128)(2,1)}, bf16[4,4,24,768]{3,2,1,0:T(8,128)(2,1)}, u32[]{:S(2)}, u32[]{:S(2)}) collective-permute-start(bf16[4,4,24,768]{3,2,1,0:T(8,128)(2,1)} %fusion.24), channel_id=1, source_target_pairs={{0,1},{1,0},{2,3},{3,2},{4,5},{5,4},{6,7},{7,6},{8,9},{9,8},{10,11... | collective-permute-start | bytes 1769480 | tf_op jit(solution)/shard_map/ppermute | solution.py:526
  212.0 7.1 %collective-permute-start.49 = (bf16[192,128]{0,1:T(8,128)(2,1)S(1)}, bf16[192,128]{0,1:T(8,128)(2,1)S(1)}, u32[]{:S(2)}, u32[]{:S(2)}) collective-permute-start(bf16[192,128]{0,1:T(8,128)(2,1)S(1)} %bitcast.347), channel_id=1, source_target_pairs={{0,6},{1,7},{2,0},{3,1},{4,2},{5,3},{6,4},{7,5},{8,14},{9,15},{10,... | collective-permute-start | bytes 147464 | tf_op jit(solution)/shard_map/ppermute | solution.py:523
  212.8 6.3 %collective-permute-start.47 = (bf16[192,128]{0,1:T(8,128)(2,1)S(1)}, bf16[192,128]{0,1:T(8,128)(2,1)S(1)}, u32[]{:S(2)}, u32[]{:S(2)}) collective-permute-start(bf16[192,128]{0,1:T(8,128)(2,1)S(1)} %bitcast.346), channel_id=1, source_target_pairs={{0,2},{1,3},{2,4},{3,5},{4,6},{5,7},{6,0},{7,1},{8,10},{9,11},{10,... | collective-permute-start | bytes 147464 | tf_op jit(solution)/shard_map/ppermute | solution.py:523
  214.1 6.2 %collective-permute-start.48 = (bf16[192,128]{0,1:T(8,128)(2,1)S(1)}, bf16[192,128]{0,1:T(8,128)(2,1)S(1)}, u32[]{:S(2)}, u32[]{:S(2)}) collective-permute-start(bf16[192,128]{0,1:T(8,128)(2,1)S(1)} %bitcast.345), channel_id=1, source_target_pairs={{0,4},{1,5},{2,6},{3,7},{4,0},{5,1},{6,2},{7,3},{8,12},{9,13},{10,... | collective-permute-start | bytes 147464 | tf_op jit(solution)/shard_map/ppermute | solution.py:523
  219.1 62.6 %collective-permute-start.61 = (bf16[4,4,24,768]{3,2,1,0:T(8,128)(2,1)}, bf16[4,4,24,768]{3,2,1,0:T(8,128)(2,1)}, u32[]{:S(2)}, u32[]{:S(2)}) collective-permute-start(bf16[4,4,24,768]{3,2,1,0:T(8,128)(2,1)} %fusion.23), channel_id=1, source_target_pairs={{0,1},{1,0},{2,3},{3,2},{4,5},{5,4},{6,7},{7,6},{8,9},{9,8},{10,11... | collective-permute-start | bytes 1769480 | tf_op jit(solution)/shard_map/ppermute | solution.py:526
  225.9 11.6 %collective-permute-start.50 = (bf16[512,384]{1,0:T(8,128)(2,1)S(1)}, bf16[512,384]{1,0:T(8,128)(2,1)S(1)}, u32[]{:S(2)}, u32[]{:S(2)}) collective-permute-start(bf16[512,384]{1,0:T(8,128)(2,1)S(1)} %fusion.21), channel_id=1, source_target_pairs={{0,1},{1,0},{2,3},{3,2},{4,5},{5,4},{6,7},{7,6},{8,9},{9,8},{10,11... | collective-permute-start | bytes 1179656 | tf_op jit(solution)/shard_map/ppermute | solution.py:526
  229.5 27.7 %collective-permute-start.76 = (bf16[96,768]{1,0:T(8,128)(2,1)}, bf16[96,768]{1,0:T(8,128)(2,1)}, u32[]{:S(2)}, u32[]{:S(2)}) collective-permute-start(bf16[96,768]{1,0:T(8,128)(2,1)} %get-tuple-element.72), channel_id=1, source_target_pairs={{0,2},{1,3},{2,4},{3,5},{4,6},{5,7},{6,0},{7,1},{8,10},{9,11},{10,... | collective-permute-start | bytes 442376 | tf_op jit(solution)/shard_map/ppermute | solution.py:523
  233.5 18.8 %collective-permute-start.69 = (bf16[4,24,768]{2,1,0:T(8,128)(2,1)}, bf16[4,24,768]{2,1,0:T(8,128)(2,1)}, u32[]{:S(2)}, u32[]{:S(2)}) collective-permute-start(bf16[4,24,768]{2,1,0:T(8,128)(2,1)} %get-tuple-element.75), channel_id=1, source_target_pairs={{0,2},{1,3},{2,4},{3,5},{4,6},{5,7},{6,0},{7,1},{8,10},{9,11},{10,... | collective-permute-start | bytes 442376 | tf_op jit(solution)/shard_map/ppermute | solution.py:523
  233.9 20.1 %collective-permute-start.71 = (bf16[4,24,768]{2,1,0:T(8,128)(2,1)}, bf16[4,24,768]{2,1,0:T(8,128)(2,1)}, u32[]{:S(2)}, u32[]{:S(2)}) collective-permute-start(bf16[4,24,768]{2,1,0:T(8,128)(2,1)} %get-tuple-element.76), channel_id=1, source_target_pairs={{0,6},{1,7},{2,0},{3,1},{4,2},{5,3},{6,4},{7,5},{8,14},{9,15},{10,... | collective-permute-start | bytes 442376 | tf_op jit(solution)/shard_map/ppermute | solution.py:523
  237.5 18.5 %collective-permute-start.70 = (bf16[4,24,768]{2,1,0:T(8,128)(2,1)}, bf16[4,24,768]{2,1,0:T(8,128)(2,1)}, u32[]{:S(2)}, u32[]{:S(2)}) collective-permute-start(bf16[4,24,768]{2,1,0:T(8,128)(2,1)} %get-tuple-element.77), channel_id=1, source_target_pairs={{0,4},{1,5},{2,6},{3,7},{4,0},{5,1},{6,2},{7,3},{8,12},{9,13},{10,... | collective-permute-start | bytes 442376 | tf_op jit(solution)/shard_map/ppermute | solution.py:523
  253.0 6.0 %collective-permute-start.78 = (bf16[96,768]{1,0:T(8,128)(2,1)S(1)}, bf16[96,768]{1,0:T(8,128)(2,1)S(1)}, u32[]{:S(2)}, u32[]{:S(2)}) collective-permute-start(bf16[96,768]{1,0:T(8,128)(2,1)S(1)} %copy-done.45), channel_id=1, source_target_pairs={{0,6},{1,7},{2,0},{3,1},{4,2},{5,3},{6,4},{7,5},{8,14},{9,15},{10,... | collective-permute-start | bytes 442376 | tf_op jit(solution)/shard_map/ppermute | solution.py:523
  253.9 13.7 %collective-permute-start.77 = (bf16[96,768]{1,0:T(8,128)(2,1)S(1)}, bf16[96,768]{1,0:T(8,128)(2,1)S(1)}, u32[]{:S(2)}, u32[]{:S(2)}) collective-permute-start(bf16[96,768]{1,0:T(8,128)(2,1)S(1)} %copy-done.44), channel_id=1, source_target_pairs={{0,4},{1,5},{2,6},{3,7},{4,0},{5,1},{6,2},{7,3},{8,12},{9,13},{10,... | collective-permute-start | bytes 442376 | tf_op jit(solution)/shard_map/ppermute | solution.py:523
  256.0 34.3 %collective-permute-start.54 = (bf16[4,4,32,576]{3,2,1,0:T(8,128)(2,1)S(1)}, bf16[4,4,32,576]{3,2,1,0:T(8,128)(2,1)S(1)}, u32[]{:S(2)}, u32[]{:S(2)}) collective-permute-start(bf16[4,4,32,576]{3,2,1,0:T(8,128)(2,1)S(1)} %fusion.22), channel_id=1, source_target_pairs={{0,1},{1,0},{2,3},{3,2},{4,5},{5,4},{6,7},{7,6},{8,9},{9,8},{10,11... | collective-permute-start | bytes 1769480 | tf_op jit(solution)/shard_map/ppermute | solution.py:526
  257.2 25.8 %collective-permute-start.51 = (bf16[128,768]{1,0:T(8,128)(2,1)S(1)}, bf16[128,768]{1,0:T(8,128)(2,1)S(1)}, u32[]{:S(2)}, u32[]{:S(2)}) collective-permute-start(bf16[128,768]{1,0:T(8,128)(2,1)S(1)} %get-tuple-element.60), channel_id=1, source_target_pairs={{0,6},{1,7},{2,0},{3,1},{4,2},{5,3},{6,4},{7,5},{8,14},{9,15},{10,... | collective-permute-start | bytes 589832 | tf_op jit(solution)/shard_map/ppermute | solution.py:523
  259.0 26.9 %collective-permute-start.53 = (bf16[128,768]{1,0:T(8,128)(2,1)S(1)}, bf16[128,768]{1,0:T(8,128)(2,1)S(1)}, u32[]{:S(2)}, u32[]{:S(2)}) collective-permute-start(bf16[128,768]{1,0:T(8,128)(2,1)S(1)} %get-tuple-element.61), channel_id=1, source_target_pairs={{0,2},{1,3},{2,4},{3,5},{4,6},{5,7},{6,0},{7,1},{8,10},{9,11},{10,... | collective-permute-start | bytes 589832 | tf_op jit(solution)/shard_map/ppermute | solution.py:523
  280.8 8.7 %collective-permute-start.52 = (bf16[128,768]{1,0:T(8,128)(2,1)S(1)}, bf16[128,768]{1,0:T(8,128)(2,1)S(1)}, u32[]{:S(2)}, u32[]{:S(2)}) collective-permute-start(bf16[128,768]{1,0:T(8,128)(2,1)S(1)} %get-tuple-element.62), channel_id=1, source_target_pairs={{0,4},{1,5},{2,6},{3,7},{4,0},{5,1},{6,2},{7,3},{8,12},{9,13},{10,... | collective-permute-start | bytes 589832 | tf_op jit(solution)/shard_map/ppermute | solution.py:523
  282.9 10.5 %collective-permute-start.62 = (bf16[4,24,768]{2,1,0:T(8,128)(2,1)S(1)}, bf16[4,24,768]{2,1,0:T(8,128)(2,1)S(1)}, u32[]{:S(2)}, u32[]{:S(2)}) collective-permute-start(bf16[4,24,768]{2,1,0:T(8,128)(2,1)S(1)} %get-tuple-element.78), channel_id=1, source_target_pairs={{0,8},{8,16},{16,24},{24,0},{1,9},{9,17},{17,25},{25,1},{2,10},{10... | collective-permute-start | bytes 442376 | tf_op jit(solution)/shard_map/ppermute | solution.py:529
  283.0 12.0 %collective-permute-start.64 = (bf16[4,24,768]{2,1,0:T(8,128)(2,1)S(1)}, bf16[4,24,768]{2,1,0:T(8,128)(2,1)S(1)}, u32[]{:S(2)}, u32[]{:S(2)}) collective-permute-start(bf16[4,24,768]{2,1,0:T(8,128)(2,1)S(1)} %get-tuple-element.79), channel_id=1, source_target_pairs={{0,24},{8,0},{16,8},{24,16},{1,25},{9,1},{17,9},{25,17},{2,26},{10... | collective-permute-start | bytes 442376 | tf_op jit(solution)/shard_map/ppermute | solution.py:529
  285.9 9.1 %collective-permute-start.63 = (bf16[4,24,768]{2,1,0:T(8,128)(2,1)S(1)}, bf16[4,24,768]{2,1,0:T(8,128)(2,1)S(1)}, u32[]{:S(2)}, u32[]{:S(2)}) collective-permute-start(bf16[4,24,768]{2,1,0:T(8,128)(2,1)S(1)} %get-tuple-element.80), channel_id=1, source_target_pairs={{0,16},{8,24},{16,0},{24,8},{1,17},{9,25},{17,1},{25,9},{2,18},{10... | collective-permute-start | bytes 442376 | tf_op jit(solution)/shard_map/ppermute | solution.py:529
  290.5 8.6 %collective-permute-start.55 = (bf16[4,32,576]{2,1,0:T(8,128)(2,1)S(1)}, bf16[4,32,576]{2,1,0:T(8,128)(2,1)S(1)}, u32[]{:S(2)}, u32[]{:S(2)}) collective-permute-start(bf16[4,32,576]{2,1,0:T(8,128)(2,1)S(1)} %get-tuple-element.69), channel_id=1, source_target_pairs={{0,8},{8,16},{16,24},{24,0},{1,9},{9,17},{17,25},{25,1},{2,10},{10... | collective-permute-start | bytes 442376 | tf_op jit(solution)/shard_map/ppermute | solution.py:529
  290.6 9.7 %collective-permute-start.57 = (bf16[4,32,576]{2,1,0:T(8,128)(2,1)S(1)}, bf16[4,32,576]{2,1,0:T(8,128)(2,1)S(1)}, u32[]{:S(2)}, u32[]{:S(2)}) collective-permute-start(bf16[4,32,576]{2,1,0:T(8,128)(2,1)S(1)} %get-tuple-element.70), channel_id=1, source_target_pairs={{0,24},{8,0},{16,8},{24,16},{1,25},{9,1},{17,9},{25,17},{2,26},{10... | collective-permute-start | bytes 442376 | tf_op jit(solution)/shard_map/ppermute | solution.py:529
  293.5 6.8 %collective-permute-start.56 = (bf16[4,32,576]{2,1,0:T(8,128)(2,1)S(1)}, bf16[4,32,576]{2,1,0:T(8,128)(2,1)S(1)}, u32[]{:S(2)}, u32[]{:S(2)}) collective-permute-start(bf16[4,32,576]{2,1,0:T(8,128)(2,1)S(1)} %get-tuple-element.71), channel_id=1, source_target_pairs={{0,16},{8,24},{16,0},{24,8},{1,17},{9,25},{17,1},{25,9},{2,18},{10... | collective-permute-start | bytes 442376 | tf_op jit(solution)/shard_map/ppermute | solution.py:529
  295.2 8.1 %collective-permute-start.65 = (bf16[24,768]{1,0:T(8,128)(2,1)S(1)}, bf16[24,768]{1,0:T(8,128)(2,1)S(1)}, u32[]{:S(2)}, u32[]{:S(2)}) collective-permute-start(bf16[24,768]{1,0:T(8,128)(2,1)S(1)} %get-tuple-element.113), channel_id=1, source_target_pairs={{0,2},{1,3},{2,4},{3,5},{4,6},{5,7},{6,0},{7,1},{8,10},{9,11},{10,... | collective-permute-start | bytes 110600 | tf_op jit(solution)/shard_map/ppermute | solution.py:523
  300.4 7.7 %collective-permute-start.58 = (bf16[32,576]{1,0:T(8,128)(2,1)S(1)}, bf16[32,576]{1,0:T(8,128)(2,1)S(1)}, u32[]{:S(2)}, u32[]{:S(2)}) collective-permute-start(bf16[32,576]{1,0:T(8,128)(2,1)S(1)} %get-tuple-element.105), channel_id=1, source_target_pairs={{0,6},{1,7},{2,0},{3,1},{4,2},{5,3},{6,4},{7,5},{8,14},{9,15},{10,... | collective-permute-start | bytes 110600 | tf_op jit(solution)/shard_map/ppermute | solution.py:523
  304.6 6.8 %collective-permute-start.60 = (bf16[32,576]{1,0:T(8,128)(2,1)S(1)}, bf16[32,576]{1,0:T(8,128)(2,1)S(1)}, u32[]{:S(2)}, u32[]{:S(2)}) collective-permute-start(bf16[32,576]{1,0:T(8,128)(2,1)S(1)} %get-tuple-element.103), channel_id=1, source_target_pairs={{0,2},{1,3},{2,4},{3,5},{4,6},{5,7},{6,0},{7,1},{8,10},{9,11},{10,... | collective-permute-start | bytes 110600 | tf_op jit(solution)/shard_map/ppermute | solution.py:523
  (76 other events, 474.3 us)

commit v2 on v0

--- a/solution.py
+++ b/solution.py
@@ -1,6 +1,11 @@
+import functools
+import math
+
 import jax
 import jax.numpy as jnp
 from jax import lax
+from jax.experimental import pallas as pl
+from jax.experimental.pallas import tpu as pltpu
 from jax.sharding import PartitionSpec as P
 
 HEADS = 12
@@ -296,6 +301,739 @@
     )
 
 
+def normal_parts(resid):
+    center = resid - jnp.mean(resid, -1, keepdims=True)
+    spread = jnp.mean(center * center, -1, keepdims=True)
+    scale = lax.rsqrt(spread + epsilon)
+    return center * scale, scale
+
+
+def normal_back(hat, scale, grad):
+    inner = jnp.mean(grad * hat, -1, keepdims=True)
+    return scale * (grad - jnp.mean(grad, -1, keepdims=True) - hat * inner)
+
+
+def dot(left, right, dims=((1,), (0,))):
+    return lax.dot_general(left, right, (dims, ((), ())), preferred_element_type=jnp.float32)
+
+
+def head_rows(block, head, extra):
+    row = lax.broadcasted_iota(jnp.int32, block.shape, 0)
+    keep = (row >= head * HEAD_DIM) & (row < (head + 1) * HEAD_DIM)
+    if extra:
+        keep = keep | (row >= extra)
+    return jnp.where(keep, block, jnp.zeros_like(block))
+
+
+def head_lanes(block, head):
+    lane = lax.broadcasted_iota(jnp.int32, block.shape, 1)
+    keep = (lane >= head * HEAD_DIM) & (lane < (head + 1) * HEAD_DIM)
+    return jnp.where(keep, block, jnp.zeros_like(block))
+
+
+def copied_kernel(kernel, first, far, count, shapes, *refs):
+    operands, refs = refs[:count], refs[count:]
+    results, refs = refs[: len(shapes)], refs[len(shapes) :]
+    moved = [i for i in range(count) if i >= first and i not in far]
+    taken, refs = refs[: len(moved)], refs[len(moved) :]
+    given, refs = refs[: len(shapes)], refs[len(shapes) :]
+    coming, going, rest = refs[0], refs[1], refs[2:]
+    local = list(operands)
+    copies = []
+    for index, at in enumerate(moved):
+        copies.append(pltpu.make_async_copy(operands[at], taken[index], coming.at[index]))
+        local[at] = taken[index]
+    for copy in copies:
+        copy.start()
+    for copy in copies:
+        copy.wait()
+    copies = [
+        pltpu.make_async_copy(given[index], results[index], going.at[index])
+        for index in range(len(shapes))
+    ]
+    kernel(*local, *given, *rest, leave=lambda *which: [copies[index].start() for index in which])
+    for copy in copies:
+        copy.wait()
+
+
+def one_step(
+    kernel, operands, shapes, flops, name, first=1, far=(), scratch=(), exps=0, limit=14
+):
+    specs = []
+    for index in range(len(operands)):
+        if index < first:
+            specs.append(pl.BlockSpec(memory_space=pltpu.SMEM))
+        elif index in far:
+            specs.append(pl.BlockSpec(memory_space=pl.ANY))
+        else:
+            specs.append(pl.BlockSpec(memory_space=pltpu.HBM))
+    moved = [
+        pltpu.VMEM(operand.shape, operand.dtype)
+        for index, operand in enumerate(operands)
+        if index >= first and index not in far
+    ]
+    given = [pltpu.VMEM(*shape) for shape in shapes]
+    return pl.pallas_call(
+        functools.partial(copied_kernel, kernel, first, far, len(operands), shapes),
+        in_specs=specs,
+        out_specs=[pl.BlockSpec(memory_space=pltpu.HBM)] * len(shapes),
+        out_shape=[pltpu.HBM(*shape) for shape in shapes],
+        scratch_shapes=moved
+        + given
+        + [pltpu.SemaphoreType.DMA((len(moved),)), pltpu.SemaphoreType.DMA((len(shapes),))]
+        + list(scratch),
+        compiler_params=pltpu.CompilerParams(vmem_limit_bytes=limit * 2**20),
+        cost_estimate=pl.CostEstimate(
+            flops=flops,
+            bytes_accessed=sum(operand.size * operand.dtype.itemsize for operand in operands),
+            transcendentals=exps,
+        ),
+        name=name,
+    )(*operands)
+
+
+def turn(block):
+    return jnp.transpose(block.astype(jnp.float32)).astype(block.dtype)
+
+
+def attend_kernel(heads, chips, places, *refs, leave):
+    own, others = refs[:chips], refs[chips : 2 * chips]
+    weight, bias_query, bias_value = refs[2 * chips : 2 * chips + 3]
+    refs = refs[2 * chips + 3 :]
+    mine_ref, query, key, value, att, log = refs[:6]
+    sent, (every, query_t, value_t, mixed) = refs[6 : 6 + chips], refs[6 + chips :]
+    low, f32 = jnp.bfloat16, jnp.float32
+    width = heads * HEAD_DIM
+    count, rows, depth = every.shape
+    spare = key.shape[1] - width
+
+    for distance in range(chips):
+        slot = lax.rem(places[0] - distance + chips, chips)
+        every[slot] = own[distance][:rows, :]
+        every[chips + slot] = others[distance][:rows, :]
+    tokens = every[...].reshape(count * rows, depth)
+    mine = chips * rows
+    mine_ref[...] = tokens[:mine]
+    first = dot(tokens[:mine], weight[:, :width]) + bias_query[...]
+    first = (first.astype(low).astype(f32) * HEAD_DIM ** (-0.5)).astype(low)
+    query[...] = first
+    one = lax.broadcasted_iota(jnp.int32, (spare, mine), 0) == 0
+    query_t[...] = jnp.concatenate([turn(first), jnp.where(one, 1.0, 0.0).astype(low)], 0)
+    second = dot(tokens, weight[:, width : 2 * width]).astype(low)
+    row = lax.broadcasted_iota(jnp.int32, (rows, spare), 0)
+    lane = lax.broadcasted_iota(jnp.int32, (rows, spare), 1)
+    for block in range(count):
+        hide = jnp.where((row < places[1 + block]) | (lane > 0), 0.0, masked_score)
+        at = slice(block * rows, (block + 1) * rows)
+        key[at, :] = jnp.concatenate([second[at].astype(f32), hide], 1).astype(low)
+    third = (dot(tokens, weight[:, 2 * width :]) + bias_value[...]).astype(low)
+    value[...] = third
+    value_t[...] = turn(third)
+    leave(0, 1, 2, 3)
+
+    pieces = 2 if chips % 2 == 0 else 1
+    for step in range(chips // pieces):
+        span = slice(step * pieces * rows, (step + 1) * pieces * rows)
+        for head in range(heads):
+            scores = dot(key[...], head_rows(query_t[:, span], head, width))
+            top = jnp.max(scores, 0, keepdims=True)
+            expos = jnp.exp(scores - top)
+            total = jnp.sum(expos, 0, keepdims=True)
+            at = slice(head * HEAD_DIM, (head + 1) * HEAD_DIM)
+            summed = dot(value_t[at, :], expos.astype(low)) / total
+            att[at, span] = summed
+            for piece in range(pieces):
+                mixed[step * pieces + piece, at, :] = summed[
+                    :, piece * rows : (piece + 1) * rows
+                ].astype(low)
+            log[head : head + 1, span] = top + jnp.log(total)
+    for distance in range(chips):
+        sent[distance][...] = mixed[lax.rem(places[0] + distance, chips)]
+    leave(*range(4, 6 + chips))
+
+
+def attend(heads, places, own, others, weight, bias_query, bias_value):
+    chips = len(own)
+    rows, depth = own[0].shape
+    count = 2 * chips
+    mine, keys = chips * rows, count * rows
+    width = heads * HEAD_DIM
+    wide = -(-(width + 1) // 128) * 128
+    low, f32 = jnp.bfloat16, jnp.float32
+    return one_step(
+        functools.partial(attend_kernel, heads, chips),
+        [places, *own, *others, weight, bias_query, bias_value],
+        [
+            ((mine, depth), low),
+            ((mine, width), low),
+            ((keys, wide), low),
+            ((keys, width), low),
+            ((width, mine), f32),
+            ((heads, mine), f32),
+        ]
+        + [((width, rows), low)] * chips,
+        flops=4 * heads * mine * keys * 256 + 6 * keys * depth * width,
+        name="attend",
+        scratch=[
+            pltpu.VMEM((count, rows, depth), low),
+            pltpu.VMEM((wide, mine), low),
+            pltpu.VMEM((width, keys), low),
+            pltpu.VMEM((chips, width, rows), low),
+        ],
+        exps=heads * mine * keys,
+    )
+
+
+def attend_back_kernel(heads, chips, places, query, key, value, att, log, *refs, leave):
+    come_refs, refs = refs[:chips], refs[chips + 1 :]
+    query_grad, kept, away, key_sum, value_sum, grad_t, query_t, key_t = refs
+    low = jnp.bfloat16
+    width, rows = come_refs[0].shape
+    mine = chips * rows
+    for distance in range(chips):
+        slot = lax.rem(places[0] - distance + chips, chips)
+        grad_t[slot] = come_refs[distance][...]
+    one = lax.broadcasted_iota(jnp.int32, (key.shape[1] - width, mine), 0) == 0
+    query_t[...] = jnp.concatenate([turn(query[...]), jnp.where(one, 1.0, 0.0).astype(low)], 0)
+    key_t[...] = turn(key[:, :width])
+    pieces = 2 if chips % 2 == 0 else 1
+    for step in range(chips // pieces):
+        span = slice(step * pieces * rows, (step + 1) * pieces * rows)
+        come = jnp.concatenate([grad_t[step * pieces + piece] for piece in range(pieces)], 1)
+        come_rows = turn(come)
+        turned = []
+        for head in range(heads):
+            at = slice(head * HEAD_DIM, (head + 1) * HEAD_DIM)
+            scores = dot(key[...], head_rows(query_t[:, span], head, width))
+            probs = jnp.exp(scores - log[head : head + 1, span])
+            prob_grad = dot(value[...], head_rows(come, head, 0))
+            delta = jnp.sum(come[at].astype(jnp.float32) * att[at, span], 0, keepdims=True)
+            score_grad = (probs * (prob_grad - delta)).astype(low)
+            turned.append(dot(key_t[at, :], score_grad))
+            key_term = dot(score_grad, head_lanes(query[span, :], head))
+            value_term = dot(probs.astype(low), head_lanes(come_rows, head))
+            if step == 0 and head == 0:
+                key_sum[...] = key_term
+                value_sum[...] = value_term
+            else:
+                key_sum[...] += key_term
+                value_sum[...] += value_term
+        gathered = jnp.concatenate(turned, 0) * HEAD_DIM ** (-0.5)
+        query_grad[span, :] = jnp.transpose(gathered).astype(low)
+    kept[...] = jnp.concatenate([key_sum[:mine, :], value_sum[:mine, :]], 1)
+    away[...] = jnp.concatenate([key_sum[mine:, :], value_sum[mine:, :]], 1).astype(low)
+    leave(0, 1, 2)
+
+
+def attend_back(heads, places, query, key, value, att, log, come, marker):
+    chips = len(come)
+    mine, width = query.shape
+    keys, wide = key.shape
+    low, f32 = jnp.bfloat16, jnp.float32
+    return one_step(
+        functools.partial(attend_back_kernel, heads, chips),
+        [places, query, key, value, att, log, *come, marker],
+        [((mine, width), low), ((mine, 2 * width), f32), ((keys - mine, 2 * width), low)],
+        flops=10 * heads * mine * keys * 256,
+        name="attend_back",
+        far=(6 + chips,),
+        scratch=[
+            pltpu.VMEM((keys, width), f32),
+            pltpu.VMEM((keys, width), f32),
+            pltpu.VMEM((chips, width, mine // chips), low),
+            pltpu.VMEM((wide, mine), low),
+            pltpu.VMEM((width, keys), low),
+        ],
+        exps=heads * mine * keys,
+    )
+
+
+def finish_kernel(
+    chips, places, mine, weight, query_grad, kept, come, short, *refs, leave
+):
+    low, f32 = jnp.bfloat16, jnp.float32
+    sent, (own_terms, away_terms, terms, blocks) = refs[:chips], refs[chips:]
+    owners, _, part, width = terms.shape
+    pair = (kept[...] + come[...].astype(f32)).astype(low)
+    grads = jnp.concatenate([query_grad[...].astype(f32), pair.astype(f32)], 1)
+    sums = jnp.sum(grads, 0, keepdims=True)
+    grads = grads.astype(low)
+    part_grad = dot(grads, weight[...], ((1,), (1,))).astype(low)
+    blocks[...] = part_grad.reshape(blocks.shape)
+    for distance in range(chips):
+        sent[distance][...] = blocks[lax.rem(places[0] + distance, chips)]
+        leave(distance)
+    terms[...] = dot(mine[...], grads, ((0,), (0,))).reshape(terms.shape)
+    core = places[1]
+    count = short.shape[2]
+    row = lax.broadcasted_iota(jnp.int32, (count, width), 0)
+    below = jnp.where(row == count - 1, sums, 0.0)
+    for index, ref, which in ((1, away_terms, 1 - core), (0, own_terms, core)):
+        for owner in range(owners):
+            block = [terms[owner, which], short[owner, which] + below]
+            ref[owner] = jnp.concatenate(block, 0).astype(ref.dtype)
+        leave(chips + index)
+
+
+def finish(chips, places, mine, weight, query_grad, kept, come, short):
+    count, depth = mine.shape
+    width = weight.shape[1]
+    owners = short.shape[0]
+    part = depth // (2 * owners)
+    held = part + short.shape[2]
+    block = (count // chips, depth)
+    return one_step(
+        functools.partial(finish_kernel, chips),
+        [places, mine, weight, query_grad, kept, come, short],
+        [
+            *[(block, jnp.bfloat16)] * chips,
+            ((owners, held, width), jnp.float32),
+            ((owners, held, width), jnp.bfloat16),
+        ],
+        flops=4 * count * depth * width,
+        name="finish",
+        scratch=[
+            pltpu.VMEM((owners, 2, part, width), jnp.float32),
+            pltpu.VMEM((chips, *block), jnp.bfloat16),
+        ],
+    )
+
+
+def bundle_kernel(own, come, w_out, w_up, out, leave):
+    f32 = jnp.float32
+    teams, chips, part, width = w_out.shape
+    owners, held, group = own.shape
+    for team in range(teams):
+        for chip in range(chips):
+            owner = team * chips + chip
+            block = own[owner] + come[owner].astype(f32)
+            block = jnp.pad(block, ((0, 0), (0, width - group)))
+            start = chip * (held + part)
+            both = jnp.concatenate([block, w_out[team, chip].astype(f32)], 0)
+            out[team, start : start + held + part] = both.astype(out.dtype)
+        out[team, chips * (held + part) :] = w_up[team]
+    leave(0)
+
+
+def bundle(own, come, w_out, w_up):
+    teams, chips, part, width = w_out.shape
+    held = own.shape[1]
+    shape = (teams, chips * (held + part) + part, width)
+    return one_step(
+        bundle_kernel,
+        [own, come, w_out, w_up],
+        [(shape, jnp.bfloat16)],
+        flops=0,
+        limit=8,
+        name="bundle",
+        first=0,
+    )[0]
+
+
+def unpack_kernel(part, group, found, *outs, leave):
+    chips, count, _ = found.shape
+    blocks = [found[chip].astype(jnp.float32) for chip in range(chips)]
+    for index in range(3):
+        columns = slice(index * group, (index + 1) * group)
+        outs[index][...] = jnp.concatenate([block[:part, columns] for block in blocks], 1)
+    total = blocks[0]
+    for block in blocks[1:]:
+        total = total + block
+    outs[3][...] = total[count - part :]
+    outs[4][...] = total[part : count - part]
+    outs[5][...] = jnp.concatenate([b[count - part - 1 : count - part] for b in blocks], 0)
+    leave(*range(6))
+
+
+def unpack(part, group, found):
+    chips, count, width = found.shape
+    shapes = [((part, width), jnp.float32)] * 4
+    shapes.append(((count - 2 * part, width), jnp.float32))
+    shapes.append(((chips, width), jnp.float32))
+    return one_step(
+        functools.partial(unpack_kernel, part, group),
+        [found],
+        shapes,
+        flops=found.size,
+        limit=8,
+        name="unpack",
+        first=0,
+    )
+
+
+def wait_kernel(*refs):
+    pass
+
+
+def after(block, *others):
+    anywhere = pl.BlockSpec(memory_space=pl.ANY)
+    return pl.pallas_call(
+        wait_kernel,
+        in_specs=[anywhere] * (1 + len(others)),
+        out_specs=anywhere,
+        out_shape=jax.ShapeDtypeStruct(block.shape, block.dtype),
+        input_output_aliases={0: 0},
+        compiler_params=pltpu.CompilerParams(vmem_limit_bytes=2**20),
+        name="after",
+    )(block, *others)
+
+
+def lay_kernel(tokens, w_out, both):
+    both[...] = jnp.concatenate([tokens[...], w_out[...]], 0)
+
+
+def lay(tokens, w_out):
+    shape = (tokens.shape[0] + w_out.shape[0], tokens.shape[1])
+    return pl.pallas_call(
+        lay_kernel,
+        in_specs=[pl.BlockSpec(memory_space=pltpu.VMEM)] * 2,
+        out_specs=pl.BlockSpec(memory_space=pltpu.VMEM),
+        out_shape=jax.ShapeDtypeStruct(shape, tokens.dtype),
+        name="lay",
+    )(tokens, w_out)
+
+
+def pack_kernel(chips, w_query, w_key, w_value, vectors, b_up, out):
+    part = w_query.shape[0]
+    group = w_query.shape[1] // chips
+    count = vectors.shape[0]
+    rest = out.shape[1] - part
+    short = jnp.concatenate(
+        [
+            jnp.pad(vectors[...].astype(jnp.float32), ((0, rest - count), (0, 128 - part))),
+            jnp.pad(
+                b_up[...].astype(jnp.float32),
+                ((0, rest - 1), (0, 3 * group - 128 - b_up.shape[1])),
+            ),
+        ],
+        1,
+    )
+    for index in range(chips):
+        columns = slice(index * group, (index + 1) * group)
+        block = jnp.concatenate(
+            [item[:, columns].astype(jnp.float32) for item in (w_query, w_key, w_value)], 1
+        )
+        both = jnp.concatenate([block, short], 0)
+        spare = out.shape[2] - both.shape[1]
+        out[index] = jnp.pad(both, ((0, 0), (0, spare))).astype(jnp.bfloat16)
+
+
+def pack(chips, w_query, w_key, w_value, vectors, b_up, held):
+    part, width = w_query.shape
+    return pl.pallas_call(
+        functools.partial(pack_kernel, chips),
+        in_specs=[pl.BlockSpec(memory_space=pltpu.VMEM)] * 5,
+        out_specs=pl.BlockSpec(memory_space=pltpu.VMEM),
+        out_shape=jax.ShapeDtypeStruct((chips, held, width), jnp.bfloat16),
+        name="pack",
+    )(w_query, w_key, w_value, vectors, b_up)
+
+
+def share_kernel(packed, w_up, out):
+    teams, count, width = out.shape
+    chips, held, _ = packed.shape
+    for team in range(teams):
+        for chip in range(chips):
+            out[team, chip * held : (chip + 1) * held] = packed[chip]
+        out[team, chips * held :] = w_up[:, team * width : (team + 1) * width]
+
+
+def share(teams, packed, w_up):
+    chips, held, width = packed.shape
+    part, hidden = w_up.shape
+    return pl.pallas_call(
+        share_kernel,
+        in_specs=[pl.BlockSpec(memory_space=pltpu.VMEM)] * 2,
+        out_specs=pl.BlockSpec(memory_space=pltpu.VMEM),
+        out_shape=jax.ShapeDtypeStruct(
+            (teams, chips * held + part, hidden // teams), jnp.bfloat16
+        ),
+        name="share",
+    )(packed, w_up)
+
+
+def pick(blocks, index, axis=0):
+    return lax.dynamic_index_in_dim(blocks, index, axis, keepdims=False)
+
+
+def ordered(found, me):
+    count = len(found)
+    rising = [found[count - 1 - i] for i in range(count)]
+    twice = jnp.stack(rising + rising[:-1], 0)
+    return lax.dynamic_slice_in_dim(twice, count - 1 - me, count, 0)
+
+
+def layer_split(
+    tokens,
+    lengths,
+    w_query,
+    b_query,
+    w_key,
+    w_value,
+    b_value,
+    w_out,
+    b_out,
+    gain_one,
+    shift_one,
+    w_up,
+    b_up,
+    w_down,
+    b_down,
+    gain_two,
+    shift_two,
+    cotangent,
+):
+    f32, low = jnp.float32, jnp.bfloat16
+    teams = lax.axis_size("batch")
+    chips = lax.axis_size("ctx") // 2
+    team = lax.axis_index("batch")
+    place = lax.axis_index("ctx")
+    chip, core = place // 2, place % 2
+    rows, width = tokens.shape
+    part = w_query.shape[0]
+    hidden = w_up.shape[1]
+    quarter = hidden // teams
+    heads = HEADS // chips
+    group = heads * HEAD_DIM
+    length = lengths[0]
+
+    def to_chip(block, distance):
+        route = [(i, (i // 2 + distance) % chips * 2 + i % 2) for i in range(2 * chips)]
+        return lax.ppermute(block, "ctx", route)
+
+    def to_core(block):
+        return lax.ppermute(block, "ctx", [(i, i ^ 1) for i in range(2 * chips)])
+
+    def to_team(block, distance):
+        return lax.ppermute(block, "batch", [(i, (i + distance) % teams) for i in range(teams)])
+
+    def from_chips(block):
+        return [block] + [to_chip(block, d) for d in range(1, chips)]
+
+    def from_teams(block):
+        return [block] + [to_team(block, d) for d in range(1, teams)]
+
+    def swap_chips(blocks, axis=0):
+        return [pick(blocks, chip, axis)] + [
+            to_chip(pick(blocks, (chip + d) % chips, axis), d) for d in range(1, chips)
+        ]
+
+    def swap_teams(blocks, axis=0):
+        return [pick(blocks, team, axis)] + [
+            to_team(pick(blocks, (team + d) % teams, axis), d) for d in range(1, teams)
+        ]
+
+    same_core = [[2 * z + c for z in range(chips)] for c in range(2)]
+
+    def trade_chips(blocks):
+        return lax.all_to_all(blocks, "ctx", 0, 0, axis_index_groups=same_core)
+
+    def trade_teams(blocks):
+        return lax.all_to_all(blocks, "batch", 0, 0)
+
+    def both_cores(block, axis):
+        other = to_core(block)
+        first = jnp.where(core == 0, block, other)
+        second = jnp.where(core == 0, other, block)
+        return jnp.stack([first, second], axis)
+
+    def cores_sum(terms, axis):
+        away = to_core(pick(terms, 1 - core, axis).astype(low))
+        return pick(terms, core, axis).astype(f32) + away.astype(f32)
+
+    def total(blocks):
+        result = blocks[0].astype(f32)
+        for block in blocks[1:]:
+            result = result + block.astype(f32)
+        return result
+
+    def return_teams(blocks):
+        return total(
+            [blocks[0]] + [to_team(blocks[d].astype(low), -d) for d in range(1, teams)]
+        )
+
+    vectors = (
+        b_query,
+        b_value,
+        b_out,
+        gain_one,
+        shift_one,
+        b_down,
+        gain_two,
+        shift_two,
+    )
+    held = -(-(part + len(vectors)) // 16) * 16
+    laid = lay(tokens, w_out)
+    packed = pack(
+        chips,
+        w_query,
+        w_key,
+        w_value,
+        jnp.stack(vectors),
+        b_up[None],
+        held,
+    )
+    packed = trade_chips(packed)
+    pieces = from_chips(after(laid, packed))
+    traded = trade_teams(share(teams, packed, w_up))
+    up_blocks = traded[:, chips * held :]
+    packed = both_cores(traded[:, : chips * held].reshape(teams, chips, held, width), 2)
+    w_heads = packed[:, :, :, :part, : 3 * group].reshape(width, 3 * group)
+    shorts = packed[:, :, :, part:].reshape(teams * chips * 2, held - part, width)
+
+    rows_of = shorts[:, :, :part].transpose(1, 0, 2).reshape(held - part, width)
+    bias_query, bias_value, bias_out, gain_first, shift_first = rows_of[:5].astype(f32)
+    bias_down, gain_second, shift_second = rows_of[5:8].astype(f32)
+    bias_up = shorts[:, 0, 128 : 128 + b_up.shape[0]].reshape(-1).astype(f32)
+    bias_up = lax.dynamic_slice_in_dim(bias_up, team * quarter, quarter)
+    bias_query = lax.dynamic_slice_in_dim(bias_query, chip * group, group)
+    bias_value = lax.dynamic_slice_in_dim(bias_value, chip * group, group)
+
+    others = [to_core(tokens)] + [to_core(piece) for piece in pieces[1:]]
+    starts = jnp.arange(chips, dtype=jnp.int32) * (2 * rows)
+    starts = jnp.concatenate([starts + core * rows, starts + (1 - core) * rows])
+    places = jnp.concatenate([chip[None], length - starts])
+
+    out_rel = [w_out] + [piece[rows:] for piece in pieces[1:]]
+    later = jnp.concatenate([up_blocks.reshape(teams * part, quarter), w_down], 0)
+    later = lax.all_gather(later, "ctx", axis=0)
+    out_blocks = after(ordered(out_rel, chip), w_heads)
+    out_blocks = trade_teams(jnp.broadcast_to(out_blocks[None], (teams,) + out_blocks.shape))
+
+    mine, query, key, value, attended, log_total, *mixed_out = attend(
+        heads,
+        places,
+        [tokens] + pieces[1:],
+        others,
+        w_heads,
+        bias_query[None],
+        bias_value[None],
+    )
+    up_part = later[:, : teams * part].reshape(2 * chips, teams, part, quarter)
+    up_part = up_part.transpose(1, 0, 2, 3).reshape(width, quarter)
+    down_part = later[:, teams * part :].reshape(quarter, width)
+    out_full = both_cores(after(out_blocks, log_total), 2).reshape(width, width)
+
+    tn = ((0,), (0,))
+    mixed_rel = [mixed_out[0]] + [to_chip(mixed_out[d], d) for d in range(1, chips)]
+    mixed_t = ordered(mixed_rel, chip).reshape(width, rows)
+    projected = dot(mixed_t, out_full, tn) + bias_out
+    hat_one, scale_one = normal_parts(tokens.astype(f32) + projected)
+    first = hat_one * gain_first + shift_first
+    first_low = first.astype(low)
+
+    wide = jnp.concatenate(from_teams(first_low), 0)
+    inner = dot(wide, up_part) + bias_up
+    cdf = 0.5 * (1.0 + lax.erf(inner * 2.0**-0.5))
+    slope = cdf + inner * (jnp.exp(-0.5 * inner * inner) * (2.0 * math.pi) ** -0.5)
+    active_low = (inner * cdf).astype(low)
+    active_low, slope = lax.optimization_barrier((active_low, slope))
+    branch_part = dot(active_low, down_part)
+    branch = return_teams(branch_part.reshape(teams, rows, width)) + bias_down
+    hat_two, scale_two = normal_parts(first + branch)
+    output = (hat_two * gain_second + shift_second).astype(low)
+    grad_out = cotangent.astype(f32)
+    grad_gain_two = jnp.sum(grad_out * hat_two, 0)
+    grad_shift_two = jnp.sum(grad_out, 0)
+    grad_second = normal_back(hat_two, scale_two, grad_out * gain_second)
+    branch_grad = grad_second.astype(low)
+    grad_b_down = jnp.sum(branch_grad.astype(f32), 0)
+    wide_grad = jnp.concatenate(from_teams(branch_grad), 0)
+    active_grad = dot(wide_grad, down_part, ((1,), (1,)))
+    inner_grad = (active_grad * slope).astype(low)
+    first_part = dot(inner_grad, up_part, ((1,), (1,))).astype(low)
+    first_part = first_part.reshape(teams, rows, width)
+    leaving = [first_part[d] for d in range(teams)]
+    come_back = [to_team(leaving[d], -d) for d in range(1, teams)]
+    first_grad = total([leaving[0]] + come_back) + grad_second
+    grad_b_up = jnp.sum(inner_grad.astype(f32), 0)
+    grad_down = dot(active_low, after(wide_grad, leaving[1]), tn)
+    grad_up = dot(wide, after(inner_grad, leaving[1]), tn)
+
+    grad_gain_one = jnp.sum(first_grad * hat_one, 0)
+    grad_shift_one = jnp.sum(first_grad, 0)
+    grad_first = normal_back(hat_one, scale_one, first_grad * gain_first)
+    proj_grad = grad_first.astype(low)
+    grad_b_out = jnp.sum(proj_grad.astype(f32), 0)
+    mixed_grad_t = dot(out_full, proj_grad, ((1,), (1,))).astype(low)
+    mixed_grad_t = mixed_grad_t.reshape(chips, group, rows)
+    leaving = [pick(mixed_grad_t, (chip + d) % chips) for d in range(chips)]
+    grad_out_w = dot(mixed_t, after(proj_grad, leaving[1]))
+    out_sum = cores_sum(grad_out_w.reshape(teams, chips, 2, part, width), 2).astype(low)
+
+    come = [leaving[0]] + [to_chip(leaving[d], d) for d in range(1, chips)]
+    query_grad, kept, away = attend_back(
+        heads, places, query, key, value, attended, log_total, come, out_sum
+    )
+    up_terms = grad_up.astype(low).reshape(teams, 2 * chips, part, quarter)
+    up_terms = up_terms.transpose(1, 0, 2, 3).reshape(2 * chips, teams * part, quarter)
+    down_terms = grad_down.astype(low).reshape(2 * chips, -1, width)
+    sums = lax.psum_scatter(
+        jnp.concatenate([up_terms, down_terms], 1), "ctx", scatter_dimension=0, tiled=False
+    )
+    up_sum = sums[: teams * part].reshape(teams, part, quarter)
+
+    small = (
+        grad_b_out,
+        grad_gain_one,
+        grad_shift_one,
+        grad_b_down,
+        grad_gain_two,
+        grad_shift_two,
+    )
+    small = jnp.stack([item.reshape(teams * chips, 2, part) for item in small], 2)
+    small = jnp.pad(small, ((0, 0),) * 2 + ((0, held - part - len(vectors) + 2), (0, 128 - part)))
+    tall = lax.dynamic_update_slice_in_dim(
+        jnp.zeros((hidden,), f32), grad_b_up, team * quarter, 0
+    ).reshape(teams * chips, 2, 1, -1)
+    lanes = 3 * group - 128 - tall.shape[-1]
+    tall = jnp.pad(tall, ((0, 0),) * 2 + ((0, held - part - 1), (0, lanes)))
+    *token_part, own_terms, away_terms = finish(
+        chips,
+        jnp.stack([chip, core]),
+        mine,
+        w_heads,
+        query_grad,
+        kept,
+        to_core(away),
+        jnp.concatenate([small, tall], 3),
+    )
+    token_come = [to_chip(token_part[d], d) for d in range(1, chips)]
+    token_grad = grad_first + total([token_part[0]] + token_come)
+    grad_tokens = token_grad.astype(low)
+
+    traded = bundle(own_terms, to_core(away_terms), out_sum, up_sum)
+    traded = trade_teams(traded)
+    out_up = traded[:, -part:].transpose(1, 0, 2).reshape(part, hidden).astype(f32)
+    terms = jnp.sum(traded[:, :-part].astype(f32), 0).astype(low)
+    out_down = after(sums, traded)[teams * part :].astype(f32)
+    found = trade_chips(after(terms.reshape(chips, held + part, width), grad_tokens))
+    out_query, out_key, out_value, out_out, short_sum, sums = unpack(part, group, found)
+    vec = [short_sum[i, :part] for i in range(6)]
+    out_b_up = short_sum[0, 128 : 128 + b_up.shape[0]]
+    own_sums = lax.dynamic_slice(sums, (team, 0), (1, 3 * group))[0].reshape(3, group)
+    own_sums = lax.dynamic_slice(own_sums, (0, place * part), (3, part))
+    return (
+        output,
+        grad_tokens,
+        out_query,
+        own_sums[0],
+        out_key,
+        out_value,
+        own_sums[2],
+        out_out,
+        vec[0],
+        vec[1],
+        vec[2],
+        out_up,
+        out_b_up,
+        out_down,
+        vec[3],
+        vec[4],
+        vec[5],
+    )
+
+
 def solution(mesh):
     in_specs = (
         P(("batch", "ctx"), None),
@@ -336,4 +1074,7 @@
         P(("batch", "ctx")),
         P(("batch", "ctx")),
     )
-    return jax.shard_map(body, mesh=mesh, in_specs=in_specs, out_specs=out_specs, check_vma=False)
+    places = mesh.shape["ctx"]
+    whole_heads = places % 2 == 0 and HEADS % (places // 2) == 0
+    step = layer_split if whole_heads else body
+    return jax.shard_map(step, mesh=mesh, in_specs=in_specs, out_specs=out_specs, check_vma=False)

time: 1190 us -> 241 us (0.20)
  waiting for transfers between devices: 963 us -> 85.1 us
  blocking collectives: 80.6 us -> 0 us
  matrix products: 68.3 us -> 11.6 us
  starting transfers between devices: 7.16 us -> 52.2 us
  Pallas kernels: 0 us -> 28.8 us
    reduce_scatter x3 -> x1, waiting for transfers between devices: 388 us -> 0.01 us  [layer_split(): lax.psum_scatter(jnp.concatenate([up_terms, down_terms], 1), 'ctx', scatt...]
    all_gather x6 -> x1, waiting for transfers between devices: 223 us -> 0.01 us  [layer_split(): later = lax.all_gather(later, 'ctx', axis=0)]
    unnamed x15 -> x2, waiting for transfers between devices: 220 us -> 0.03 us
    unnamed x2 -> x0, blocking collectives: 80.6 us -> none
    ppermute x44 -> x33, waiting for transfers between devices: 133 us -> 68.2 us  [the longest x12 38.3 us: to_chip(): return lax.ppermute(block, 'ctx', route)]
    dot_general x74 -> x9, matrix products: 68.3 us -> 11.6 us  [dot(): lax.dot_general(left, right, (dims, ((), ())), preferred_element_type=jnp...]
    pallas_call x0 -> x16, Pallas kernels: none -> 28.8 us  [the longest x5 23.6 us: one_step(): pl.pallas_call(functools.partial(copied_kernel, kernel, first, far, len(o...]
    ppermute x44 -> x33, starting transfers between devices: 6.69 us -> 30.7 us  [the longest x12 16.1 us: to_chip(): return lax.ppermute(block, 'ctx', route)]
  transfers between devices with their start and end apart: 56 -> 40, of which waited for: 41 -> 22; matrix products, arithmetic and copies ran while one was open for 8% -> 11% of each run, Pallas kernels for 0% -> 10%
where the time goes in v2:
time: 241 us; the launch traced here: 240 us
  waiting for transfers between devices  85.1 us (35%)
  starting transfers between devices  52.2 us (22%)
  local copies, waits for them, and re-layouts  29.4 us (12%)
  Pallas kernels  28.8 us (12%)
  other arithmetic  17.2 us (7%)
  between operations  15.7 us (7%)
  matrix products  11.6 us (5%)
    ppermute x12, waiting for transfers between devices, to_chip(): return lax.ppermute(block, 'ctx', route)  38.3 us
    ppermute x12, waiting for transfers between devices, to_team(): lax.ppermute(block, 'batch', [(i, (i + distance) % teams) for i in range(...  25.7 us
    pallas_call x5, Pallas kernels, one_step(): pl.pallas_call(functools.partial(copied_kernel, kernel, first, far, len(o...  23.6 us
    ppermute x12, starting transfers between devices, to_chip(): return lax.ppermute(block, 'ctx', route)  16.1 us
    all_to_all x2, waiting for transfers between devices, trade_chips(): return lax.all_to_all(blocks, 'ctx', 0, 0, axis_index_groups=same_core)  14.9 us
    ppermute x12, starting transfers between devices, to_team(): lax.ppermute(block, 'batch', [(i, (i + distance) % teams) for i in range(...  13.5 us
    dot_general x9, matrix products, dot(): lax.dot_general(left, right, (dims, ((), ())), preferred_element_type=jnp...  11.6 us
    all_to_all x3, starting transfers between devices, trade_teams(): return lax.all_to_all(blocks, 'batch', 0, 0)  11.4 us
  transfers between devices with their start and end apart: 40, of which 22 were waited for; matrix products, arithmetic and copies ran while one was open for 11% of the time, Pallas kernels for 10%

profile of v2, /device:TPU:0, one launch (start us, length us, event | category | flops | bytes accessed | tf_op | source)
XLA Modules:
  0.0 240.0 jit_solution(9129289363892222077)
XLA Ops:
  7.2 1.4 stack.99.vectors
  8.6 1.6 pack.1
  10.1 6.3 %all-to-all-start = ((bf16[4,32,768]{2,1,0:T(8,128)(2,1)}), bf16[4,32,768]{2,1,0:T(8,128)(2,1)S(1)}, u32[]{:S(2)}, u32[]{:S(2)}) async-start(bf16[4,32,768]{2,1,0:T(8,128)(2,1)} %pack.1), calls=%async_computation | async-start | bytes 393216 | tf_op jit(solution)/shard_map/all_to_all | solution.py:829
  16.5 1.6 lay.1.refs_0_
  18.1 5.9 %all-to-all-done.refs_1_.packed = bf16[4,32,768]{2,1,0:T(8,128)(2,1)S(1)} async-done(((bf16[4,32,768]{2,1,0:T(8,128)(2,1)}), bf16[4,32,768]{2,1,0:T(8,128)(2,1)S(1)}, u32[]{:S(2)}, u32[]{:S(2)}) %all-to-all-start) | async-done | bytes 196640 | tf_op jit(solution)/shard_map/all_to_all | solution.py:829
  24.9 1.4 collective-permute-start.2
  27.8 2.0 share.1
  29.8 4.2 %all-to-all-start.1 = ((bf16[4,152,768]{2,1,0:T(8,128)(2,1)}), bf16[4,152,768]{2,1,0:T(8,128)(2,1)}, u32[]{:S(2)}, u32[]{:S(2)}) async-start(bf16[4,152,768]{2,1,0:T(8,128)(2,1)} %share.1), calls=%async_computation.1 | async-start | bytes 1867776 | tf_op jit(solution)/shard_map/all_to_all | solution.py:832
  34.3 11.6 %collective-permute-done.1.refs_3_ = bf16[152,768]{1,0:T(8,128)(2,1)S(1)} collective-permute-done((bf16[152,768]{1,0:T(8,128)(2,1)S(1)}, bf16[152,768]{1,0:T(8,128)(2,1)S(1)}, u32[]{:S(2)}, u32[]{:S(2)}) %collective-permute-start.1) | collective-permute-done | bytes 233504 | tf_op jit(solution)/shard_map/ppermute | solution.py:802
  46.5 1.2 slice.158
  50.1 1.5 select_bitcast_fusion.1
  52.9 1.3 fusion.6
  54.2 9.4 %attend.1 = (bf16[512,768]{1,0:T(8,128)(2,1)}, bf16[512,192]{1,0:T(8,128)(2,1)}, bf16[1024,256]{1,0:T(8,128)(2,1)}, bf16[1024,192]{1,0:T(8,128)(2,1)}, f32[192,5...) custom-call(s32[9]{0:T(128)S(1)} %pad_add_fusion.refs_0_, ...), custom_call_target="tpu_custom_call" | custom-call | flops 2516582400 | bytes 2680356 | tf_op jit(solution)/shard_map/attend/pallas_call | solution.py:376
  63.6 2.5 %collective-permute-start.8 = (bf16[192,128]{1,0:T(8,128)(2,1)}, bf16[192,128]{1,0:T(8,128)(2,1)S(1)}, u32[]{:S(2)}, u32[]{:S(2)}) collective-permute-start(bf16[192,128]{1,0:T(8,128)(2,1)} %get-tuple-element.44), channel_id=1, source_target_pairs={{0,6},{1,7},{2,0},{3,1},{4,2},{5,3},{6,4},{7,5},{8,14},{9,15},{10,... | collective-permute-start | bytes 147464 | tf_op jit(solution)/shard_map/ppermute | solution.py:802
  68.0 3.5 %all-to-all-start.2 = ((bf16[4,4,24,768]{3,2,1,0:T(8,128)(2,1)}), bf16[4,4,24,768]{3,2,1,0:T(8,128)(2,1)S(1)}, u32[]{:S(2)}, u32[]{:S(2)}) async-start(bf16[4,4,24,768]{3,2,1,0:T(8,128)(2,1)} %broadcast_in_dim.10), calls=%async_computation.2 | async-start | bytes 1179648 | tf_op jit(solution)/shard_map/all_to_all | solution.py:832
  72.4 1.8 collective-permute-start.10
  74.2 7.0 %collective-permute-done.9 = bf16[192,128]{1,0:T(8,128)(2,1)S(1)} collective-permute-done((bf16[192,128]{1,0:T(8,128)(2,1)S(1)}, bf16[192,128]{1,0:T(8,128)(2,1)S(1)}, u32[]{:S(2)}, u32[]{:S(2)}) %collective-permute-start.9) | collective-permute-done | bytes 49184 | tf_op jit(solution)/shard_map/ppermute | solution.py:802
  81.5 1.8 collective-permute-done.11
  85.1 2.7 %collective-permute-start.14 = (bf16[128,768]{1,0:T(8,128)(2,1)S(1)}, bf16[128,768]{1,0:T(8,128)(2,1)S(1)}, u32[]{:S(2)}, u32[]{:S(2)}) collective-permute-start(bf16[128,768]{1,0:T(8,128)(2,1)S(1)} %fusion.19), channel_id=1, source_target_pairs={{0,24},{8,0},{16,8},{24,16},{1,25},{9,1},{17,9},{25,17},{2,26},{10... | collective-permute-start | bytes 589832 | tf_op jit(solution)/shard_map/ppermute | solution.py:808
  88.9 1.8 fusion.31
  90.8 2.3 collective-permute-done.14
  93.1 5.7 %collective-permute-done.13 = bf16[128,768]{1,0:T(8,128)(2,1)} collective-permute-done((bf16[128,768]{1,0:T(8,128)(2,1)S(1)}, bf16[128,768]{1,0:T(8,128)(2,1)}, u32[]{:S(2)}, u32[]{:S(2)}) %collective-permute-start.13) | collective-permute-done | bytes 196640 | tf_op jit(solution)/shard_map/ppermute | solution.py:808
  98.8 3.4 %fusion.3 = (f32[512,768]{1,0:T(8,128)}, bf16[512,768]{1,0:T(8,128)(2,1)S(1)}) fusion(f32[768]{0:T(1024)S(1)} %dynamic_slice.45, bf16[768,768]{1,0:T(8,128)(2,1)S(1)} %bitcast.156, bf16[128,768]{1,0:T(8,128)(2,1)S(1)} %collective-permute-done.14, bf16[128,768]{1,0:T(8,128)(2,1)} %collective-permute-done.13, bf16[128,768]{1,0:T(8,128)(2,1)} %collective-permute-done.12, ...), kind=kOutput, calls=%fused_computation.5 | convolution fusion | flops 611450880 | bytes 4328448 | tf_op jit(solution)/shard_map/dot_general | solution.py:317
  102.2 2.0 fusion.37
  105.5 1.5 collective-permute-start.17
  108.2 1.4 mul.177
  109.6 1.4 add.223
  111.0 1.3 collective-permute-done.15
  112.3 3.0 %collective-permute-done.17 = bf16[128,768]{1,0:T(8,128)(2,1)S(1)} collective-permute-done((bf16[128,768]{1,0:T(8,128)(2,1)}, bf16[128,768]{1,0:T(8,128)(2,1)S(1)}, u32[]{:S(2)}, u32[]{:S(2)}) %collective-permute-start.17) | collective-permute-done | bytes 196640 | tf_op jit(solution)/shard_map/ppermute | solution.py:808
  116.2 1.6 fusion.29
  119.5 1.2 collective-permute-start.20
  122.5 4.3 %collective-permute-done.20 = bf16[128,768]{1,0:T(8,128)(2,1)S(1)} collective-permute-done((bf16[128,768]{1,0:T(8,128)(2,1)S(1)}, bf16[128,768]{1,0:T(8,128)(2,1)S(1)}, u32[]{:S(2)}, u32[]{:S(2)}) %collective-permute-start.20) | collective-permute-done | bytes 196640 | tf_op jit(solution)/shard_map/ppermute | solution.py:808
  126.8 4.0 %collective-permute-done.19 = bf16[128,768]{1,0:T(8,128)(2,1)S(1)} collective-permute-done((bf16[128,768]{1,0:T(8,128)(2,1)S(1)}, bf16[128,768]{1,0:T(8,128)(2,1)S(1)}, u32[]{:S(2)}, u32[]{:S(2)}) %collective-permute-start.19) | collective-permute-done | bytes 196640 | tf_op jit(solution)/shard_map/ppermute | solution.py:808
  130.9 1.4 convert_reduce_fusion
  135.4 1.8 convolution_convert_fusion.1
  137.3 1.5 pad_maximum_fusion
  140.3 2.6 %collective-permute-start.21 = (bf16[128,768]{1,0:T(8,128)(2,1)S(1)}, bf16[128,768]{1,0:T(8,128)(2,1)}, u32[]{:S(2)}, u32[]{:S(2)}) collective-permute-start(bf16[128,768]{1,0:T(8,128)(2,1)S(1)} %get-tuple-element.95.refs_1_), channel_id=1, source_target_pairs={{0,24},{8,0},{16,8},{24,16},{1,25},{9,1},{17,9},{25,17},{2,26},{10... | collective-permute-start | bytes 589832 | tf_op jit(solution)/shard_map/ppermute | solution.py:808
  142.9 1.4 add.228
  144.3 2.2 collective-permute-done.23
  146.5 2.0 collective-permute-done.22
  148.5 2.3 multiply_reduce_fusion
  150.9 1.6 convert_reduce_fusion.3
  153.4 1.4 copy-done.16
  156.1 2.8 %collective-permute-start.26 = (bf16[192,128]{1,0:T(8,128)(2,1)S(1)}, bf16[192,128]{1,0:T(8,128)(2,1)S(1)}, u32[]{:S(2)}, u32[]{:S(2)}) collective-permute-start(bf16[192,128]{1,0:T(8,128)(2,1)S(1)} %get-tuple-element.102), channel_id=1, source_target_pairs={{0,6},{1,7},{2,0},{3,1},{4,2},{5,3},{6,4},{7,5},{8,14},{9,15},{10,... | collective-permute-start | bytes 147464 | tf_op jit(solution)/shard_map/ppermute | solution.py:802
  158.9 1.1 collective-permute-start.25
  160.0 1.6 fusion.5.refs_10_.refs_2_
  161.6 1.7 collective-permute-done.26.refs_9_
  163.3 4.7 %collective-permute-done.25.refs_8_ = bf16[192,128]{1,0:T(8,128)(2,1)S(1)} collective-permute-done((bf16[192,128]{1,0:T(8,128)(2,1)S(1)}, bf16[192,128]{1,0:T(8,128)(2,1)S(1)}, u32[]{:S(2)}, u32[]{:S(2)}) %collective-permute-start.25) | collective-permute-done | bytes 49184 | tf_op jit(solution)/shard_map/ppermute | solution.py:802
  168.9 6.8 %attend_back.1 = (bf16[512,192]{1,0:T(8,128)(2,1)}, f32[512,384]{1,0:T(8,128)}, bf16[512,384]{1,0:T(8,128)(2,1)}) custom-call(s32[9]{0:T(128)S(1)} %pad_add_fusion.refs_0_, bf16[512,192]{1,0:T(8,128)(2,1)S(1)} %copy-done.13, bf16[1024,256]{1,0:T(8,128)(2,1)S(1)} %copy-done.10, bf16[1024,192]{1,0:T(8,128)(2,1)S(1)} %copy-done.11, f32[192,512]{1,0:T(8,128)S(1)} %copy-done.12, ...), custom_call_target="tpu_custom_call" | custom-call | flops 4026531840 | bytes 2299940 | tf_op jit(solution)/shard_map/attend_back/pallas_call | solution.py:376
  177.8 1.1 copy-done.7
  179.8 4.4 %finish.1 = (bf16[128,768]{1,0:T(8,128)(2,1)}, bf16[128,768]{1,0:T(8,128)(2,1)}, bf16[128,768]{1,0:T(8,128)(2,1)}, bf16[128,768]{1,0:T(8,128)(2,1)}, f32[16,32,5...) custom-call(s32[2]{0:T(128)S(1)} %pad_add_fusion.1.refs_0_, bf16[512,768]{1,0:T(8,128)(2,1)S(1)} %copy-done.6, ...), custom_call_target="tpu_custom_call" | custom-call | flops 905969664 | bytes 3637256 | tf_op jit(solution)/shard_map/finish/pallas_call | solution.py:376
  185.4 1.3 collective-permute-done.32.refs_1_
  186.6 1.3 copy-done.1
  188.0 2.0 bundle.1
  190.0 3.7 %all-to-all-start.3 = ((bf16[4,248,768]{2,1,0:T(8,128)(2,1)}), bf16[4,248,768]{2,1,0:T(8,128)(2,1)S(1)}, u32[]{:S(2)}, u32[]{:S(2)}) async-start(bf16[4,248,768]{2,1,0:T(8,128)(2,1)} %bundle.1), calls=%async_computation.4 | async-start | bytes 3047424 | tf_op jit(solution)/shard_map/all_to_all | solution.py:832
  193.8 2.8 %collective-permute-start.30 = (bf16[128,768]{1,0:T(8,128)(2,1)S(1)}, bf16[128,768]{1,0:T(8,128)(2,1)S(1)}, u32[]{:S(2)}, u32[]{:S(2)}) collective-permute-start(bf16[128,768]{1,0:T(8,128)(2,1)S(1)} %copy-done.49), channel_id=1, source_target_pairs={{0,4},{1,5},{2,6},{3,7},{4,0},{5,1},{6,2},{7,3},{8,12},{9,13},{10,... | collective-permute-start | bytes 589832 | tf_op jit(solution)/shard_map/ppermute | solution.py:802
  196.6 1.1 collective-permute-start.31
  197.6 5.8 %collective-permute-done.29 = bf16[128,768]{1,0:T(8,128)(2,1)S(1)} collective-permute-done((bf16[128,768]{1,0:T(8,128)(2,1)S(1)}, bf16[128,768]{1,0:T(8,128)(2,1)S(1)}, u32[]{:S(2)}, u32[]{:S(2)}) %collective-permute-start.29) | collective-permute-done | bytes 196640 | tf_op jit(solution)/shard_map/ppermute | solution.py:802
  203.4 7.5 %collective-permute-done.30 = bf16[128,768]{1,0:T(8,128)(2,1)S(1)} collective-permute-done((bf16[128,768]{1,0:T(8,128)(2,1)S(1)}, bf16[128,768]{1,0:T(8,128)(2,1)S(1)}, u32[]{:S(2)}, u32[]{:S(2)}) %collective-permute-start.30) | collective-permute-done | bytes 196640 | tf_op jit(solution)/shard_map/ppermute | solution.py:802
  211.1 2.0 all-to-all-done.3.refs_1_
  214.1 3.6 %all-to-all-start.4 = ((bf16[4,56,768]{2,1,0:T(8,128)(2,1)}), bf16[4,56,768]{2,1,0:T(8,128)(2,1)S(1)}, u32[]{:S(2)}, u32[]{:S(2)}) async-start(bf16[4,56,768]{2,1,0:T(8,128)(2,1)} %after.14), calls=%async_computation.5 | async-start | bytes 688128 | tf_op jit(solution)/shard_map/all_to_all | solution.py:829
  219.2 9.0 %all-to-all-done.4.refs_0_ = bf16[4,56,768]{2,1,0:T(8,128)(2,1)S(1)} async-done(((bf16[4,56,768]{2,1,0:T(8,128)(2,1)}), bf16[4,56,768]{2,1,0:T(8,128)(2,1)S(1)}, u32[]{:S(2)}, u32[]{:S(2)}) %all-to-all-start.4) | async-done | bytes 344096 | tf_op jit(solution)/shard_map/all_to_all | solution.py:829
  229.1 1.2 slice_bitcast_fusion.6
  230.3 1.4 slice_bitcast_fusion.3
  (250 shorter events, 35.5 us)
Async XLA Ops:
  10.1 13.8 %all-to-all-start = ((bf16[4,32,768]{2,1,0:T(8,128)(2,1)}), bf16[4,32,768]{2,1,0:T(8,128)(2,1)S(1)}, u32[]{:S(2)}, u32[]{:S(2)}) async-start(bf16[4,32,768]{2,1,0:T(8,128)(2,1)} %pack.1), calls=%async_computation | async-start | bytes 393216 | tf_op jit(solution)/shard_map/all_to_all | solution.py:829
  16.5 37.7 %collective-permute-start.3 = (bf16[128,768]{1,0:T(8,128)(2,1)}, bf16[128,768]{1,0:T(8,128)(2,1)S(1)}, u32[]{:S(2)}, u32[]{:S(2)}) collective-permute-start(bf16[128,768]{1,0:T(8,128)(2,1)} %refs_1_.1), channel_id=1, source_target_pairs={{0,1},{1,0},{2,3},{3,2},{4,5},{5,4},{6,7},{7,6},{8,9},{9,8},{10,11... | collective-permute-start | bytes 589832 | tf_op jit(solution)/shard_map/ppermute | solution.py:805
  24.9 9.2 %collective-permute-start.2 = (bf16[152,768]{1,0:T(8,128)(2,1)S(1)}, bf16[152,768]{1,0:T(8,128)(2,1)S(1)}, u32[]{:S(2)}, u32[]{:S(2)}) collective-permute-start(bf16[152,768]{1,0:T(8,128)(2,1)S(1)} %after.8), channel_id=1, source_target_pairs={{0,6},{1,7},{2,0},{3,1},{4,2},{5,3},{6,4},{7,5},{8,14},{9,15},{10,... | collective-permute-start | bytes 700424 | tf_op jit(solution)/shard_map/ppermute | solution.py:802
  27.1 18.8 %collective-permute-start.1 = (bf16[152,768]{1,0:T(8,128)(2,1)S(1)}, bf16[152,768]{1,0:T(8,128)(2,1)S(1)}, u32[]{:S(2)}, u32[]{:S(2)}) collective-permute-start(bf16[152,768]{1,0:T(8,128)(2,1)S(1)} %after.8), channel_id=1, source_target_pairs={{0,4},{1,5},{2,6},{3,7},{4,0},{5,1},{6,2},{7,3},{8,12},{9,13},{10,... | collective-permute-start | bytes 700424 | tf_op jit(solution)/shard_map/ppermute | solution.py:802
  27.6 18.3 %collective-permute-start = (bf16[152,768]{1,0:T(8,128)(2,1)S(1)}, bf16[152,768]{1,0:T(8,128)(2,1)S(1)}, u32[]{:S(2)}, u32[]{:S(2)}) collective-permute-start(bf16[152,768]{1,0:T(8,128)(2,1)S(1)} %after.8), channel_id=1, source_target_pairs={{0,2},{1,3},{2,4},{3,5},{4,6},{5,7},{6,0},{7,1},{8,10},{9,11},{10,... | collective-permute-start | bytes 700424 | tf_op jit(solution)/shard_map/ppermute | solution.py:802
  27.8 18.6 %copy-start.31 = (bf16[24,768]{1,0:T(8,128)(2,1)S(1)}, bf16[24,768]{1,0:T(8,128)(2,1)}, u32[]{:S(2)}) copy-start(bf16[24,768]{1,0:T(8,128)(2,1)} %w_out.1) | copy-start | bytes 110596
  29.8 16.6 %all-to-all-start.1 = ((bf16[4,152,768]{2,1,0:T(8,128)(2,1)}), bf16[4,152,768]{2,1,0:T(8,128)(2,1)}, u32[]{:S(2)}, u32[]{:S(2)}) async-start(bf16[4,152,768]{2,1,0:T(8,128)(2,1)} %share.1), calls=%async_computation.1 | async-start | bytes 1867776 | tf_op jit(solution)/shard_map/all_to_all | solution.py:832
  34.1 14.8 %copy-start.32 = (bf16[96,768]{1,0:T(8,128)(2,1)S(1)}, bf16[96,768]{1,0:T(8,128)(2,1)}, u32[]{:S(2)}) copy-start(bf16[96,768]{1,0:T(8,128)(2,1)} %param.31) | copy-start | bytes 442372
  34.1 54.8 %all-gather.3.cloned.1.call-start = ((), (), s32[]{:S(2)}) async-start(), calls=%async_computation.7 | async-start | bytes 2654208 | tf_op jit(solution)/shard_map/all_gather | solution.py:899
  34.2 20.0 %collective-permute-start.6 = (bf16[152,768]{1,0:T(8,128)(2,1)S(1)}, bf16[152,768]{1,0:T(8,128)(2,1)S(1)}, u32[]{:S(2)}, u32[]{:S(2)}) collective-permute-start(bf16[152,768]{1,0:T(8,128)(2,1)S(1)} %collective-permute-done.2.refs_4_), channel_id=1, source_target_pairs={{0,1},{1,0},{2,3},{3,2},{4,5},{5,4},{6,7},{7,6},{8,9},{9,8},{10,11... | collective-permute-start | bytes 700424 | tf_op jit(solution)/shard_map/ppermute | solution.py:805
  45.9 8.3 %collective-permute-start.5 = (bf16[152,768]{1,0:T(8,128)(2,1)S(1)}, bf16[152,768]{1,0:T(8,128)(2,1)S(1)}, u32[]{:S(2)}, u32[]{:S(2)}) collective-permute-start(bf16[152,768]{1,0:T(8,128)(2,1)S(1)} %collective-permute-done.1.refs_3_), channel_id=1, source_target_pairs={{0,1},{1,0},{2,3},{3,2},{4,5},{5,4},{6,7},{7,6},{8,9},{9,8},{10,11... | collective-permute-start | bytes 700424 | tf_op jit(solution)/shard_map/ppermute | solution.py:805
  45.9 8.3 %collective-permute-start.4 = (bf16[152,768]{1,0:T(8,128)(2,1)S(1)}, bf16[152,768]{1,0:T(8,128)(2,1)S(1)}, u32[]{:S(2)}, u32[]{:S(2)}) collective-permute-start(bf16[152,768]{1,0:T(8,128)(2,1)S(1)} %collective-permute-done.refs_2_), channel_id=1, source_target_pairs={{0,1},{1,0},{2,3},{3,2},{4,5},{5,4},{6,7},{7,6},{8,9},{9,8},{10,11... | collective-permute-start | bytes 700424 | tf_op jit(solution)/shard_map/ppermute | solution.py:805
  47.7 2.5 %collective-permute-start.7 = (bf16[4,4,32,768]{3,2,1,0:T(8,128)(2,1)S(1)}, bf16[4,4,32,768]{3,2,1,0:T(8,128)(2,1)}, u32[]{:S(2)}, u32[]{:S(2)}) collective-permute-start(bf16[4,4,32,768]{3,2,1,0:T(8,128)(2,1)S(1)} %bitcast.151), channel_id=1, source_target_pairs={{0,1},{1,0},{2,3},{3,2},{4,5},{5,4},{6,7},{7,6},{8,9},{9,8},{10,11... | collective-permute-start | bytes 2359304 | tf_op jit(solution)/shard_map/ppermute | solution.py:805
  63.6 10.6 %collective-permute-start.8 = (bf16[192,128]{1,0:T(8,128)(2,1)}, bf16[192,128]{1,0:T(8,128)(2,1)S(1)}, u32[]{:S(2)}, u32[]{:S(2)}) collective-permute-start(bf16[192,128]{1,0:T(8,128)(2,1)} %get-tuple-element.44), channel_id=1, source_target_pairs={{0,6},{1,7},{2,0},{3,1},{4,2},{5,3},{6,4},{7,5},{8,14},{9,15},{10,... | collective-permute-start | bytes 147464 | tf_op jit(solution)/shard_map/ppermute | solution.py:802
  66.8 14.5 %copy-start.34 = (bf16[192,128]{1,0:T(8,128)(2,1)S(1)}, bf16[192,128]{1,0:T(8,128)(2,1)}, u32[]{:S(2)}) copy-start(bf16[192,128]{1,0:T(8,128)(2,1)} %get-tuple-element.47) | copy-start | bytes 147460
  66.8 14.5 %copy-start.9 = (f32[3,512]{1,0:T(4,128)S(1)}, f32[3,512]{1,0:T(4,128)}, u32[]{:S(2)}) copy-start(f32[3,512]{1,0:T(4,128)} %get-tuple-element.48.refs_1_.refs_5_) | copy-start | bytes 18436
  67.0 17.8 %copy-start.35 = (f32[768]{0:T(1024)}, f32[768]{0:T(1024)S(1)}, u32[]{:S(2)}) copy-start(f32[768]{0:T(1024)S(1)} %add.211) | copy-start | bytes 9220
  68.0 13.2 %all-to-all-start.2 = ((bf16[4,4,24,768]{3,2,1,0:T(8,128)(2,1)}), bf16[4,4,24,768]{3,2,1,0:T(8,128)(2,1)S(1)}, u32[]{:S(2)}, u32[]{:S(2)}) async-start(bf16[4,4,24,768]{3,2,1,0:T(8,128)(2,1)} %broadcast_in_dim.10), calls=%async_computation.2 | async-start | bytes 1179648 | tf_op jit(solution)/shard_map/all_to_all | solution.py:832
  71.5 113.0 %reduce-scatter.2.cloned.1.call-start = ((), (), s32[]{:S(2)}) async-start(), calls=%async_computation.6 | async-start | bytes 2654208 | tf_op jit(solution)/shard_map/reduce_scatter | solution.py:971
  71.6 9.6 %collective-permute-start.9 = (bf16[192,128]{1,0:T(8,128)(2,1)S(1)}, bf16[192,128]{1,0:T(8,128)(2,1)S(1)}, u32[]{:S(2)}, u32[]{:S(2)}) collective-permute-start(bf16[192,128]{1,0:T(8,128)(2,1)S(1)} %copy-done.52), channel_id=1, source_target_pairs={{0,4},{1,5},{2,6},{3,7},{4,0},{5,1},{6,2},{7,3},{8,12},{9,13},{10,... | collective-permute-start | bytes 147464 | tf_op jit(solution)/shard_map/ppermute | solution.py:802
  72.4 8.8 %collective-permute-start.10 = (bf16[192,128]{1,0:T(8,128)(2,1)S(1)}, bf16[192,128]{1,0:T(8,128)(2,1)S(1)}, u32[]{:S(2)}, u32[]{:S(2)}) collective-permute-start(bf16[192,128]{1,0:T(8,128)(2,1)S(1)} %copy-done.51), channel_id=1, source_target_pairs={{0,2},{1,3},{2,4},{3,5},{4,6},{5,7},{6,0},{7,1},{8,10},{9,11},{10,... | collective-permute-start | bytes 147464 | tf_op jit(solution)/shard_map/ppermute | solution.py:802
  81.3 2.1 collective-permute-start.11
  85.0 13.7 %copy-start.28 = (bf16[128,768]{1,0:T(8,128)(2,1)}, bf16[128,768]{1,0:T(8,128)(2,1)S(1)}, u32[]{:S(2)}) copy-start(bf16[128,768]{1,0:T(8,128)(2,1)S(1)} %fusion.19) | copy-start | bytes 589828
  85.1 8.1 %collective-permute-start.14 = (bf16[128,768]{1,0:T(8,128)(2,1)S(1)}, bf16[128,768]{1,0:T(8,128)(2,1)S(1)}, u32[]{:S(2)}, u32[]{:S(2)}) collective-permute-start(bf16[128,768]{1,0:T(8,128)(2,1)S(1)} %fusion.19), channel_id=1, source_target_pairs={{0,24},{8,0},{16,8},{24,16},{1,25},{9,1},{17,9},{25,17},{2,26},{10... | collective-permute-start | bytes 589832 | tf_op jit(solution)/shard_map/ppermute | solution.py:808
  87.8 11.0 %collective-permute-start.13 = (bf16[128,768]{1,0:T(8,128)(2,1)S(1)}, bf16[128,768]{1,0:T(8,128)(2,1)}, u32[]{:S(2)}, u32[]{:S(2)}) collective-permute-start(bf16[128,768]{1,0:T(8,128)(2,1)S(1)} %fusion.19), channel_id=1, source_target_pairs={{0,16},{8,24},{16,0},{24,8},{1,17},{9,25},{17,1},{25,9},{2,18},{10... | collective-permute-start | bytes 589832 | tf_op jit(solution)/shard_map/ppermute | solution.py:808
  88.4 10.4 %collective-permute-start.12 = (bf16[128,768]{1,0:T(8,128)(2,1)S(1)}, bf16[128,768]{1,0:T(8,128)(2,1)}, u32[]{:S(2)}, u32[]{:S(2)}) collective-permute-start(bf16[128,768]{1,0:T(8,128)(2,1)S(1)} %fusion.19), channel_id=1, source_target_pairs={{0,8},{8,16},{16,24},{24,0},{1,9},{9,17},{17,25},{25,1},{2,10},{10... | collective-permute-start | bytes 589832 | tf_op jit(solution)/shard_map/ppermute | solution.py:808
  90.8 11.4 %copy-start.22 = (bf16[4,8,24,768]{3,2,1,0:T(8,128)(2,1)}, bf16[4,8,24,768]{3,2,1,0:T(8,128)(2,1)S(1)}, u32[]{:S(2)}) copy-start(bf16[4,8,24,768]{3,2,1,0:T(8,128)(2,1)S(1)} %copy.56) | copy-start | bytes 3538948
  93.1 9.1 %copy-start.46 = (bf16[128,768]{1,0:T(8,128)(2,1)}, bf16[128,768]{1,0:T(8,128)(2,1)S(1)}, u32[]{:S(2)}) copy-start(bf16[128,768]{1,0:T(8,128)(2,1)S(1)} %collective-permute-done.14) | copy-start | bytes 589828
  104.2 13.8 %copy-start.20 = (bf16[128,768]{1,0:T(8,128)(2,1)S(1)}, bf16[128,768]{1,0:T(8,128)(2,1)}, u32[]{:S(2)}) copy-start(bf16[128,768]{1,0:T(8,128)(2,1)} %param.35) | copy-start | bytes 589828
  105.0 7.3 %collective-permute-start.15 = (bf16[128,768]{1,0:T(8,128)(2,1)}, bf16[128,768]{1,0:T(8,128)(2,1)S(1)}, u32[]{:S(2)}, u32[]{:S(2)}) collective-permute-start(bf16[128,768]{1,0:T(8,128)(2,1)} %get-tuple-element.98), channel_id=1, source_target_pairs={{0,24},{8,0},{16,8},{24,16},{1,25},{9,1},{17,9},{25,17},{2,26},{10... | collective-permute-start | bytes 589832 | tf_op jit(solution)/shard_map/ppermute | solution.py:808
  105.5 9.8 %collective-permute-start.17 = (bf16[128,768]{1,0:T(8,128)(2,1)}, bf16[128,768]{1,0:T(8,128)(2,1)S(1)}, u32[]{:S(2)}, u32[]{:S(2)}) collective-permute-start(bf16[128,768]{1,0:T(8,128)(2,1)} %get-tuple-element.99), channel_id=1, source_target_pairs={{0,8},{8,16},{16,24},{24,0},{1,9},{9,17},{17,25},{25,1},{2,10},{10... | collective-permute-start | bytes 589832 | tf_op jit(solution)/shard_map/ppermute | solution.py:808
  107.0 9.2 %collective-permute-start.16 = (bf16[128,768]{1,0:T(8,128)(2,1)S(1)}, bf16[128,768]{1,0:T(8,128)(2,1)}, u32[]{:S(2)}, u32[]{:S(2)}) collective-permute-start(bf16[128,768]{1,0:T(8,128)(2,1)S(1)} %get-tuple-element.100), channel_id=1, source_target_pairs={{0,16},{8,24},{16,0},{24,8},{1,17},{9,25},{17,1},{25,9},{2,18},{10... | collective-permute-start | bytes 589832 | tf_op jit(solution)/shard_map/ppermute | solution.py:808
  116.2 14.7 %copy-start.53 = (f32[512,768]{1,0:T(8,128)S(1)}, f32[512,768]{1,0:T(8,128)}, u32[]{:S(2)}) copy-start(f32[512,768]{1,0:T(8,128)} %get-tuple-element.50) | copy-start | bytes 4718596
  117.7 14.6 %copy-start.41 = (f32[128]{0:T(128)}, f32[128]{0:T(128)S(1)}, u32[]{:S(2)}) copy-start(f32[128]{0:T(128)S(1)} %broadcast_multiply_fusion.4) | copy-start | bytes 1540
  118.0 14.4 %copy-start.42 = (f32[128]{0:T(128)}, f32[128]{0:T(128)S(1)}, u32[]{:S(2)}) copy-start(f32[128]{0:T(128)S(1)} %add_rsqrt_fusion) | copy-start | bytes 1540
  118.8 13.6 %copy-start.44 = (f32[128]{0:T(128)}, f32[128]{0:T(128)S(1)}, u32[]{:S(2)}) copy-start(f32[128]{0:T(128)S(1)} %broadcast_multiply_fusion.2) | copy-start | bytes 1540
  118.8 13.6 %copy-start.45 = (f32[128]{0:T(128)}, f32[128]{0:T(128)S(1)}, u32[]{:S(2)}) copy-start(f32[128]{0:T(128)S(1)} %broadcast_multiply_fusion.3) | copy-start | bytes 1540
  119.5 12.8 %copy-start.23 = (bf16[4,8,24,768]{3,2,1,0:T(8,128)(2,1)S(1)}, bf16[4,8,24,768]{3,2,1,0:T(8,128)(2,1)}, u32[]{:S(2)}) copy-start(bf16[4,8,24,768]{3,2,1,0:T(8,128)(2,1)} %copy-done.22) | copy-start | bytes 3538948
  119.5 7.3 %collective-permute-start.20 = (bf16[128,768]{1,0:T(8,128)(2,1)S(1)}, bf16[128,768]{1,0:T(8,128)(2,1)S(1)}, u32[]{:S(2)}, u32[]{:S(2)}) collective-permute-start(bf16[128,768]{1,0:T(8,128)(2,1)S(1)} %get-tuple-element.80), channel_id=1, source_target_pairs={{0,24},{8,0},{16,8},{24,16},{1,25},{9,1},{17,9},{25,17},{2,26},{10... | collective-permute-start | bytes 589832 | tf_op jit(solution)/shard_map/ppermute | solution.py:808
  120.8 10.1 %collective-permute-start.19 = (bf16[128,768]{1,0:T(8,128)(2,1)S(1)}, bf16[128,768]{1,0:T(8,128)(2,1)S(1)}, u32[]{:S(2)}, u32[]{:S(2)}) collective-permute-start(bf16[128,768]{1,0:T(8,128)(2,1)S(1)} %get-tuple-element.80), channel_id=1, source_target_pairs={{0,16},{8,24},{16,0},{24,8},{1,17},{9,25},{17,1},{25,9},{2,18},{10... | collective-permute-start | bytes 589832 | tf_op jit(solution)/shard_map/ppermute | solution.py:808
  121.7 9.2 %collective-permute-start.18 = (bf16[128,768]{1,0:T(8,128)(2,1)S(1)}, bf16[128,768]{1,0:T(8,128)(2,1)S(1)}, u32[]{:S(2)}, u32[]{:S(2)}) collective-permute-start(bf16[128,768]{1,0:T(8,128)(2,1)S(1)} %get-tuple-element.80), channel_id=1, source_target_pairs={{0,8},{8,16},{16,24},{24,0},{1,9},{9,17},{17,25},{25,1},{2,10},{10... | collective-permute-start | bytes 589832 | tf_op jit(solution)/shard_map/ppermute | solution.py:808
  138.9 7.7 %collective-permute-start.23 = (bf16[128,768]{1,0:T(8,128)(2,1)S(1)}, bf16[128,768]{1,0:T(8,128)(2,1)}, u32[]{:S(2)}, u32[]{:S(2)}) collective-permute-start(bf16[128,768]{1,0:T(8,128)(2,1)S(1)} %get-tuple-element.96), channel_id=1, source_target_pairs={{0,8},{8,16},{16,24},{24,0},{1,9},{9,17},{17,25},{25,1},{2,10},{10... | collective-permute-start | bytes 589832 | tf_op jit(solution)/shard_map/ppermute | solution.py:808
  139.3 9.2 %collective-permute-start.22 = (bf16[128,768]{1,0:T(8,128)(2,1)S(1)}, bf16[128,768]{1,0:T(8,128)(2,1)}, u32[]{:S(2)}, u32[]{:S(2)}) collective-permute-start(bf16[128,768]{1,0:T(8,128)(2,1)S(1)} %get-tuple-element.97), channel_id=1, source_target_pairs={{0,16},{8,24},{16,0},{24,8},{1,17},{9,25},{17,1},{25,9},{2,18},{10... | collective-permute-start | bytes 589832 | tf_op jit(solution)/shard_map/ppermute | solution.py:808
  140.3 8.2 %collective-permute-start.21 = (bf16[128,768]{1,0:T(8,128)(2,1)S(1)}, bf16[128,768]{1,0:T(8,128)(2,1)}, u32[]{:S(2)}, u32[]{:S(2)}) collective-permute-start(bf16[128,768]{1,0:T(8,128)(2,1)S(1)} %get-tuple-element.95.refs_1_), channel_id=1, source_target_pairs={{0,24},{8,0},{16,8},{24,16},{1,25},{9,1},{17,9},{25,17},{2,26},{10... | collective-permute-start | bytes 589832 | tf_op jit(solution)/shard_map/ppermute | solution.py:808
  144.3 8.1 %copy-start.15 = (bf16[4,4,2,24,768]{4,3,2,1,0:T(8,128)(2,1)S(1)}, bf16[4,4,2,24,768]{4,3,2,1,0:T(8,128)(2,1)}, u32[]{:S(2)}) copy-start(bf16[4,4,2,24,768]{4,3,2,1,0:T(8,128)(2,1)} %copy-done.14) | copy-start | bytes 3538948
  154.8 13.1 %copy-start.10 = (bf16[1024,256]{1,0:T(8,128)(2,1)S(1)}, bf16[1024,256]{1,0:T(8,128)(2,1)}, u32[]{:S(2)}) copy-start(bf16[1024,256]{1,0:T(8,128)(2,1)} %get-tuple-element.53.refs_2_) | copy-start | bytes 1572868
  154.8 13.1 %copy-start.11 = (bf16[1024,192]{1,0:T(8,128)(2,1)S(1)}, bf16[1024,192]{1,0:T(8,128)(2,1)}, u32[]{:S(2)}) copy-start(bf16[1024,192]{1,0:T(8,128)(2,1)} %get-tuple-element.54.refs_3_) | copy-start | bytes 1179652
  154.9 13.1 %copy-start.12 = (f32[192,512]{1,0:T(8,128)S(1)}, f32[192,512]{1,0:T(8,128)}, u32[]{:S(2)}) copy-start(f32[192,512]{1,0:T(8,128)} %get-tuple-element.55.refs_4_) | copy-start | bytes 1179652
  154.9 5.1 %collective-permute-start.27 = (bf16[4,4,24,768]{3,2,1,0:T(8,128)(2,1)S(1)}, bf16[4,4,24,768]{3,2,1,0:T(8,128)(2,1)}, u32[]{:S(2)}, u32[]{:S(2)}) collective-permute-start(bf16[4,4,24,768]{3,2,1,0:T(8,128)(2,1)S(1)} %fusion.7), channel_id=1, source_target_pairs={{0,1},{1,0},{2,3},{3,2},{4,5},{5,4},{6,7},{7,6},{8,9},{9,8},{10,11... | collective-permute-start | bytes 1769480 | tf_op jit(solution)/shard_map/ppermute | solution.py:805
  155.0 12.9 %collective-permute-start.24 = (bf16[192,128]{1,0:T(8,128)(2,1)S(1)}, bf16[192,128]{1,0:T(8,128)(2,1)S(1)}, u32[]{:S(2)}, u32[]{:S(2)}) collective-permute-start(bf16[192,128]{1,0:T(8,128)(2,1)S(1)} %get-tuple-element.104.refs_1_), channel_id=1, source_target_pairs={{0,2},{1,3},{2,4},{3,5},{4,6},{5,7},{6,0},{7,1},{8,10},{9,11},{10,... | collective-permute-start | bytes 147464 | tf_op jit(solution)/shard_map/ppermute | solution.py:802
  156.1 7.2 %collective-permute-start.26 = (bf16[192,128]{1,0:T(8,128)(2,1)S(1)}, bf16[192,128]{1,0:T(8,128)(2,1)S(1)}, u32[]{:S(2)}, u32[]{:S(2)}) collective-permute-start(bf16[192,128]{1,0:T(8,128)(2,1)S(1)} %get-tuple-element.102), channel_id=1, source_target_pairs={{0,6},{1,7},{2,0},{3,1},{4,2},{5,3},{6,4},{7,5},{8,14},{9,15},{10,... | collective-permute-start | bytes 147464 | tf_op jit(solution)/shard_map/ppermute | solution.py:802
  158.9 9.1 %collective-permute-start.25 = (bf16[192,128]{1,0:T(8,128)(2,1)S(1)}, bf16[192,128]{1,0:T(8,128)(2,1)S(1)}, u32[]{:S(2)}, u32[]{:S(2)}) collective-permute-start(bf16[192,128]{1,0:T(8,128)(2,1)S(1)} %get-tuple-element.103), channel_id=1, source_target_pairs={{0,4},{1,5},{2,6},{3,7},{4,0},{5,1},{6,2},{7,3},{8,12},{9,13},{10,... | collective-permute-start | bytes 147464 | tf_op jit(solution)/shard_map/ppermute | solution.py:802
  168.9 7.1 %copy-start.36 = (f32[768]{0:T(1024)S(1)}, f32[768]{0:T(1024)}, u32[]{:S(2)}) copy-start(f32[768]{0:T(1024)} %get-tuple-element.78) | copy-start | bytes 9220
  168.9 7.2 %copy-start.38 = (f32[768]{0:T(1024)S(1)}, f32[768]{0:T(1024)}, u32[]{:S(2)}) copy-start(f32[768]{0:T(1024)} %get-tuple-element.79) | copy-start | bytes 9220
  168.9 7.3 %copy-start.43 = (f32[768]{0:T(1024)S(1)}, f32[768]{0:T(1024)}, u32[]{:S(2)}) copy-start(f32[768]{0:T(1024)} %get-tuple-element.126) | copy-start | bytes 9220
  175.7 2.0 collective-permute-start.28
  184.3 2.4 collective-permute-start.32
  190.0 21.0 %copy-start.21 = (f32[128,768]{1,0:T(8,128)S(1)}, f32[128,768]{1,0:T(8,128)}, u32[]{:S(2)}) copy-start(f32[128,768]{1,0:T(8,128)} %get-tuple-element.83) | copy-start | bytes 1179652
  190.0 21.0 %copy-start.30 = (bf16[128,768]{1,0:T(8,128)(2,1)S(1)}, bf16[128,768]{1,0:T(8,128)(2,1)}, u32[]{:S(2)}) copy-start(bf16[128,768]{1,0:T(8,128)(2,1)} %get-tuple-element.59) | copy-start | bytes 589828
  190.0 23.1 %all-to-all-start.3 = ((bf16[4,248,768]{2,1,0:T(8,128)(2,1)}), bf16[4,248,768]{2,1,0:T(8,128)(2,1)S(1)}, u32[]{:S(2)}, u32[]{:S(2)}) async-start(bf16[4,248,768]{2,1,0:T(8,128)(2,1)} %bundle.1), calls=%async_computation.4 | async-start | bytes 3047424 | tf_op jit(solution)/shard_map/all_to_all | solution.py:832
  193.7 9.7 %collective-permute-start.29 = (bf16[128,768]{1,0:T(8,128)(2,1)S(1)}, bf16[128,768]{1,0:T(8,128)(2,1)S(1)}, u32[]{:S(2)}, u32[]{:S(2)}) collective-permute-start(bf16[128,768]{1,0:T(8,128)(2,1)S(1)} %copy-done.50), channel_id=1, source_target_pairs={{0,2},{1,3},{2,4},{3,5},{4,6},{5,7},{6,0},{7,1},{8,10},{9,11},{10,... | collective-permute-start | bytes 589832 | tf_op jit(solution)/shard_map/ppermute | solution.py:802
  193.8 17.2 %collective-permute-start.30 = (bf16[128,768]{1,0:T(8,128)(2,1)S(1)}, bf16[128,768]{1,0:T(8,128)(2,1)S(1)}, u32[]{:S(2)}, u32[]{:S(2)}) collective-permute-start(bf16[128,768]{1,0:T(8,128)(2,1)S(1)} %copy-done.49), channel_id=1, source_target_pairs={{0,4},{1,5},{2,6},{3,7},{4,0},{5,1},{6,2},{7,3},{8,12},{9,13},{10,... | collective-permute-start | bytes 589832 | tf_op jit(solution)/shard_map/ppermute | solution.py:802
  196.6 14.4 %collective-permute-start.31 = (bf16[128,768]{1,0:T(8,128)(2,1)S(1)}, bf16[128,768]{1,0:T(8,128)(2,1)S(1)}, u32[]{:S(2)}, u32[]{:S(2)}) collective-permute-start(bf16[128,768]{1,0:T(8,128)(2,1)S(1)} %copy-done.48), channel_id=1, source_target_pairs={{0,6},{1,7},{2,0},{3,1},{4,2},{5,3},{6,4},{7,5},{8,14},{9,15},{10,... | collective-permute-start | bytes 589832 | tf_op jit(solution)/shard_map/ppermute | solution.py:802
  214.1 14.1 %all-to-all-start.4 = ((bf16[4,56,768]{2,1,0:T(8,128)(2,1)}), bf16[4,56,768]{2,1,0:T(8,128)(2,1)S(1)}, u32[]{:S(2)}, u32[]{:S(2)}) async-start(bf16[4,56,768]{2,1,0:T(8,128)(2,1)} %after.14), calls=%async_computation.5 | async-start | bytes 688128 | tf_op jit(solution)/shard_map/all_to_all | solution.py:829
  (30 other events, 87.5 us)
Sparse Core Ops, SparseCore 0:
  49.8 36.6 all-gather.2
  139.0 37.6 reduce-scatter.1

commit v3 on v2

--- a/solution.py
+++ b/solution.py
@@ -549,20 +549,18 @@
 
 
 def finish_kernel(
-    chips, places, mine, weight, query_grad, kept, come, short, *refs, leave
+    places, mine, weight, query_grad, kept, come, short, marker, *refs, leave
 ):
     low, f32 = jnp.bfloat16, jnp.float32
-    sent, (own_terms, away_terms, terms, blocks) = refs[:chips], refs[chips:]
+    token_part, own_terms, away_terms, terms = refs
     owners, _, part, width = terms.shape
     pair = (kept[...] + come[...].astype(f32)).astype(low)
     grads = jnp.concatenate([query_grad[...].astype(f32), pair.astype(f32)], 1)
     sums = jnp.sum(grads, 0, keepdims=True)
     grads = grads.astype(low)
     part_grad = dot(grads, weight[...], ((1,), (1,))).astype(low)
-    blocks[...] = part_grad.reshape(blocks.shape)
-    for distance in range(chips):
-        sent[distance][...] = blocks[lax.rem(places[0] + distance, chips)]
-        leave(distance)
+    token_part[...] = part_grad.reshape(token_part.shape)
+    leave(0)
     terms[...] = dot(mine[...], grads, ((0,), (0,))).reshape(terms.shape)
     core = places[1]
     count = short.shape[2]
@@ -572,62 +570,58 @@
         for owner in range(owners):
             block = [terms[owner, which], short[owner, which] + below]
             ref[owner] = jnp.concatenate(block, 0).astype(ref.dtype)
-        leave(chips + index)
-
-
-def finish(chips, places, mine, weight, query_grad, kept, come, short):
+        leave(1 + index)
+
+
+def finish(chips, places, mine, weight, query_grad, kept, come, short, marker):
     count, depth = mine.shape
     width = weight.shape[1]
     owners = short.shape[0]
     part = depth // (2 * owners)
     held = part + short.shape[2]
-    block = (count // chips, depth)
     return one_step(
-        functools.partial(finish_kernel, chips),
-        [places, mine, weight, query_grad, kept, come, short],
+        finish_kernel,
+        [places, mine, weight, query_grad, kept, come, short, marker],
         [
-            *[(block, jnp.bfloat16)] * chips,
+            ((chips, count // chips, depth), jnp.bfloat16),
             ((owners, held, width), jnp.float32),
             ((owners, held, width), jnp.bfloat16),
         ],
         flops=4 * count * depth * width,
         name="finish",
-        scratch=[
-            pltpu.VMEM((owners, 2, part, width), jnp.float32),
-            pltpu.VMEM((chips, *block), jnp.bfloat16),
-        ],
-    )
-
-
-def bundle_kernel(own, come, w_out, w_up, out, leave):
+        far=(7,),
+        scratch=[pltpu.VMEM((owners, 2, part, width), jnp.float32)],
+    )
+
+
+def bundle_kernel(places, own, come, w_up, *outs, leave):
     f32 = jnp.float32
-    teams, chips, part, width = w_out.shape
+    teams, part, width = w_up.shape
     owners, held, group = own.shape
-    for team in range(teams):
+    chips = owners // teams
+    for distance, out in enumerate(outs):
+        team = lax.rem(places[0] + distance, teams)
         for chip in range(chips):
             owner = team * chips + chip
             block = own[owner] + come[owner].astype(f32)
             block = jnp.pad(block, ((0, 0), (0, width - group)))
-            start = chip * (held + part)
-            both = jnp.concatenate([block, w_out[team, chip].astype(f32)], 0)
-            out[team, start : start + held + part] = both.astype(out.dtype)
-        out[team, chips * (held + part) :] = w_up[team]
-    leave(0)
-
-
-def bundle(own, come, w_out, w_up):
-    teams, chips, part, width = w_out.shape
-    held = own.shape[1]
-    shape = (teams, chips * (held + part) + part, width)
+            out[chip * held : (chip + 1) * held] = block.astype(out.dtype)
+        out[chips * held :] = w_up[team]
+        leave(distance)
+
+
+def bundle(places, own, come, w_up):
+    teams, part, width = w_up.shape
+    owners, held, _ = own.shape
+    shape = (owners // teams * held + part, width)
     return one_step(
         bundle_kernel,
-        [own, come, w_out, w_up],
-        [(shape, jnp.bfloat16)],
+        [places, own, come, w_up],
+        [(shape, jnp.bfloat16)] * teams,
         flops=0,
         limit=8,
         name="bundle",
-        first=0,
-    )[0]
+    )
 
 
 def unpack_kernel(part, group, found, *outs, leave):
@@ -665,13 +659,17 @@
     pass
 
 
-def after(block, *others):
+def after(block, *others, pinned=False):
     anywhere = pl.BlockSpec(memory_space=pl.ANY)
+    shape = jax.ShapeDtypeStruct(block.shape, block.dtype)
+    if pinned:
+        block = pltpu.with_memory_space_constraint(block, pltpu.HBM)
+        shape = pltpu.HBM(block.shape, block.dtype)
     return pl.pallas_call(
         wait_kernel,
         in_specs=[anywhere] * (1 + len(others)),
         out_specs=anywhere,
-        out_shape=jax.ShapeDtypeStruct(block.shape, block.dtype),
+        out_shape=shape,
         input_output_aliases={0: 0},
         compiler_params=pltpu.CompilerParams(vmem_limit_bytes=2**20),
         name="after",
@@ -874,7 +872,7 @@
         held,
     )
     packed = trade_chips(packed)
-    pieces = from_chips(after(laid, packed))
+    pieces = from_chips(after(laid, packed, pinned=True))
     traded = trade_teams(share(teams, packed, w_up))
     up_blocks = traded[:, chips * held :]
     packed = both_cores(traded[:, : chips * held].reshape(teams, chips, held, width), 2)
@@ -973,6 +971,7 @@
     )
     up_sum = sums[: teams * part].reshape(teams, part, quarter)
 
+    out_traded = trade_teams(out_sum)
     small = (
         grad_b_out,
         grad_gain_one,
@@ -988,7 +987,7 @@
     ).reshape(teams * chips, 2, 1, -1)
     lanes = 3 * group - 128 - tall.shape[-1]
     tall = jnp.pad(tall, ((0, 0),) * 2 + ((0, held - part - 1), (0, lanes)))
-    *token_part, own_terms, away_terms = finish(
+    token_part, own_terms, away_terms = finish(
         chips,
         jnp.stack([chip, core]),
         mine,
@@ -997,17 +996,21 @@
         kept,
         to_core(away),
         jnp.concatenate([small, tall], 3),
-    )
-    token_come = [to_chip(token_part[d], d) for d in range(1, chips)]
-    token_grad = grad_first + total([token_part[0]] + token_come)
+        out_traded,
+    )
+    bundles = bundle(team[None], own_terms, to_core(away_terms), up_sum)
+    traded = [bundles[0]] + [to_team(bundles[d], d) for d in range(1, teams)]
+    token_come = trade_chips(token_part)
+    token_come = after(token_come, *traded[1:])
+    token_grad = grad_first + jnp.sum(token_come.astype(f32), 0)
     grad_tokens = token_grad.astype(low)
-
-    traded = bundle(own_terms, to_core(away_terms), out_sum, up_sum)
-    traded = trade_teams(traded)
-    out_up = traded[:, -part:].transpose(1, 0, 2).reshape(part, hidden).astype(f32)
-    terms = jnp.sum(traded[:, :-part].astype(f32), 0).astype(low)
-    out_down = after(sums, traded)[teams * part :].astype(f32)
-    found = trade_chips(after(terms.reshape(chips, held + part, width), grad_tokens))
+    out_up = ordered([block[-part:] for block in traded], team)
+    out_up = out_up.transpose(1, 0, 2).reshape(part, hidden).astype(f32)
+    terms = total([block[:-part] for block in traded]).astype(low)
+    out_down = after(sums, traded[1])[teams * part :].astype(f32)
+    out_sum = jnp.sum(out_traded.astype(f32), 0).astype(low)
+    terms = jnp.concatenate([terms.reshape(chips, held, width), out_sum], 1)
+    found = trade_chips(after(terms, grad_tokens))
     out_query, out_key, out_value, out_out, short_sum, sums = unpack(part, group, found)
     vec = [short_sum[i, :part] for i in range(6)]
     out_b_up = short_sum[0, 128 : 128 + b_up.shape[0]]

time: 241 us -> 234 us (0.971)
  local copies, waits for them, and re-layouts: 29.4 us -> 23.2 us
  starting transfers between devices: 52.2 us -> 56 us
  waiting for transfers between devices: 85.1 us -> 82.6 us
    ppermute x12 -> x9, waiting for transfers between devices: 38.3 us -> 20.3 us  [to_chip(): return lax.ppermute(block, 'ctx', route)]
    all_to_all x2 -> x3, waiting for transfers between devices: 14.9 us -> 27.5 us  [trade_chips(): return lax.all_to_all(blocks, 'ctx', 0, 0, axis_index_groups=same_core)]
    ppermute x12 -> x15, starting transfers between devices: 13.5 us -> 17.8 us  [to_team(): lax.ppermute(block, 'batch', [(i, (i + distance) % teams) for i in range(...]
    ppermute x12 -> x15, waiting for transfers between devices: 25.7 us -> 30 us  [to_team(): lax.ppermute(block, 'batch', [(i, (i + distance) % teams) for i in range(...]
    all_to_all x2 -> x3, starting transfers between devices: 9.93 us -> 13.8 us  [trade_chips(): return lax.all_to_all(blocks, 'ctx', 0, 0, axis_index_groups=same_core)]
    ppermute x12 -> x9, starting transfers between devices: 16.1 us -> 12.5 us  [to_chip(): return lax.ppermute(block, 'ctx', route)]
    unnamed x121 -> x101, local copies, waits for them, and re-layouts: 9.64 us -> 7.35 us
  transfers between devices with their start and end apart: 40 -> 41, of which waited for: 22 -> 18; matrix products, arithmetic and copies ran while one was open for 11% -> 11% of each run, Pallas kernels for 10% -> 11%
where the time goes in v3:
time: 234 us; the launch traced here: 233 us
  waiting for transfers between devices  82.6 us (35%)
  starting transfers between devices  56 us (24%)
  Pallas kernels  28.2 us (12%)
  local copies, waits for them, and re-layouts  23.2 us (10%)
  other arithmetic  16 us (7%)
  between operations  15.7 us (7%)
  matrix products  10.9 us (5%)
    ppermute x15, waiting for transfers between devices, to_team(): lax.ppermute(block, 'batch', [(i, (i + distance) % teams) for i in range(...  30 us
    all_to_all x3, waiting for transfers between devices, trade_chips(): return lax.all_to_all(blocks, 'ctx', 0, 0, axis_index_groups=same_core)  27.5 us
    pallas_call x5, Pallas kernels, one_step(): pl.pallas_call(functools.partial(copied_kernel, kernel, first, far, len(o...  23 us
    ppermute x9, waiting for transfers between devices, to_chip(): return lax.ppermute(block, 'ctx', route)  20.3 us
    ppermute x15, starting transfers between devices, to_team(): lax.ppermute(block, 'batch', [(i, (i + distance) % teams) for i in range(...  17.8 us
    all_to_all x3, starting transfers between devices, trade_chips(): return lax.all_to_all(blocks, 'ctx', 0, 0, axis_index_groups=same_core)  13.8 us
    ppermute x9, starting transfers between devices, to_chip(): return lax.ppermute(block, 'ctx', route)  12.5 us
    dot_general x9, matrix products, dot(): lax.dot_general(left, right, (dims, ((), ())), preferred_element_type=jnp...  10.9 us
  transfers between devices with their start and end apart: 41, of which 18 were waited for; matrix products, arithmetic and copies ran while one was open for 11% of the time, Pallas kernels for 11%

profile of v3, /device:TPU:0, one launch (start us, length us, event | category | flops | bytes accessed | tf_op | source)
XLA Modules:
  0.0 232.7 jit_solution(2753377731369288843)
XLA Ops:
  7.2 1.4 stack.117.vectors
  8.6 1.6 pack.1
  10.1 6.3 %all-to-all-start = ((bf16[4,32,768]{2,1,0:T(8,128)(2,1)}), bf16[4,32,768]{2,1,0:T(8,128)(2,1)S(1)}, u32[]{:S(2)}, u32[]{:S(2)}) async-start(bf16[4,32,768]{2,1,0:T(8,128)(2,1)} %pack.1), calls=%async_computation | async-start | bytes 393216 | tf_op jit(solution)/shard_map/all_to_all | solution.py:827
  16.5 1.6 lay.1.refs_0_
  18.1 5.9 %all-to-all-done.refs_1_.packed = bf16[4,32,768]{2,1,0:T(8,128)(2,1)S(1)} async-done(((bf16[4,32,768]{2,1,0:T(8,128)(2,1)}), bf16[4,32,768]{2,1,0:T(8,128)(2,1)S(1)}, u32[]{:S(2)}, u32[]{:S(2)}) %all-to-all-start) | async-done | bytes 196640 | tf_op jit(solution)/shard_map/all_to_all | solution.py:827
  24.0 1.4 collective-permute-start.2
  26.9 2.0 share.1
  28.9 3.7 %all-to-all-start.1 = ((bf16[4,152,768]{2,1,0:T(8,128)(2,1)}), bf16[4,152,768]{2,1,0:T(8,128)(2,1)S(1)}, u32[]{:S(2)}, u32[]{:S(2)}) async-start(bf16[4,152,768]{2,1,0:T(8,128)(2,1)} %share.1), calls=%async_computation.1 | async-start | bytes 1867776 | tf_op jit(solution)/shard_map/all_to_all | solution.py:830
  32.7 12.4 %collective-permute-done.1.refs_3_ = bf16[152,768]{1,0:T(8,128)(2,1)S(1)} collective-permute-done((bf16[152,768]{1,0:T(8,128)(2,1)}, bf16[152,768]{1,0:T(8,128)(2,1)S(1)}, u32[]{:S(2)}, u32[]{:S(2)}) %collective-permute-start.1) | collective-permute-done | bytes 233504 | tf_op jit(solution)/shard_map/ppermute | solution.py:800
  45.7 1.0 slice.182
  47.5 1.8 collective-permute-done.7
  49.3 1.5 select_bitcast_fusion.1
  52.3 1.3 fusion.6
  53.6 9.4 %attend.1 = (bf16[512,768]{1,0:T(8,128)(2,1)}, bf16[512,192]{1,0:T(8,128)(2,1)}, bf16[1024,256]{1,0:T(8,128)(2,1)}, bf16[1024,192]{1,0:T(8,128)(2,1)}, f32[192,5...) custom-call(s32[9]{0:T(128)S(1)} %pad_add_fusion.refs_0_, ...), custom_call_target="tpu_custom_call" | custom-call | flops 2516582400 | bytes 2680356 | tf_op jit(solution)/shard_map/attend/pallas_call | solution.py:376
  63.0 1.5 collective-permute-start.8
  65.8 3.5 %all-to-all-start.2 = ((bf16[4,4,24,768]{3,2,1,0:T(8,128)(2,1)}), bf16[4,4,24,768]{3,2,1,0:T(8,128)(2,1)S(1)}, u32[]{:S(2)}, u32[]{:S(2)}) async-start(bf16[4,4,24,768]{3,2,1,0:T(8,128)(2,1)} %broadcast_in_dim.12), calls=%async_computation.2 | async-start | bytes 1179648 | tf_op jit(solution)/shard_map/all_to_all | solution.py:830
  69.3 1.6 collective-permute-start.9
  70.9 2.0 collective-permute-start.10
  73.0 6.3 %collective-permute-done.9 = bf16[192,128]{1,0:T(8,128)(2,1)S(1)} collective-permute-done((bf16[192,128]{1,0:T(8,128)(2,1)S(1)}, bf16[192,128]{1,0:T(8,128)(2,1)S(1)}, u32[]{:S(2)}, u32[]{:S(2)}) %collective-permute-start.9) | collective-permute-done | bytes 49184 | tf_op jit(solution)/shard_map/ppermute | solution.py:800
  79.6 1.9 collective-permute-done.11
  83.2 2.8 %collective-permute-start.14 = (bf16[128,768]{1,0:T(8,128)(2,1)S(1)}, bf16[128,768]{1,0:T(8,128)(2,1)S(1)}, u32[]{:S(2)}, u32[]{:S(2)}) collective-permute-start(bf16[128,768]{1,0:T(8,128)(2,1)S(1)} %fusion.19), channel_id=1, source_target_pairs={{0,24},{8,0},{16,8},{24,16},{1,25},{9,1},{17,9},{25,17},{2,26},{10... | collective-permute-start | bytes 589832 | tf_op jit(solution)/shard_map/ppermute | solution.py:806
  87.1 1.8 fusion.31
  89.0 2.3 collective-permute-done.14
  91.3 5.6 %collective-permute-done.13 = bf16[128,768]{1,0:T(8,128)(2,1)S(1)} collective-permute-done((bf16[128,768]{1,0:T(8,128)(2,1)S(1)}, bf16[128,768]{1,0:T(8,128)(2,1)S(1)}, u32[]{:S(2)}, u32[]{:S(2)}) %collective-permute-start.13) | collective-permute-done | bytes 196640 | tf_op jit(solution)/shard_map/ppermute | solution.py:806
  96.9 2.8 %fusion.3 = (f32[512,768]{1,0:T(8,128)}, bf16[512,768]{1,0:T(8,128)(2,1)S(1)}) fusion(f32[768]{0:T(1024)S(1)} %dynamic_slice.48, bf16[768,768]{1,0:T(8,128)(2,1)S(1)} %bitcast.175, bf16[128,768]{1,0:T(8,128)(2,1)S(1)} %collective-permute-done.14, bf16[128,768]{1,0:T(8,128)(2,1)S(1)} %collective-permute-done.13, ...), kind=kOutput, calls=%fused_computation.5 | convolution fusion | flops 611450880 | bytes 4328448 | tf_op jit(solution)/shard_map/dot_general | solution.py:317
  99.7 1.9 fusion.37
  102.4 1.5 collective-permute-start.17
  104.5 4.3 %collective-permute-done.15 = bf16[128,768]{1,0:T(8,128)(2,1)S(1)} collective-permute-done((bf16[128,768]{1,0:T(8,128)(2,1)S(1)}, bf16[128,768]{1,0:T(8,128)(2,1)S(1)}, u32[]{:S(2)}, u32[]{:S(2)}) %collective-permute-start.15) | collective-permute-done | bytes 196640 | tf_op jit(solution)/shard_map/ppermute | solution.py:806
  108.8 3.1 %collective-permute-done.17 = bf16[128,768]{1,0:T(8,128)(2,1)S(1)} collective-permute-done((bf16[128,768]{1,0:T(8,128)(2,1)S(1)}, bf16[128,768]{1,0:T(8,128)(2,1)S(1)}, u32[]{:S(2)}, u32[]{:S(2)}) %collective-permute-start.17) | collective-permute-done | bytes 196640 | tf_op jit(solution)/shard_map/ppermute | solution.py:806
  112.8 1.4 fusion.29
  115.8 1.1 collective-permute-start.19
  116.9 1.1 collective-permute-start.18
  118.0 4.4 %collective-permute-done.20 = bf16[128,768]{1,0:T(8,128)(2,1)S(1)} collective-permute-done((bf16[128,768]{1,0:T(8,128)(2,1)S(1)}, bf16[128,768]{1,0:T(8,128)(2,1)S(1)}, u32[]{:S(2)}, u32[]{:S(2)}) %collective-permute-start.20) | collective-permute-done | bytes 196640 | tf_op jit(solution)/shard_map/ppermute | solution.py:806
  122.4 3.7 %collective-permute-done.19 = bf16[128,768]{1,0:T(8,128)(2,1)S(1)} collective-permute-done((bf16[128,768]{1,0:T(8,128)(2,1)S(1)}, bf16[128,768]{1,0:T(8,128)(2,1)S(1)}, u32[]{:S(2)}, u32[]{:S(2)}) %collective-permute-start.19) | collective-permute-done | bytes 196640 | tf_op jit(solution)/shard_map/ppermute | solution.py:806
  131.3 1.6 pad_maximum_fusion
  133.3 1.2 collective-permute-start.22
  134.4 2.5 %collective-permute-start.21 = (bf16[128,768]{1,0:T(8,128)(2,1)S(1)}, bf16[128,768]{1,0:T(8,128)(2,1)}, u32[]{:S(2)}, u32[]{:S(2)}) collective-permute-start(bf16[128,768]{1,0:T(8,128)(2,1)S(1)} %get-tuple-element.97.refs_1_), channel_id=1, source_target_pairs={{0,24},{8,0},{16,8},{24,16},{1,25},{9,1},{17,9},{25,17},{2,26},{10... | collective-permute-start | bytes 589832 | tf_op jit(solution)/shard_map/ppermute | solution.py:806
  137.0 3.9 %collective-permute-done.23 = bf16[128,768]{1,0:T(8,128)(2,1)S(1)} collective-permute-done((bf16[128,768]{1,0:T(8,128)(2,1)S(1)}, bf16[128,768]{1,0:T(8,128)(2,1)S(1)}, u32[]{:S(2)}, u32[]{:S(2)}) %collective-permute-start.23) | collective-permute-done | bytes 196640 | tf_op jit(solution)/shard_map/ppermute | solution.py:806
  140.9 2.0 collective-permute-done.22
  142.9 2.2 multiply_reduce_fusion
  145.0 1.0 convert_reduce_fusion.4
  146.5 1.9 fusion.20
  148.5 2.2 fusion.7
  150.6 1.3 collective-permute-start.24
  151.9 2.6 %collective-permute-start.26 = (bf16[192,128]{1,0:T(8,128)(2,1)S(1)}, bf16[192,128]{1,0:T(8,128)(2,1)S(1)}, u32[]{:S(2)}, u32[]{:S(2)}) collective-permute-start(bf16[192,128]{1,0:T(8,128)(2,1)S(1)} %get-tuple-element.104), channel_id=1, source_target_pairs={{0,6},{1,7},{2,0},{3,1},{4,2},{5,3},{6,4},{7,5},{8,14},{9,15},{10,... | collective-permute-start | bytes 147464 | tf_op jit(solution)/shard_map/ppermute | solution.py:800
  154.5 1.5 collective-permute-start.25
  155.9 2.2 fusion.5.refs_10_
  158.1 3.6 %all-to-all-start.3 = ((bf16[4,4,24,768]{3,2,1,0:T(8,128)(2,1)}), bf16[4,4,24,768]{3,2,1,0:T(8,128)(2,1)S(1)}, u32[]{:S(2)}, u32[]{:S(2)}) async-start(bf16[4,4,24,768]{3,2,1,0:T(8,128)(2,1)} %fusion.5.refs_10_), calls=%async_computation.3 | async-start | bytes 1179648 | tf_op jit(solution)/shard_map/all_to_all | solution.py:830
  161.8 1.6 collective-permute-done.25.refs_8_
  164.3 6.8 %attend_back.1 = (bf16[512,192]{1,0:T(8,128)(2,1)}, f32[512,384]{1,0:T(8,128)}, bf16[512,384]{1,0:T(8,128)(2,1)}) custom-call(s32[9]{0:T(128)S(1)} %pad_add_fusion.refs_0_, bf16[512,192]{1,0:T(8,128)(2,1)S(1)} %copy-done.12, bf16[1024,256]{1,0:T(8,128)(2,1)S(1)} %copy-done.9, bf16[1024,192]{1,0:T(8,128)(2,1)S(1)} %copy-done.10, f32[192,512]{1,0:T(8,128)S(1)} %copy-done.11, ...), custom_call_target="tpu_custom_call" | custom-call | flops 4026531840 | bytes 2299940 | tf_op jit(solution)/shard_map/attend_back/pallas_call | solution.py:376
  173.9 1.1 copy-done.4
  175.0 0.9 copy-done.7
  175.9 4.3 %finish.1 = (bf16[4,128,768]{2,1,0:T(8,128)(2,1)}, f32[16,32,576]{2,1,0:T(8,128)}, bf16[16,32,576]{2,1,0:T(8,128)(2,1)}) custom-call(s32[2]{0:T(128)S(1)} %pad_add_fusion.1.refs_0_, bf16[512,768]{1,0:T(8,128)(2,1)S(1)} %copy-done.3, bf16[768,576]{1,0:T(8,128)(2,1)S(1)} %bitcast.163, bf16[512,192]{1,0:T(8,128)(2,1)S(1)} %copy-done.7, ...), custom_call_target="tpu_custom_call" | custom-call | flops 905969664 | bytes 4227080 | tf_op jit(solution)/shard_map/finish/pallas_call | solution.py:376
  180.2 3.9 %all-to-all-start.4 = ((bf16[4,128,768]{2,1,0:T(8,128)(2,1)}), bf16[4,128,768]{2,1,0:T(8,128)(2,1)S(1)}, u32[]{:S(2)}, u32[]{:S(2)}) async-start(bf16[4,128,768]{2,1,0:T(8,128)(2,1)} %get-tuple-element.60), calls=%async_computation.4 | async-start | bytes 1572864 | tf_op jit(solution)/shard_map/all_to_all | solution.py:827
  185.4 1.1 collective-permute-done.29.refs_2_
  186.5 1.5 bundle.1
  188.0 2.6 %collective-permute-start.30 = (bf16[152,768]{1,0:T(8,128)(2,1)}, bf16[152,768]{1,0:T(8,128)(2,1)S(1)}, u32[]{:S(2)}, u32[]{:S(2)}) collective-permute-start(bf16[152,768]{1,0:T(8,128)(2,1)} %get-tuple-element.63), channel_id=1, source_target_pairs={{0,8},{8,16},{16,24},{24,0},{1,9},{9,17},{17,25},{25,1},{2,10},{10... | collective-permute-start | bytes 700424 | tf_op jit(solution)/shard_map/ppermute | solution.py:806
  190.7 1.4 collective-permute-start.32
  192.2 12.7 %all-to-all-done.4.refs_0_ = bf16[4,128,768]{2,1,0:T(8,128)(2,1)S(1)} async-done(((bf16[4,128,768]{2,1,0:T(8,128)(2,1)}), bf16[4,128,768]{2,1,0:T(8,128)(2,1)S(1)}, u32[]{:S(2)}, u32[]{:S(2)}) %all-to-all-start.4) | async-done | bytes 786464 | tf_op jit(solution)/shard_map/all_to_all | solution.py:827
  206.8 3.6 %all-to-all-start.5 = ((bf16[4,56,768]{2,1,0:T(8,128)(2,1)}), bf16[4,56,768]{2,1,0:T(8,128)(2,1)S(1)}, u32[]{:S(2)}, u32[]{:S(2)}) async-start(bf16[4,56,768]{2,1,0:T(8,128)(2,1)} %after.16), calls=%async_computation.6 | async-start | bytes 688128 | tf_op jit(solution)/shard_map/all_to_all | solution.py:827
  212.0 8.9 %all-to-all-done.5.refs_0_ = bf16[4,56,768]{2,1,0:T(8,128)(2,1)S(1)} async-done(((bf16[4,56,768]{2,1,0:T(8,128)(2,1)}), bf16[4,56,768]{2,1,0:T(8,128)(2,1)S(1)}, u32[]{:S(2)}, u32[]{:S(2)}) %all-to-all-start.5) | async-done | bytes 344096 | tf_op jit(solution)/shard_map/all_to_all | solution.py:827
  220.8 1.0 unpack.1
  221.8 1.2 slice_bitcast_fusion.9
  223.0 1.4 slice_bitcast_fusion.6
  (237 shorter events, 27.8 us)
Async XLA Ops:
  10.1 13.8 %all-to-all-start = ((bf16[4,32,768]{2,1,0:T(8,128)(2,1)}), bf16[4,32,768]{2,1,0:T(8,128)(2,1)S(1)}, u32[]{:S(2)}, u32[]{:S(2)}) async-start(bf16[4,32,768]{2,1,0:T(8,128)(2,1)} %pack.1), calls=%async_computation | async-start | bytes 393216 | tf_op jit(solution)/shard_map/all_to_all | solution.py:827
  16.5 37.1 %collective-permute-start.3 = (bf16[128,768]{1,0:T(8,128)(2,1)}, bf16[128,768]{1,0:T(8,128)(2,1)S(1)}, u32[]{:S(2)}, u32[]{:S(2)}) collective-permute-start(bf16[128,768]{1,0:T(8,128)(2,1)} %refs_1_.1), channel_id=1, source_target_pairs={{0,1},{1,0},{2,3},{3,2},{4,5},{5,4},{6,7},{7,6},{8,9},{9,8},{10,11... | collective-permute-start | bytes 589832 | tf_op jit(solution)/shard_map/ppermute | solution.py:803
  24.0 2.9 %copy-start = (bf16[4,32,768]{2,1,0:T(8,128)(2,1)}, bf16[4,32,768]{2,1,0:T(8,128)(2,1)S(1)}, u32[]{:S(2)}) copy-start(bf16[4,32,768]{2,1,0:T(8,128)(2,1)S(1)} %all-to-all-done.refs_1_.packed) | copy-start | bytes 589828
  24.0 8.7 %collective-permute-start.2 = (bf16[152,768]{1,0:T(8,128)(2,1)}, bf16[152,768]{1,0:T(8,128)(2,1)S(1)}, u32[]{:S(2)}, u32[]{:S(2)}) collective-permute-start(bf16[152,768]{1,0:T(8,128)(2,1)} %after.9), channel_id=1, source_target_pairs={{0,6},{1,7},{2,0},{3,1},{4,2},{5,3},{6,4},{7,5},{8,14},{9,15},{10,... | collective-permute-start | bytes 700424 | tf_op jit(solution)/shard_map/ppermute | solution.py:800
  26.1 19.0 %collective-permute-start.1 = (bf16[152,768]{1,0:T(8,128)(2,1)}, bf16[152,768]{1,0:T(8,128)(2,1)S(1)}, u32[]{:S(2)}, u32[]{:S(2)}) collective-permute-start(bf16[152,768]{1,0:T(8,128)(2,1)} %after.9), channel_id=1, source_target_pairs={{0,4},{1,5},{2,6},{3,7},{4,0},{5,1},{6,2},{7,3},{8,12},{9,13},{10,... | collective-permute-start | bytes 700424 | tf_op jit(solution)/shard_map/ppermute | solution.py:800
  26.7 18.5 %collective-permute-start = (bf16[152,768]{1,0:T(8,128)(2,1)}, bf16[152,768]{1,0:T(8,128)(2,1)S(1)}, u32[]{:S(2)}, u32[]{:S(2)}) collective-permute-start(bf16[152,768]{1,0:T(8,128)(2,1)} %after.9), channel_id=1, source_target_pairs={{0,2},{1,3},{2,4},{3,5},{4,6},{5,7},{6,0},{7,1},{8,10},{9,11},{10,... | collective-permute-start | bytes 700424 | tf_op jit(solution)/shard_map/ppermute | solution.py:800
  26.9 18.8 %copy-start.29 = (bf16[24,768]{1,0:T(8,128)(2,1)S(1)}, bf16[24,768]{1,0:T(8,128)(2,1)}, u32[]{:S(2)}) copy-start(bf16[24,768]{1,0:T(8,128)(2,1)} %w_out.1) | copy-start | bytes 110596
  28.9 16.8 %all-to-all-start.1 = ((bf16[4,152,768]{2,1,0:T(8,128)(2,1)}), bf16[4,152,768]{2,1,0:T(8,128)(2,1)S(1)}, u32[]{:S(2)}, u32[]{:S(2)}) async-start(bf16[4,152,768]{2,1,0:T(8,128)(2,1)} %share.1), calls=%async_computation.1 | async-start | bytes 1867776 | tf_op jit(solution)/shard_map/all_to_all | solution.py:830
  32.6 14.1 %copy-start.30 = (bf16[96,768]{1,0:T(8,128)(2,1)S(1)}, bf16[96,768]{1,0:T(8,128)(2,1)}, u32[]{:S(2)}) copy-start(bf16[96,768]{1,0:T(8,128)(2,1)} %param.31) | copy-start | bytes 442372
  32.6 54.5 %all-gather.3.cloned.1.call-start = ((), (), s32[]{:S(2)}) async-start(), calls=%async_computation.8 | async-start | bytes 2654208 | tf_op jit(solution)/shard_map/all_gather | solution.py:897
  32.6 20.9 %collective-permute-start.6 = (bf16[152,768]{1,0:T(8,128)(2,1)S(1)}, bf16[152,768]{1,0:T(8,128)(2,1)S(1)}, u32[]{:S(2)}, u32[]{:S(2)}) collective-permute-start(bf16[152,768]{1,0:T(8,128)(2,1)S(1)} %collective-permute-done.2.refs_4_), channel_id=1, source_target_pairs={{0,1},{1,0},{2,3},{3,2},{4,5},{5,4},{6,7},{7,6},{8,9},{9,8},{10,11... | collective-permute-start | bytes 700424 | tf_op jit(solution)/shard_map/ppermute | solution.py:803
  45.2 8.4 %collective-permute-start.5 = (bf16[152,768]{1,0:T(8,128)(2,1)S(1)}, bf16[152,768]{1,0:T(8,128)(2,1)S(1)}, u32[]{:S(2)}, u32[]{:S(2)}) collective-permute-start(bf16[152,768]{1,0:T(8,128)(2,1)S(1)} %collective-permute-done.1.refs_3_), channel_id=1, source_target_pairs={{0,1},{1,0},{2,3},{3,2},{4,5},{5,4},{6,7},{7,6},{8,9},{9,8},{10,11... | collective-permute-start | bytes 700424 | tf_op jit(solution)/shard_map/ppermute | solution.py:803
  45.2 8.4 %collective-permute-start.4 = (bf16[152,768]{1,0:T(8,128)(2,1)S(1)}, bf16[152,768]{1,0:T(8,128)(2,1)S(1)}, u32[]{:S(2)}, u32[]{:S(2)}) collective-permute-start(bf16[152,768]{1,0:T(8,128)(2,1)S(1)} %collective-permute-done.refs_2_), channel_id=1, source_target_pairs={{0,1},{1,0},{2,3},{3,2},{4,5},{5,4},{6,7},{7,6},{8,9},{9,8},{10,11... | collective-permute-start | bytes 700424 | tf_op jit(solution)/shard_map/ppermute | solution.py:803
  46.7 2.6 %collective-permute-start.7 = (bf16[4,4,32,768]{3,2,1,0:T(8,128)(2,1)}, bf16[4,4,32,768]{3,2,1,0:T(8,128)(2,1)}, u32[]{:S(2)}, u32[]{:S(2)}) collective-permute-start(bf16[4,4,32,768]{3,2,1,0:T(8,128)(2,1)} %bitcast.11), channel_id=1, source_target_pairs={{0,1},{1,0},{2,3},{3,2},{4,5},{5,4},{6,7},{7,6},{8,9},{9,8},{10,11... | collective-permute-start | bytes 2359304 | tf_op jit(solution)/shard_map/ppermute | solution.py:803
  63.0 10.0 %collective-permute-start.8 = (bf16[192,128]{1,0:T(8,128)(2,1)}, bf16[192,128]{1,0:T(8,128)(2,1)S(1)}, u32[]{:S(2)}, u32[]{:S(2)}) collective-permute-start(bf16[192,128]{1,0:T(8,128)(2,1)} %get-tuple-element.45), channel_id=1, source_target_pairs={{0,6},{1,7},{2,0},{3,1},{4,2},{5,3},{6,4},{7,5},{8,14},{9,15},{10,... | collective-permute-start | bytes 147464 | tf_op jit(solution)/shard_map/ppermute | solution.py:800
  64.5 4.8 %copy-start.39 = (bf16[192,128]{1,0:T(8,128)(2,1)S(1)}, bf16[192,128]{1,0:T(8,128)(2,1)}, u32[]{:S(2)}) copy-start(bf16[192,128]{1,0:T(8,128)(2,1)} %get-tuple-element.46) | copy-start | bytes 147460
  64.5 6.4 %copy-start.38 = (bf16[192,128]{1,0:T(8,128)(2,1)S(1)}, bf16[192,128]{1,0:T(8,128)(2,1)}, u32[]{:S(2)}) copy-start(bf16[192,128]{1,0:T(8,128)(2,1)} %get-tuple-element.47) | copy-start | bytes 147460
  64.6 14.8 %copy-start.31 = (bf16[192,128]{1,0:T(8,128)(2,1)S(1)}, bf16[192,128]{1,0:T(8,128)(2,1)}, u32[]{:S(2)}) copy-start(bf16[192,128]{1,0:T(8,128)(2,1)} %get-tuple-element.48) | copy-start | bytes 147460
  64.6 14.8 %copy-start.8 = (f32[3,512]{1,0:T(4,128)S(1)}, f32[3,512]{1,0:T(4,128)}, u32[]{:S(2)}) copy-start(f32[3,512]{1,0:T(4,128)} %get-tuple-element.49.refs_1_.refs_5_) | copy-start | bytes 18436
  65.8 13.6 %all-to-all-start.2 = ((bf16[4,4,24,768]{3,2,1,0:T(8,128)(2,1)}), bf16[4,4,24,768]{3,2,1,0:T(8,128)(2,1)S(1)}, u32[]{:S(2)}, u32[]{:S(2)}) async-start(bf16[4,4,24,768]{3,2,1,0:T(8,128)(2,1)} %broadcast_in_dim.12), calls=%async_computation.2 | async-start | bytes 1179648 | tf_op jit(solution)/shard_map/all_to_all | solution.py:830
  69.3 115.2 %reduce-scatter.2.cloned.1.call-start = ((), (), s32[]{:S(2)}) async-start(), calls=%async_computation.7 | async-start | bytes 2654208 | tf_op jit(solution)/shard_map/reduce_scatter | solution.py:969
  69.3 10.0 %collective-permute-start.9 = (bf16[192,128]{1,0:T(8,128)(2,1)S(1)}, bf16[192,128]{1,0:T(8,128)(2,1)S(1)}, u32[]{:S(2)}, u32[]{:S(2)}) collective-permute-start(bf16[192,128]{1,0:T(8,128)(2,1)S(1)} %copy-done.39), channel_id=1, source_target_pairs={{0,4},{1,5},{2,6},{3,7},{4,0},{5,1},{6,2},{7,3},{8,12},{9,13},{10,... | collective-permute-start | bytes 147464 | tf_op jit(solution)/shard_map/ppermute | solution.py:800
  70.9 8.4 %collective-permute-start.10 = (bf16[192,128]{1,0:T(8,128)(2,1)S(1)}, bf16[192,128]{1,0:T(8,128)(2,1)S(1)}, u32[]{:S(2)}, u32[]{:S(2)}) collective-permute-start(bf16[192,128]{1,0:T(8,128)(2,1)S(1)} %copy-done.38), channel_id=1, source_target_pairs={{0,2},{1,3},{2,4},{3,5},{4,6},{5,7},{6,0},{7,1},{8,10},{9,11},{10,... | collective-permute-start | bytes 147464 | tf_op jit(solution)/shard_map/ppermute | solution.py:800
  79.4 2.1 collective-permute-start.11
  83.2 13.7 %copy-start.27 = (bf16[128,768]{1,0:T(8,128)(2,1)}, bf16[128,768]{1,0:T(8,128)(2,1)S(1)}, u32[]{:S(2)}) copy-start(bf16[128,768]{1,0:T(8,128)(2,1)S(1)} %fusion.19) | copy-start | bytes 589828
  83.2 8.1 %collective-permute-start.14 = (bf16[128,768]{1,0:T(8,128)(2,1)S(1)}, bf16[128,768]{1,0:T(8,128)(2,1)S(1)}, u32[]{:S(2)}, u32[]{:S(2)}) collective-permute-start(bf16[128,768]{1,0:T(8,128)(2,1)S(1)} %fusion.19), channel_id=1, source_target_pairs={{0,24},{8,0},{16,8},{24,16},{1,25},{9,1},{17,9},{25,17},{2,26},{10... | collective-permute-start | bytes 589832 | tf_op jit(solution)/shard_map/ppermute | solution.py:806
  86.0 10.9 %collective-permute-start.13 = (bf16[128,768]{1,0:T(8,128)(2,1)S(1)}, bf16[128,768]{1,0:T(8,128)(2,1)S(1)}, u32[]{:S(2)}, u32[]{:S(2)}) collective-permute-start(bf16[128,768]{1,0:T(8,128)(2,1)S(1)} %fusion.19), channel_id=1, source_target_pairs={{0,16},{8,24},{16,0},{24,8},{1,17},{9,25},{17,1},{25,9},{2,18},{10... | collective-permute-start | bytes 589832 | tf_op jit(solution)/shard_map/ppermute | solution.py:806
  86.6 10.3 %collective-permute-start.12 = (bf16[128,768]{1,0:T(8,128)(2,1)S(1)}, bf16[128,768]{1,0:T(8,128)(2,1)S(1)}, u32[]{:S(2)}, u32[]{:S(2)}) collective-permute-start(bf16[128,768]{1,0:T(8,128)(2,1)S(1)} %fusion.19), channel_id=1, source_target_pairs={{0,8},{8,16},{16,24},{24,0},{1,9},{9,17},{17,25},{25,1},{2,10},{10... | collective-permute-start | bytes 589832 | tf_op jit(solution)/shard_map/ppermute | solution.py:806
  88.9 10.8 %copy-start.17 = (bf16[8,96,768]{2,1,0:T(8,128)(2,1)}, bf16[8,96,768]{2,1,0:T(8,128)(2,1)S(1)}, u32[]{:S(2)}) copy-start(bf16[8,96,768]{2,1,0:T(8,128)(2,1)S(1)} %get-tuple-element.89) | copy-start | bytes 3538948
  89.0 10.7 %copy-start.21 = (bf16[4,8,24,768]{3,2,1,0:T(8,128)(2,1)}, bf16[4,8,24,768]{3,2,1,0:T(8,128)(2,1)S(1)}, u32[]{:S(2)}) copy-start(bf16[4,8,24,768]{3,2,1,0:T(8,128)(2,1)S(1)} %copy.57) | copy-start | bytes 3538948
  91.3 8.4 %copy-start.32 = (bf16[128,768]{1,0:T(8,128)(2,1)}, bf16[128,768]{1,0:T(8,128)(2,1)S(1)}, u32[]{:S(2)}) copy-start(bf16[128,768]{1,0:T(8,128)(2,1)S(1)} %collective-permute-done.14) | copy-start | bytes 589828
  96.9 2.8 %copy-start.34 = (bf16[128,768]{1,0:T(8,128)(2,1)}, bf16[128,768]{1,0:T(8,128)(2,1)S(1)}, u32[]{:S(2)}) copy-start(bf16[128,768]{1,0:T(8,128)(2,1)S(1)} %collective-permute-done.13) | copy-start | bytes 589828
  101.7 12.7 %copy-start.19 = (bf16[128,768]{1,0:T(8,128)(2,1)S(1)}, bf16[128,768]{1,0:T(8,128)(2,1)}, u32[]{:S(2)}) copy-start(bf16[128,768]{1,0:T(8,128)(2,1)} %param.35) | copy-start | bytes 589828
  101.7 7.1 %collective-permute-start.15 = (bf16[128,768]{1,0:T(8,128)(2,1)S(1)}, bf16[128,768]{1,0:T(8,128)(2,1)S(1)}, u32[]{:S(2)}, u32[]{:S(2)}) collective-permute-start(bf16[128,768]{1,0:T(8,128)(2,1)S(1)} %get-tuple-element.100), channel_id=1, source_target_pairs={{0,24},{8,0},{16,8},{24,16},{1,25},{9,1},{17,9},{25,17},{2,26},{10... | collective-permute-start | bytes 589832 | tf_op jit(solution)/shard_map/ppermute | solution.py:806
  102.4 9.5 %collective-permute-start.17 = (bf16[128,768]{1,0:T(8,128)(2,1)S(1)}, bf16[128,768]{1,0:T(8,128)(2,1)S(1)}, u32[]{:S(2)}, u32[]{:S(2)}) collective-permute-start(bf16[128,768]{1,0:T(8,128)(2,1)S(1)} %get-tuple-element.101), channel_id=1, source_target_pairs={{0,8},{8,16},{16,24},{24,0},{1,9},{9,17},{17,25},{25,1},{2,10},{10... | collective-permute-start | bytes 589832 | tf_op jit(solution)/shard_map/ppermute | solution.py:806
  103.8 9.0 %collective-permute-start.16 = (bf16[128,768]{1,0:T(8,128)(2,1)S(1)}, bf16[128,768]{1,0:T(8,128)(2,1)S(1)}, u32[]{:S(2)}, u32[]{:S(2)}) collective-permute-start(bf16[128,768]{1,0:T(8,128)(2,1)S(1)} %get-tuple-element.102), channel_id=1, source_target_pairs={{0,16},{8,24},{16,0},{24,8},{1,17},{9,25},{17,1},{25,9},{2,18},{10... | collective-permute-start | bytes 589832 | tf_op jit(solution)/shard_map/ppermute | solution.py:806
  112.8 13.3 %copy-start.18 = (bf16[8,96,768]{2,1,0:T(8,128)(2,1)S(1)}, bf16[8,96,768]{2,1,0:T(8,128)(2,1)}, u32[]{:S(2)}) copy-start(bf16[8,96,768]{2,1,0:T(8,128)(2,1)} %copy-done.17) | copy-start | bytes 3538948
  112.8 13.3 %copy-start.40 = (f32[512,768]{1,0:T(8,128)S(1)}, f32[512,768]{1,0:T(8,128)}, u32[]{:S(2)}) copy-start(f32[512,768]{1,0:T(8,128)} %get-tuple-element.51) | copy-start | bytes 4718596
  114.9 12.1 %copy-start.22 = (bf16[4,8,24,768]{3,2,1,0:T(8,128)(2,1)S(1)}, bf16[4,8,24,768]{3,2,1,0:T(8,128)(2,1)}, u32[]{:S(2)}) copy-start(bf16[4,8,24,768]{3,2,1,0:T(8,128)(2,1)} %copy-done.21) | copy-start | bytes 3538948
  114.9 7.5 %collective-permute-start.20 = (bf16[128,768]{1,0:T(8,128)(2,1)S(1)}, bf16[128,768]{1,0:T(8,128)(2,1)S(1)}, u32[]{:S(2)}, u32[]{:S(2)}) collective-permute-start(bf16[128,768]{1,0:T(8,128)(2,1)S(1)} %get-tuple-element.82), channel_id=1, source_target_pairs={{0,24},{8,0},{16,8},{24,16},{1,25},{9,1},{17,9},{25,17},{2,26},{10... | collective-permute-start | bytes 589832 | tf_op jit(solution)/shard_map/ppermute | solution.py:806
  115.8 10.3 %collective-permute-start.19 = (bf16[128,768]{1,0:T(8,128)(2,1)S(1)}, bf16[128,768]{1,0:T(8,128)(2,1)S(1)}, u32[]{:S(2)}, u32[]{:S(2)}) collective-permute-start(bf16[128,768]{1,0:T(8,128)(2,1)S(1)} %get-tuple-element.82), channel_id=1, source_target_pairs={{0,16},{8,24},{16,0},{24,8},{1,17},{9,25},{17,1},{25,9},{2,18},{10... | collective-permute-start | bytes 589832 | tf_op jit(solution)/shard_map/ppermute | solution.py:806
  116.9 9.2 %collective-permute-start.18 = (bf16[128,768]{1,0:T(8,128)(2,1)S(1)}, bf16[128,768]{1,0:T(8,128)(2,1)S(1)}, u32[]{:S(2)}, u32[]{:S(2)}) collective-permute-start(bf16[128,768]{1,0:T(8,128)(2,1)S(1)} %get-tuple-element.82), channel_id=1, source_target_pairs={{0,8},{8,16},{16,24},{24,0},{1,9},{9,17},{17,25},{25,1},{2,10},{10... | collective-permute-start | bytes 589832 | tf_op jit(solution)/shard_map/ppermute | solution.py:806
  132.9 8.0 %collective-permute-start.23 = (bf16[128,768]{1,0:T(8,128)(2,1)S(1)}, bf16[128,768]{1,0:T(8,128)(2,1)S(1)}, u32[]{:S(2)}, u32[]{:S(2)}) collective-permute-start(bf16[128,768]{1,0:T(8,128)(2,1)S(1)} %get-tuple-element.98), channel_id=1, source_target_pairs={{0,8},{8,16},{16,24},{24,0},{1,9},{9,17},{17,25},{25,1},{2,10},{10... | collective-permute-start | bytes 589832 | tf_op jit(solution)/shard_map/ppermute | solution.py:806
  133.3 9.6 %collective-permute-start.22 = (bf16[128,768]{1,0:T(8,128)(2,1)S(1)}, bf16[128,768]{1,0:T(8,128)(2,1)S(1)}, u32[]{:S(2)}, u32[]{:S(2)}) collective-permute-start(bf16[128,768]{1,0:T(8,128)(2,1)S(1)} %get-tuple-element.99), channel_id=1, source_target_pairs={{0,16},{8,24},{16,0},{24,8},{1,17},{9,25},{17,1},{25,9},{2,18},{10... | collective-permute-start | bytes 589832 | tf_op jit(solution)/shard_map/ppermute | solution.py:806
  134.4 8.4 %collective-permute-start.21 = (bf16[128,768]{1,0:T(8,128)(2,1)S(1)}, bf16[128,768]{1,0:T(8,128)(2,1)}, u32[]{:S(2)}, u32[]{:S(2)}) collective-permute-start(bf16[128,768]{1,0:T(8,128)(2,1)S(1)} %get-tuple-element.97.refs_1_), channel_id=1, source_target_pairs={{0,24},{8,0},{16,8},{24,16},{1,25},{9,1},{17,9},{25,17},{2,26},{10... | collective-permute-start | bytes 589832 | tf_op jit(solution)/shard_map/ppermute | solution.py:806
  137.0 9.0 %copy-start.14 = (bf16[4,4,2,24,768]{4,3,2,1,0:T(8,128)(2,1)S(1)}, bf16[4,4,2,24,768]{4,3,2,1,0:T(8,128)(2,1)}, u32[]{:S(2)}) copy-start(bf16[4,4,2,24,768]{4,3,2,1,0:T(8,128)(2,1)} %copy-done.13) | copy-start | bytes 3538948
  150.6 5.3 %collective-permute-start.27 = (bf16[4,4,24,768]{3,2,1,0:T(8,128)(2,1)}, bf16[4,4,24,768]{3,2,1,0:T(8,128)(2,1)S(1)}, u32[]{:S(2)}, u32[]{:S(2)}) collective-permute-start(bf16[4,4,24,768]{3,2,1,0:T(8,128)(2,1)} %fusion.7), channel_id=1, source_target_pairs={{0,1},{1,0},{2,3},{3,2},{4,5},{5,4},{6,7},{7,6},{8,9},{9,8},{10,11... | collective-permute-start | bytes 1769480 | tf_op jit(solution)/shard_map/ppermute | solution.py:803
  150.6 12.7 %collective-permute-start.24 = (bf16[192,128]{1,0:T(8,128)(2,1)S(1)}, bf16[192,128]{1,0:T(8,128)(2,1)S(1)}, u32[]{:S(2)}, u32[]{:S(2)}) collective-permute-start(bf16[192,128]{1,0:T(8,128)(2,1)S(1)} %get-tuple-element.106.refs_1_), channel_id=1, source_target_pairs={{0,2},{1,3},{2,4},{3,5},{4,6},{5,7},{6,0},{7,1},{8,10},{9,11},{10,... | collective-permute-start | bytes 147464 | tf_op jit(solution)/shard_map/ppermute | solution.py:800
  151.9 9.9 %collective-permute-start.26 = (bf16[192,128]{1,0:T(8,128)(2,1)S(1)}, bf16[192,128]{1,0:T(8,128)(2,1)S(1)}, u32[]{:S(2)}, u32[]{:S(2)}) collective-permute-start(bf16[192,128]{1,0:T(8,128)(2,1)S(1)} %get-tuple-element.104), channel_id=1, source_target_pairs={{0,6},{1,7},{2,0},{3,1},{4,2},{5,3},{6,4},{7,5},{8,14},{9,15},{10,... | collective-permute-start | bytes 147464 | tf_op jit(solution)/shard_map/ppermute | solution.py:800
  154.4 8.9 %copy-start.9 = (bf16[1024,256]{1,0:T(8,128)(2,1)S(1)}, bf16[1024,256]{1,0:T(8,128)(2,1)}, u32[]{:S(2)}) copy-start(bf16[1024,256]{1,0:T(8,128)(2,1)} %get-tuple-element.54.refs_2_) | copy-start | bytes 1572868
  154.5 8.9 %copy-start.10 = (bf16[1024,192]{1,0:T(8,128)(2,1)S(1)}, bf16[1024,192]{1,0:T(8,128)(2,1)}, u32[]{:S(2)}) copy-start(bf16[1024,192]{1,0:T(8,128)(2,1)} %get-tuple-element.55.refs_3_) | copy-start | bytes 1179652
  154.5 8.9 %copy-start.11 = (f32[192,512]{1,0:T(8,128)S(1)}, f32[192,512]{1,0:T(8,128)}, u32[]{:S(2)}) copy-start(f32[192,512]{1,0:T(8,128)} %get-tuple-element.56.refs_4_) | copy-start | bytes 1179652
  154.5 8.9 %collective-permute-start.25 = (bf16[192,128]{1,0:T(8,128)(2,1)S(1)}, bf16[192,128]{1,0:T(8,128)(2,1)S(1)}, u32[]{:S(2)}, u32[]{:S(2)}) collective-permute-start(bf16[192,128]{1,0:T(8,128)(2,1)S(1)} %get-tuple-element.105), channel_id=1, source_target_pairs={{0,4},{1,5},{2,6},{3,7},{4,0},{5,1},{6,2},{7,3},{8,12},{9,13},{10,... | collective-permute-start | bytes 147464 | tf_op jit(solution)/shard_map/ppermute | solution.py:800
  158.1 15.7 %all-to-all-start.3 = ((bf16[4,4,24,768]{3,2,1,0:T(8,128)(2,1)}), bf16[4,4,24,768]{3,2,1,0:T(8,128)(2,1)S(1)}, u32[]{:S(2)}, u32[]{:S(2)}) async-start(bf16[4,4,24,768]{3,2,1,0:T(8,128)(2,1)} %fusion.5.refs_10_), calls=%async_computation.3 | async-start | bytes 1179648 | tf_op jit(solution)/shard_map/all_to_all | solution.py:830
  171.1 2.7 %collective-permute-start.28 = (bf16[512,384]{1,0:T(8,128)(2,1)}, bf16[512,384]{1,0:T(8,128)(2,1)S(1)}, u32[]{:S(2)}, u32[]{:S(2)}) collective-permute-start(bf16[512,384]{1,0:T(8,128)(2,1)} %get-tuple-element.59), channel_id=1, source_target_pairs={{0,1},{1,0},{2,3},{3,2},{4,5},{5,4},{6,7},{7,6},{8,9},{9,8},{10,11... | collective-permute-start | bytes 1179656 | tf_op jit(solution)/shard_map/ppermute | solution.py:803
  180.2 6.2 %copy-start.1 = (f32[16,32,576]{2,1,0:T(8,128)S(1)}, f32[16,32,576]{2,1,0:T(8,128)}, u32[]{:S(2)}) copy-start(f32[16,32,576]{2,1,0:T(8,128)} %get-tuple-element.61.refs_1_) | copy-start | bytes 3538948
  180.2 24.7 %all-to-all-start.4 = ((bf16[4,128,768]{2,1,0:T(8,128)(2,1)}), bf16[4,128,768]{2,1,0:T(8,128)(2,1)S(1)}, u32[]{:S(2)}, u32[]{:S(2)}) async-start(bf16[4,128,768]{2,1,0:T(8,128)(2,1)} %get-tuple-element.60), calls=%async_computation.4 | async-start | bytes 1572864 | tf_op jit(solution)/shard_map/all_to_all | solution.py:827
  184.1 2.3 collective-permute-start.29
  188.0 16.9 %collective-permute-start.30 = (bf16[152,768]{1,0:T(8,128)(2,1)}, bf16[152,768]{1,0:T(8,128)(2,1)S(1)}, u32[]{:S(2)}, u32[]{:S(2)}) collective-permute-start(bf16[152,768]{1,0:T(8,128)(2,1)} %get-tuple-element.63), channel_id=1, source_target_pairs={{0,8},{8,16},{16,24},{24,0},{1,9},{9,17},{17,25},{25,1},{2,10},{10... | collective-permute-start | bytes 700424 | tf_op jit(solution)/shard_map/ppermute | solution.py:806
  190.6 14.4 %collective-permute-start.31 = (bf16[152,768]{1,0:T(8,128)(2,1)}, bf16[152,768]{1,0:T(8,128)(2,1)S(1)}, u32[]{:S(2)}, u32[]{:S(2)}) collective-permute-start(bf16[152,768]{1,0:T(8,128)(2,1)} %get-tuple-element.64), channel_id=1, source_target_pairs={{0,16},{8,24},{16,0},{24,8},{1,17},{9,25},{17,1},{25,9},{2,18},{10... | collective-permute-start | bytes 700424 | tf_op jit(solution)/shard_map/ppermute | solution.py:806
  190.7 14.3 %collective-permute-start.32 = (bf16[152,768]{1,0:T(8,128)(2,1)}, bf16[152,768]{1,0:T(8,128)(2,1)S(1)}, u32[]{:S(2)}, u32[]{:S(2)}) collective-permute-start(bf16[152,768]{1,0:T(8,128)(2,1)} %get-tuple-element.65), channel_id=1, source_target_pairs={{0,24},{8,0},{16,8},{24,16},{1,25},{9,1},{17,9},{25,17},{2,26},{10... | collective-permute-start | bytes 700424 | tf_op jit(solution)/shard_map/ppermute | solution.py:806
  192.2 12.9 %copy-start.20 = (f32[128,768]{1,0:T(8,128)S(1)}, f32[128,768]{1,0:T(8,128)}, u32[]{:S(2)}) copy-start(f32[128,768]{1,0:T(8,128)} %get-tuple-element.85) | copy-start | bytes 1179652
  206.8 4.5 %copy-start.2 = (bf16[1,192,768]{2,1,0:T(8,128)(2,1)S(1)}, bf16[1,192,768]{2,1,0:T(8,128)(2,1)}, u32[]{:S(2)}) copy-start(bf16[1,192,768]{2,1,0:T(8,128)(2,1)} %reduce-scatter.2.cloned.1.call-done) | copy-start | bytes 884740
  206.8 14.1 %all-to-all-start.5 = ((bf16[4,56,768]{2,1,0:T(8,128)(2,1)}), bf16[4,56,768]{2,1,0:T(8,128)(2,1)S(1)}, u32[]{:S(2)}, u32[]{:S(2)}) async-start(bf16[4,56,768]{2,1,0:T(8,128)(2,1)} %after.16), calls=%async_computation.6 | async-start | bytes 688128 | tf_op jit(solution)/shard_map/all_to_all | solution.py:827
  (18 other events, 24.4 us)
Sparse Core Ops, SparseCore 0:
  47.7 36.8 all-gather.2
  133.0 37.9 reduce-scatter.1

commit v4 on v3

--- a/solution.py
+++ b/solution.py
@@ -956,7 +956,7 @@
     mixed_grad_t = dot(out_full, proj_grad, ((1,), (1,))).astype(low)
     mixed_grad_t = mixed_grad_t.reshape(chips, group, rows)
     leaving = [pick(mixed_grad_t, (chip + d) % chips) for d in range(chips)]
-    grad_out_w = dot(mixed_t, after(proj_grad, leaving[1]))
+    grad_out_w = dot(mixed_t, after(proj_grad, leaving[1])).astype(low)
     out_sum = cores_sum(grad_out_w.reshape(teams, chips, 2, part, width), 2).astype(low)
 
     come = [leaving[0]] + [to_chip(leaving[d], d) for d in range(1, chips)]

time: 234 us -> 233 us (level)
  transfers between devices with their start and end apart: 41 -> 41, of which waited for: 18 -> 18; matrix products, arithmetic and copies ran while one was open for 11% -> 10% of each run, Pallas kernels for 11% -> 11%
where the time goes in v4:
time: 233 us; the launch traced here: 232 us
  waiting for transfers between devices  83.2 us (36%)
  starting transfers between devices  56 us (24%)
  Pallas kernels  28.2 us (12%)
  local copies, waits for them, and re-layouts  22.2 us (10%)
  other arithmetic  16 us (7%)
  between operations  15.8 us (7%)
  matrix products  10.4 us (4%)
    ppermute x15, waiting for transfers between devices, to_team(): lax.ppermute(block, 'batch', [(i, (i + distance) % teams) for i in range(...  30 us
    all_to_all x3, waiting for transfers between devices, trade_chips(): return lax.all_to_all(blocks, 'ctx', 0, 0, axis_index_groups=same_core)  27.8 us
    pallas_call x5, Pallas kernels, one_step(): pl.pallas_call(functools.partial(copied_kernel, kernel, first, far, len(o...  23 us
    ppermute x9, waiting for transfers between devices, to_chip(): return lax.ppermute(block, 'ctx', route)  20.7 us
    ppermute x15, starting transfers between devices, to_team(): lax.ppermute(block, 'batch', [(i, (i + distance) % teams) for i in range(...  17.7 us
    all_to_all x3, starting transfers between devices, trade_chips(): return lax.all_to_all(blocks, 'ctx', 0, 0, axis_index_groups=same_core)  13.7 us
    ppermute x9, starting transfers between devices, to_chip(): return lax.ppermute(block, 'ctx', route)  12.5 us
    all_to_all x3, starting transfers between devices, trade_teams(): return lax.all_to_all(blocks, 'batch', 0, 0)  10.8 us
  transfers between devices with their start and end apart: 41, of which 18 were waited for; matrix products, arithmetic and copies ran while one was open for 10% of the time, Pallas kernels for 11%

profile of v4, /device:TPU:0, one launch (start us, length us, event | category | flops | bytes accessed | tf_op | source)
XLA Modules:
  0.0 231.8 jit_solution(3660900010511194943)
XLA Ops:
  7.2 1.4 stack.117.vectors
  8.6 1.6 pack.1
  10.1 6.3 %all-to-all-start = ((bf16[4,32,768]{2,1,0:T(8,128)(2,1)}), bf16[4,32,768]{2,1,0:T(8,128)(2,1)S(1)}, u32[]{:S(2)}, u32[]{:S(2)}) async-start(bf16[4,32,768]{2,1,0:T(8,128)(2,1)} %pack.1), calls=%async_computation | async-start | bytes 393216 | tf_op jit(solution)/shard_map/all_to_all | solution.py:827
  16.5 1.6 lay.1.refs_0_
  18.1 5.9 %all-to-all-done.refs_1_.packed = bf16[4,32,768]{2,1,0:T(8,128)(2,1)S(1)} async-done(((bf16[4,32,768]{2,1,0:T(8,128)(2,1)}), bf16[4,32,768]{2,1,0:T(8,128)(2,1)S(1)}, u32[]{:S(2)}, u32[]{:S(2)}) %all-to-all-start) | async-done | bytes 196640 | tf_op jit(solution)/shard_map/all_to_all | solution.py:827
  24.0 1.4 collective-permute-start.2
  26.9 2.0 share.1
  28.9 3.7 %all-to-all-start.1 = ((bf16[4,152,768]{2,1,0:T(8,128)(2,1)}), bf16[4,152,768]{2,1,0:T(8,128)(2,1)S(1)}, u32[]{:S(2)}, u32[]{:S(2)}) async-start(bf16[4,152,768]{2,1,0:T(8,128)(2,1)} %share.1), calls=%async_computation.1 | async-start | bytes 1867776 | tf_op jit(solution)/shard_map/all_to_all | solution.py:830
  32.7 12.4 %collective-permute-done.1.refs_3_ = bf16[152,768]{1,0:T(8,128)(2,1)S(1)} collective-permute-done((bf16[152,768]{1,0:T(8,128)(2,1)}, bf16[152,768]{1,0:T(8,128)(2,1)S(1)}, u32[]{:S(2)}, u32[]{:S(2)}) %collective-permute-start.1) | collective-permute-done | bytes 233504 | tf_op jit(solution)/shard_map/ppermute | solution.py:800
  45.7 1.0 slice.182
  47.5 1.8 collective-permute-done.7
  49.3 1.5 select_bitcast_fusion.1
  52.3 1.3 fusion.6
  53.6 9.4 %attend.1 = (bf16[512,768]{1,0:T(8,128)(2,1)}, bf16[512,192]{1,0:T(8,128)(2,1)}, bf16[1024,256]{1,0:T(8,128)(2,1)}, bf16[1024,192]{1,0:T(8,128)(2,1)}, f32[192,5...) custom-call(s32[9]{0:T(128)S(1)} %pad_add_fusion.refs_0_, ...), custom_call_target="tpu_custom_call" | custom-call | flops 2516582400 | bytes 2680356 | tf_op jit(solution)/shard_map/attend/pallas_call | solution.py:376
  63.0 1.5 collective-permute-start.8
  65.8 3.5 %all-to-all-start.2 = ((bf16[4,4,24,768]{3,2,1,0:T(8,128)(2,1)}), bf16[4,4,24,768]{3,2,1,0:T(8,128)(2,1)S(1)}, u32[]{:S(2)}, u32[]{:S(2)}) async-start(bf16[4,4,24,768]{3,2,1,0:T(8,128)(2,1)} %broadcast_in_dim.12), calls=%async_computation.2 | async-start | bytes 1179648 | tf_op jit(solution)/shard_map/all_to_all | solution.py:830
  69.3 1.6 collective-permute-start.9
  70.9 2.0 collective-permute-start.10
  73.0 6.3 %collective-permute-done.9 = bf16[192,128]{1,0:T(8,128)(2,1)S(1)} collective-permute-done((bf16[192,128]{1,0:T(8,128)(2,1)S(1)}, bf16[192,128]{1,0:T(8,128)(2,1)S(1)}, u32[]{:S(2)}, u32[]{:S(2)}) %collective-permute-start.9) | collective-permute-done | bytes 49184 | tf_op jit(solution)/shard_map/ppermute | solution.py:800
  79.6 1.9 collective-permute-done.11
  83.2 2.8 %collective-permute-start.14 = (bf16[128,768]{1,0:T(8,128)(2,1)S(1)}, bf16[128,768]{1,0:T(8,128)(2,1)S(1)}, u32[]{:S(2)}, u32[]{:S(2)}) collective-permute-start(bf16[128,768]{1,0:T(8,128)(2,1)S(1)} %fusion.18), channel_id=1, source_target_pairs={{0,24},{8,0},{16,8},{24,16},{1,25},{9,1},{17,9},{25,17},{2,26},{10... | collective-permute-start | bytes 589832 | tf_op jit(solution)/shard_map/ppermute | solution.py:806
  87.1 1.8 fusion.28
  89.0 2.3 collective-permute-done.14
  91.3 5.6 %collective-permute-done.13 = bf16[128,768]{1,0:T(8,128)(2,1)S(1)} collective-permute-done((bf16[128,768]{1,0:T(8,128)(2,1)S(1)}, bf16[128,768]{1,0:T(8,128)(2,1)S(1)}, u32[]{:S(2)}, u32[]{:S(2)}) %collective-permute-start.13) | collective-permute-done | bytes 196640 | tf_op jit(solution)/shard_map/ppermute | solution.py:806
  96.9 2.8 %fusion.3 = (f32[512,768]{1,0:T(8,128)}, bf16[512,768]{1,0:T(8,128)(2,1)S(1)}) fusion(f32[768]{0:T(1024)S(1)} %dynamic_slice.48, bf16[768,768]{1,0:T(8,128)(2,1)S(1)} %bitcast.168, bf16[128,768]{1,0:T(8,128)(2,1)S(1)} %collective-permute-done.14, bf16[128,768]{1,0:T(8,128)(2,1)S(1)} %collective-permute-done.13, ...), kind=kOutput, calls=%fused_computation.5 | convolution fusion | flops 611450880 | bytes 4328448 | tf_op jit(solution)/shard_map/dot_general | solution.py:317
  99.7 1.9 fusion.34
  102.4 1.5 collective-permute-start.17
  104.5 4.3 %collective-permute-done.15 = bf16[128,768]{1,0:T(8,128)(2,1)S(1)} collective-permute-done((bf16[128,768]{1,0:T(8,128)(2,1)S(1)}, bf16[128,768]{1,0:T(8,128)(2,1)S(1)}, u32[]{:S(2)}, u32[]{:S(2)}) %collective-permute-start.15) | collective-permute-done | bytes 196640 | tf_op jit(solution)/shard_map/ppermute | solution.py:806
  108.8 3.1 %collective-permute-done.17 = bf16[128,768]{1,0:T(8,128)(2,1)S(1)} collective-permute-done((bf16[128,768]{1,0:T(8,128)(2,1)S(1)}, bf16[128,768]{1,0:T(8,128)(2,1)S(1)}, u32[]{:S(2)}, u32[]{:S(2)}) %collective-permute-start.17) | collective-permute-done | bytes 196640 | tf_op jit(solution)/shard_map/ppermute | solution.py:806
  112.8 1.4 fusion.26
  115.8 1.1 collective-permute-start.19
  116.9 1.1 collective-permute-start.18
  118.0 4.4 %collective-permute-done.20 = bf16[128,768]{1,0:T(8,128)(2,1)S(1)} collective-permute-done((bf16[128,768]{1,0:T(8,128)(2,1)S(1)}, bf16[128,768]{1,0:T(8,128)(2,1)S(1)}, u32[]{:S(2)}, u32[]{:S(2)}) %collective-permute-start.20) | collective-permute-done | bytes 196640 | tf_op jit(solution)/shard_map/ppermute | solution.py:806
  122.4 3.7 %collective-permute-done.19 = bf16[128,768]{1,0:T(8,128)(2,1)S(1)} collective-permute-done((bf16[128,768]{1,0:T(8,128)(2,1)S(1)}, bf16[128,768]{1,0:T(8,128)(2,1)S(1)}, u32[]{:S(2)}, u32[]{:S(2)}) %collective-permute-start.19) | collective-permute-done | bytes 196640 | tf_op jit(solution)/shard_map/ppermute | solution.py:806
  131.3 1.6 pad_maximum_fusion
  133.3 1.2 collective-permute-start.22
  134.4 2.5 %collective-permute-start.21 = (bf16[128,768]{1,0:T(8,128)(2,1)S(1)}, bf16[128,768]{1,0:T(8,128)(2,1)}, u32[]{:S(2)}, u32[]{:S(2)}) collective-permute-start(bf16[128,768]{1,0:T(8,128)(2,1)S(1)} %get-tuple-element.97.refs_1_), channel_id=1, source_target_pairs={{0,24},{8,0},{16,8},{24,16},{1,25},{9,1},{17,9},{25,17},{2,26},{10... | collective-permute-start | bytes 589832 | tf_op jit(solution)/shard_map/ppermute | solution.py:806
  137.0 3.9 %collective-permute-done.23 = bf16[128,768]{1,0:T(8,128)(2,1)S(1)} collective-permute-done((bf16[128,768]{1,0:T(8,128)(2,1)S(1)}, bf16[128,768]{1,0:T(8,128)(2,1)S(1)}, u32[]{:S(2)}, u32[]{:S(2)}) %collective-permute-start.23) | collective-permute-done | bytes 196640 | tf_op jit(solution)/shard_map/ppermute | solution.py:806
  140.9 2.0 collective-permute-done.22
  142.9 2.2 multiply_reduce_fusion
  145.0 1.0 convert_reduce_fusion.4
  146.5 1.5 convolution_convert_fusion.2
  148.0 1.1 dynamic-slice_bitcast_fusion
  149.2 1.3 collective-permute-start.24
  150.6 2.6 %collective-permute-start.26 = (bf16[192,128]{1,0:T(8,128)(2,1)S(1)}, bf16[192,128]{1,0:T(8,128)(2,1)S(1)}, u32[]{:S(2)}, u32[]{:S(2)}) collective-permute-start(bf16[192,128]{1,0:T(8,128)(2,1)S(1)} %get-tuple-element.104), channel_id=1, source_target_pairs={{0,6},{1,7},{2,0},{3,1},{4,2},{5,3},{6,4},{7,5},{8,14},{9,15},{10,... | collective-permute-start | bytes 147464 | tf_op jit(solution)/shard_map/ppermute | solution.py:800
  153.1 1.5 collective-permute-start.25
  154.6 2.2 fusion.5.refs_10_
  156.8 3.6 %all-to-all-start.3 = ((bf16[4,4,24,768]{3,2,1,0:T(8,128)(2,1)}), bf16[4,4,24,768]{3,2,1,0:T(8,128)(2,1)S(1)}, u32[]{:S(2)}, u32[]{:S(2)}) async-start(bf16[4,4,24,768]{3,2,1,0:T(8,128)(2,1)} %fusion.5.refs_10_), calls=%async_computation.3 | async-start | bytes 1179648 | tf_op jit(solution)/shard_map/all_to_all | solution.py:830
  160.4 1.9 collective-permute-done.25.refs_8_
  163.3 6.8 %attend_back.1 = (bf16[512,192]{1,0:T(8,128)(2,1)}, f32[512,384]{1,0:T(8,128)}, bf16[512,384]{1,0:T(8,128)(2,1)}) custom-call(s32[9]{0:T(128)S(1)} %pad_add_fusion.refs_0_, bf16[512,192]{1,0:T(8,128)(2,1)S(1)} %copy-done.12, bf16[1024,256]{1,0:T(8,128)(2,1)S(1)} %copy-done.9, bf16[1024,192]{1,0:T(8,128)(2,1)S(1)} %copy-done.10, f32[192,512]{1,0:T(8,128)S(1)} %copy-done.11, ...), custom_call_target="tpu_custom_call" | custom-call | flops 4026531840 | bytes 2299940 | tf_op jit(solution)/shard_map/attend_back/pallas_call | solution.py:376
  172.9 1.1 copy-done.4
  174.0 0.9 copy-done.7
  175.0 4.3 %finish.1 = (bf16[4,128,768]{2,1,0:T(8,128)(2,1)}, f32[16,32,576]{2,1,0:T(8,128)}, bf16[16,32,576]{2,1,0:T(8,128)(2,1)}) custom-call(s32[2]{0:T(128)S(1)} %pad_add_fusion.1.refs_0_, bf16[512,768]{1,0:T(8,128)(2,1)S(1)} %copy-done.3, bf16[768,576]{1,0:T(8,128)(2,1)S(1)} %bitcast.156, bf16[512,192]{1,0:T(8,128)(2,1)S(1)} %copy-done.7, ...), custom_call_target="tpu_custom_call" | custom-call | flops 905969664 | bytes 4227080 | tf_op jit(solution)/shard_map/finish/pallas_call | solution.py:376
  179.3 3.8 %all-to-all-start.4 = ((bf16[4,128,768]{2,1,0:T(8,128)(2,1)}), bf16[4,128,768]{2,1,0:T(8,128)(2,1)S(1)}, u32[]{:S(2)}, u32[]{:S(2)}) async-start(bf16[4,128,768]{2,1,0:T(8,128)(2,1)} %get-tuple-element.60), calls=%async_computation.4 | async-start | bytes 1572864 | tf_op jit(solution)/shard_map/all_to_all | solution.py:827
  184.4 1.0 collective-permute-done.29.refs_2_
  185.4 1.5 bundle.1
  186.9 2.4 %collective-permute-start.30 = (bf16[152,768]{1,0:T(8,128)(2,1)}, bf16[152,768]{1,0:T(8,128)(2,1)S(1)}, u32[]{:S(2)}, u32[]{:S(2)}) collective-permute-start(bf16[152,768]{1,0:T(8,128)(2,1)} %get-tuple-element.63), channel_id=1, source_target_pairs={{0,8},{8,16},{16,24},{24,0},{1,9},{9,17},{17,25},{25,1},{2,10},{10... | collective-permute-start | bytes 700424 | tf_op jit(solution)/shard_map/ppermute | solution.py:806
  189.4 1.5 collective-permute-start.32
  191.0 12.9 %all-to-all-done.4.refs_0_ = bf16[4,128,768]{2,1,0:T(8,128)(2,1)S(1)} async-done(((bf16[4,128,768]{2,1,0:T(8,128)(2,1)}), bf16[4,128,768]{2,1,0:T(8,128)(2,1)S(1)}, u32[]{:S(2)}, u32[]{:S(2)}) %all-to-all-start.4) | async-done | bytes 786464 | tf_op jit(solution)/shard_map/all_to_all | solution.py:827
  205.8 3.6 %all-to-all-start.5 = ((bf16[4,56,768]{2,1,0:T(8,128)(2,1)}), bf16[4,56,768]{2,1,0:T(8,128)(2,1)S(1)}, u32[]{:S(2)}, u32[]{:S(2)}) async-start(bf16[4,56,768]{2,1,0:T(8,128)(2,1)} %after.16), calls=%async_computation.6 | async-start | bytes 688128 | tf_op jit(solution)/shard_map/all_to_all | solution.py:827
  211.0 9.0 %all-to-all-done.5.refs_0_ = bf16[4,56,768]{2,1,0:T(8,128)(2,1)S(1)} async-done(((bf16[4,56,768]{2,1,0:T(8,128)(2,1)}), bf16[4,56,768]{2,1,0:T(8,128)(2,1)S(1)}, u32[]{:S(2)}, u32[]{:S(2)}) %all-to-all-start.5) | async-done | bytes 344096 | tf_op jit(solution)/shard_map/all_to_all | solution.py:827
  220.0 1.0 unpack.1
  220.9 1.2 slice_bitcast_fusion.9
  222.1 1.4 slice_bitcast_fusion.6
  (237 shorter events, 27.9 us)
Async XLA Ops:
  10.1 13.8 %all-to-all-start = ((bf16[4,32,768]{2,1,0:T(8,128)(2,1)}), bf16[4,32,768]{2,1,0:T(8,128)(2,1)S(1)}, u32[]{:S(2)}, u32[]{:S(2)}) async-start(bf16[4,32,768]{2,1,0:T(8,128)(2,1)} %pack.1), calls=%async_computation | async-start | bytes 393216 | tf_op jit(solution)/shard_map/all_to_all | solution.py:827
  16.5 37.1 %collective-permute-start.3 = (bf16[128,768]{1,0:T(8,128)(2,1)}, bf16[128,768]{1,0:T(8,128)(2,1)S(1)}, u32[]{:S(2)}, u32[]{:S(2)}) collective-permute-start(bf16[128,768]{1,0:T(8,128)(2,1)} %refs_1_.1), channel_id=1, source_target_pairs={{0,1},{1,0},{2,3},{3,2},{4,5},{5,4},{6,7},{7,6},{8,9},{9,8},{10,11... | collective-permute-start | bytes 589832 | tf_op jit(solution)/shard_map/ppermute | solution.py:803
  24.0 2.9 %copy-start = (bf16[4,32,768]{2,1,0:T(8,128)(2,1)}, bf16[4,32,768]{2,1,0:T(8,128)(2,1)S(1)}, u32[]{:S(2)}) copy-start(bf16[4,32,768]{2,1,0:T(8,128)(2,1)S(1)} %all-to-all-done.refs_1_.packed) | copy-start | bytes 589828
  24.0 8.7 %collective-permute-start.2 = (bf16[152,768]{1,0:T(8,128)(2,1)}, bf16[152,768]{1,0:T(8,128)(2,1)S(1)}, u32[]{:S(2)}, u32[]{:S(2)}) collective-permute-start(bf16[152,768]{1,0:T(8,128)(2,1)} %after.9), channel_id=1, source_target_pairs={{0,6},{1,7},{2,0},{3,1},{4,2},{5,3},{6,4},{7,5},{8,14},{9,15},{10,... | collective-permute-start | bytes 700424 | tf_op jit(solution)/shard_map/ppermute | solution.py:800
  26.1 19.0 %collective-permute-start.1 = (bf16[152,768]{1,0:T(8,128)(2,1)}, bf16[152,768]{1,0:T(8,128)(2,1)S(1)}, u32[]{:S(2)}, u32[]{:S(2)}) collective-permute-start(bf16[152,768]{1,0:T(8,128)(2,1)} %after.9), channel_id=1, source_target_pairs={{0,4},{1,5},{2,6},{3,7},{4,0},{5,1},{6,2},{7,3},{8,12},{9,13},{10,... | collective-permute-start | bytes 700424 | tf_op jit(solution)/shard_map/ppermute | solution.py:800
  26.7 18.5 %collective-permute-start = (bf16[152,768]{1,0:T(8,128)(2,1)}, bf16[152,768]{1,0:T(8,128)(2,1)S(1)}, u32[]{:S(2)}, u32[]{:S(2)}) collective-permute-start(bf16[152,768]{1,0:T(8,128)(2,1)} %after.9), channel_id=1, source_target_pairs={{0,2},{1,3},{2,4},{3,5},{4,6},{5,7},{6,0},{7,1},{8,10},{9,11},{10,... | collective-permute-start | bytes 700424 | tf_op jit(solution)/shard_map/ppermute | solution.py:800
  26.9 18.8 %copy-start.29 = (bf16[24,768]{1,0:T(8,128)(2,1)S(1)}, bf16[24,768]{1,0:T(8,128)(2,1)}, u32[]{:S(2)}) copy-start(bf16[24,768]{1,0:T(8,128)(2,1)} %w_out.1) | copy-start | bytes 110596
  28.9 16.8 %all-to-all-start.1 = ((bf16[4,152,768]{2,1,0:T(8,128)(2,1)}), bf16[4,152,768]{2,1,0:T(8,128)(2,1)S(1)}, u32[]{:S(2)}, u32[]{:S(2)}) async-start(bf16[4,152,768]{2,1,0:T(8,128)(2,1)} %share.1), calls=%async_computation.1 | async-start | bytes 1867776 | tf_op jit(solution)/shard_map/all_to_all | solution.py:830
  32.6 14.1 %copy-start.30 = (bf16[96,768]{1,0:T(8,128)(2,1)S(1)}, bf16[96,768]{1,0:T(8,128)(2,1)}, u32[]{:S(2)}) copy-start(bf16[96,768]{1,0:T(8,128)(2,1)} %param.31) | copy-start | bytes 442372
  32.6 54.5 %all-gather.3.cloned.1.call-start = ((), (), s32[]{:S(2)}) async-start(), calls=%async_computation.8 | async-start | bytes 2654208 | tf_op jit(solution)/shard_map/all_gather | solution.py:897
  32.6 20.9 %collective-permute-start.6 = (bf16[152,768]{1,0:T(8,128)(2,1)S(1)}, bf16[152,768]{1,0:T(8,128)(2,1)S(1)}, u32[]{:S(2)}, u32[]{:S(2)}) collective-permute-start(bf16[152,768]{1,0:T(8,128)(2,1)S(1)} %collective-permute-done.2.refs_4_), channel_id=1, source_target_pairs={{0,1},{1,0},{2,3},{3,2},{4,5},{5,4},{6,7},{7,6},{8,9},{9,8},{10,11... | collective-permute-start | bytes 700424 | tf_op jit(solution)/shard_map/ppermute | solution.py:803
  45.2 8.4 %collective-permute-start.5 = (bf16[152,768]{1,0:T(8,128)(2,1)S(1)}, bf16[152,768]{1,0:T(8,128)(2,1)S(1)}, u32[]{:S(2)}, u32[]{:S(2)}) collective-permute-start(bf16[152,768]{1,0:T(8,128)(2,1)S(1)} %collective-permute-done.1.refs_3_), channel_id=1, source_target_pairs={{0,1},{1,0},{2,3},{3,2},{4,5},{5,4},{6,7},{7,6},{8,9},{9,8},{10,11... | collective-permute-start | bytes 700424 | tf_op jit(solution)/shard_map/ppermute | solution.py:803
  45.2 8.4 %collective-permute-start.4 = (bf16[152,768]{1,0:T(8,128)(2,1)S(1)}, bf16[152,768]{1,0:T(8,128)(2,1)S(1)}, u32[]{:S(2)}, u32[]{:S(2)}) collective-permute-start(bf16[152,768]{1,0:T(8,128)(2,1)S(1)} %collective-permute-done.refs_2_), channel_id=1, source_target_pairs={{0,1},{1,0},{2,3},{3,2},{4,5},{5,4},{6,7},{7,6},{8,9},{9,8},{10,11... | collective-permute-start | bytes 700424 | tf_op jit(solution)/shard_map/ppermute | solution.py:803
  46.7 2.6 %collective-permute-start.7 = (bf16[4,4,32,768]{3,2,1,0:T(8,128)(2,1)}, bf16[4,4,32,768]{3,2,1,0:T(8,128)(2,1)}, u32[]{:S(2)}, u32[]{:S(2)}) collective-permute-start(bf16[4,4,32,768]{3,2,1,0:T(8,128)(2,1)} %bitcast.11), channel_id=1, source_target_pairs={{0,1},{1,0},{2,3},{3,2},{4,5},{5,4},{6,7},{7,6},{8,9},{9,8},{10,11... | collective-permute-start | bytes 2359304 | tf_op jit(solution)/shard_map/ppermute | solution.py:803
  63.0 10.0 %collective-permute-start.8 = (bf16[192,128]{1,0:T(8,128)(2,1)}, bf16[192,128]{1,0:T(8,128)(2,1)S(1)}, u32[]{:S(2)}, u32[]{:S(2)}) collective-permute-start(bf16[192,128]{1,0:T(8,128)(2,1)} %get-tuple-element.45), channel_id=1, source_target_pairs={{0,6},{1,7},{2,0},{3,1},{4,2},{5,3},{6,4},{7,5},{8,14},{9,15},{10,... | collective-permute-start | bytes 147464 | tf_op jit(solution)/shard_map/ppermute | solution.py:800
  64.5 4.8 %copy-start.39 = (bf16[192,128]{1,0:T(8,128)(2,1)S(1)}, bf16[192,128]{1,0:T(8,128)(2,1)}, u32[]{:S(2)}) copy-start(bf16[192,128]{1,0:T(8,128)(2,1)} %get-tuple-element.46) | copy-start | bytes 147460
  64.5 6.4 %copy-start.38 = (bf16[192,128]{1,0:T(8,128)(2,1)S(1)}, bf16[192,128]{1,0:T(8,128)(2,1)}, u32[]{:S(2)}) copy-start(bf16[192,128]{1,0:T(8,128)(2,1)} %get-tuple-element.47) | copy-start | bytes 147460
  64.6 14.8 %copy-start.31 = (bf16[192,128]{1,0:T(8,128)(2,1)S(1)}, bf16[192,128]{1,0:T(8,128)(2,1)}, u32[]{:S(2)}) copy-start(bf16[192,128]{1,0:T(8,128)(2,1)} %get-tuple-element.48) | copy-start | bytes 147460
  64.6 14.8 %copy-start.8 = (f32[3,512]{1,0:T(4,128)S(1)}, f32[3,512]{1,0:T(4,128)}, u32[]{:S(2)}) copy-start(f32[3,512]{1,0:T(4,128)} %get-tuple-element.49.refs_1_.refs_5_) | copy-start | bytes 18436
  65.8 13.6 %all-to-all-start.2 = ((bf16[4,4,24,768]{3,2,1,0:T(8,128)(2,1)}), bf16[4,4,24,768]{3,2,1,0:T(8,128)(2,1)S(1)}, u32[]{:S(2)}, u32[]{:S(2)}) async-start(bf16[4,4,24,768]{3,2,1,0:T(8,128)(2,1)} %broadcast_in_dim.12), calls=%async_computation.2 | async-start | bytes 1179648 | tf_op jit(solution)/shard_map/all_to_all | solution.py:830
  69.3 114.2 %reduce-scatter.2.cloned.1.call-start = ((), (), s32[]{:S(2)}) async-start(), calls=%async_computation.7 | async-start | bytes 2654208 | tf_op jit(solution)/shard_map/reduce_scatter | solution.py:969
  69.3 10.0 %collective-permute-start.9 = (bf16[192,128]{1,0:T(8,128)(2,1)S(1)}, bf16[192,128]{1,0:T(8,128)(2,1)S(1)}, u32[]{:S(2)}, u32[]{:S(2)}) collective-permute-start(bf16[192,128]{1,0:T(8,128)(2,1)S(1)} %copy-done.39), channel_id=1, source_target_pairs={{0,4},{1,5},{2,6},{3,7},{4,0},{5,1},{6,2},{7,3},{8,12},{9,13},{10,... | collective-permute-start | bytes 147464 | tf_op jit(solution)/shard_map/ppermute | solution.py:800
  70.9 8.4 %collective-permute-start.10 = (bf16[192,128]{1,0:T(8,128)(2,1)S(1)}, bf16[192,128]{1,0:T(8,128)(2,1)S(1)}, u32[]{:S(2)}, u32[]{:S(2)}) collective-permute-start(bf16[192,128]{1,0:T(8,128)(2,1)S(1)} %copy-done.38), channel_id=1, source_target_pairs={{0,2},{1,3},{2,4},{3,5},{4,6},{5,7},{6,0},{7,1},{8,10},{9,11},{10,... | collective-permute-start | bytes 147464 | tf_op jit(solution)/shard_map/ppermute | solution.py:800
  79.4 2.1 collective-permute-start.11
  83.2 13.7 %copy-start.27 = (bf16[128,768]{1,0:T(8,128)(2,1)}, bf16[128,768]{1,0:T(8,128)(2,1)S(1)}, u32[]{:S(2)}) copy-start(bf16[128,768]{1,0:T(8,128)(2,1)S(1)} %fusion.18) | copy-start | bytes 589828
  83.2 8.1 %collective-permute-start.14 = (bf16[128,768]{1,0:T(8,128)(2,1)S(1)}, bf16[128,768]{1,0:T(8,128)(2,1)S(1)}, u32[]{:S(2)}, u32[]{:S(2)}) collective-permute-start(bf16[128,768]{1,0:T(8,128)(2,1)S(1)} %fusion.18), channel_id=1, source_target_pairs={{0,24},{8,0},{16,8},{24,16},{1,25},{9,1},{17,9},{25,17},{2,26},{10... | collective-permute-start | bytes 589832 | tf_op jit(solution)/shard_map/ppermute | solution.py:806
  86.0 10.9 %collective-permute-start.13 = (bf16[128,768]{1,0:T(8,128)(2,1)S(1)}, bf16[128,768]{1,0:T(8,128)(2,1)S(1)}, u32[]{:S(2)}, u32[]{:S(2)}) collective-permute-start(bf16[128,768]{1,0:T(8,128)(2,1)S(1)} %fusion.18), channel_id=1, source_target_pairs={{0,16},{8,24},{16,0},{24,8},{1,17},{9,25},{17,1},{25,9},{2,18},{10... | collective-permute-start | bytes 589832 | tf_op jit(solution)/shard_map/ppermute | solution.py:806
  86.6 10.3 %collective-permute-start.12 = (bf16[128,768]{1,0:T(8,128)(2,1)S(1)}, bf16[128,768]{1,0:T(8,128)(2,1)S(1)}, u32[]{:S(2)}, u32[]{:S(2)}) collective-permute-start(bf16[128,768]{1,0:T(8,128)(2,1)S(1)} %fusion.18), channel_id=1, source_target_pairs={{0,8},{8,16},{16,24},{24,0},{1,9},{9,17},{17,25},{25,1},{2,10},{10... | collective-permute-start | bytes 589832 | tf_op jit(solution)/shard_map/ppermute | solution.py:806
  88.9 10.8 %copy-start.17 = (bf16[8,96,768]{2,1,0:T(8,128)(2,1)}, bf16[8,96,768]{2,1,0:T(8,128)(2,1)S(1)}, u32[]{:S(2)}) copy-start(bf16[8,96,768]{2,1,0:T(8,128)(2,1)S(1)} %get-tuple-element.89) | copy-start | bytes 3538948
  89.0 10.7 %copy-start.21 = (bf16[4,8,24,768]{3,2,1,0:T(8,128)(2,1)}, bf16[4,8,24,768]{3,2,1,0:T(8,128)(2,1)S(1)}, u32[]{:S(2)}) copy-start(bf16[4,8,24,768]{3,2,1,0:T(8,128)(2,1)S(1)} %copy.56) | copy-start | bytes 3538948
  91.3 8.4 %copy-start.32 = (bf16[128,768]{1,0:T(8,128)(2,1)}, bf16[128,768]{1,0:T(8,128)(2,1)S(1)}, u32[]{:S(2)}) copy-start(bf16[128,768]{1,0:T(8,128)(2,1)S(1)} %collective-permute-done.14) | copy-start | bytes 589828
  96.9 2.8 %copy-start.34 = (bf16[128,768]{1,0:T(8,128)(2,1)}, bf16[128,768]{1,0:T(8,128)(2,1)S(1)}, u32[]{:S(2)}) copy-start(bf16[128,768]{1,0:T(8,128)(2,1)S(1)} %collective-permute-done.13) | copy-start | bytes 589828
  101.7 12.7 %copy-start.19 = (bf16[128,768]{1,0:T(8,128)(2,1)S(1)}, bf16[128,768]{1,0:T(8,128)(2,1)}, u32[]{:S(2)}) copy-start(bf16[128,768]{1,0:T(8,128)(2,1)} %param.35) | copy-start | bytes 589828
  101.7 7.1 %collective-permute-start.15 = (bf16[128,768]{1,0:T(8,128)(2,1)S(1)}, bf16[128,768]{1,0:T(8,128)(2,1)S(1)}, u32[]{:S(2)}, u32[]{:S(2)}) collective-permute-start(bf16[128,768]{1,0:T(8,128)(2,1)S(1)} %get-tuple-element.100), channel_id=1, source_target_pairs={{0,24},{8,0},{16,8},{24,16},{1,25},{9,1},{17,9},{25,17},{2,26},{10... | collective-permute-start | bytes 589832 | tf_op jit(solution)/shard_map/ppermute | solution.py:806
  102.4 9.5 %collective-permute-start.17 = (bf16[128,768]{1,0:T(8,128)(2,1)S(1)}, bf16[128,768]{1,0:T(8,128)(2,1)S(1)}, u32[]{:S(2)}, u32[]{:S(2)}) collective-permute-start(bf16[128,768]{1,0:T(8,128)(2,1)S(1)} %get-tuple-element.101), channel_id=1, source_target_pairs={{0,8},{8,16},{16,24},{24,0},{1,9},{9,17},{17,25},{25,1},{2,10},{10... | collective-permute-start | bytes 589832 | tf_op jit(solution)/shard_map/ppermute | solution.py:806
  103.8 9.0 %collective-permute-start.16 = (bf16[128,768]{1,0:T(8,128)(2,1)S(1)}, bf16[128,768]{1,0:T(8,128)(2,1)S(1)}, u32[]{:S(2)}, u32[]{:S(2)}) collective-permute-start(bf16[128,768]{1,0:T(8,128)(2,1)S(1)} %get-tuple-element.102), channel_id=1, source_target_pairs={{0,16},{8,24},{16,0},{24,8},{1,17},{9,25},{17,1},{25,9},{2,18},{10... | collective-permute-start | bytes 589832 | tf_op jit(solution)/shard_map/ppermute | solution.py:806
  112.8 13.3 %copy-start.18 = (bf16[8,96,768]{2,1,0:T(8,128)(2,1)S(1)}, bf16[8,96,768]{2,1,0:T(8,128)(2,1)}, u32[]{:S(2)}) copy-start(bf16[8,96,768]{2,1,0:T(8,128)(2,1)} %copy-done.17) | copy-start | bytes 3538948
  112.8 13.3 %copy-start.40 = (f32[512,768]{1,0:T(8,128)S(1)}, f32[512,768]{1,0:T(8,128)}, u32[]{:S(2)}) copy-start(f32[512,768]{1,0:T(8,128)} %get-tuple-element.51) | copy-start | bytes 4718596
  114.9 12.1 %copy-start.22 = (bf16[4,8,24,768]{3,2,1,0:T(8,128)(2,1)S(1)}, bf16[4,8,24,768]{3,2,1,0:T(8,128)(2,1)}, u32[]{:S(2)}) copy-start(bf16[4,8,24,768]{3,2,1,0:T(8,128)(2,1)} %copy-done.21) | copy-start | bytes 3538948
  114.9 7.5 %collective-permute-start.20 = (bf16[128,768]{1,0:T(8,128)(2,1)S(1)}, bf16[128,768]{1,0:T(8,128)(2,1)S(1)}, u32[]{:S(2)}, u32[]{:S(2)}) collective-permute-start(bf16[128,768]{1,0:T(8,128)(2,1)S(1)} %get-tuple-element.82), channel_id=1, source_target_pairs={{0,24},{8,0},{16,8},{24,16},{1,25},{9,1},{17,9},{25,17},{2,26},{10... | collective-permute-start | bytes 589832 | tf_op jit(solution)/shard_map/ppermute | solution.py:806
  115.8 10.3 %collective-permute-start.19 = (bf16[128,768]{1,0:T(8,128)(2,1)S(1)}, bf16[128,768]{1,0:T(8,128)(2,1)S(1)}, u32[]{:S(2)}, u32[]{:S(2)}) collective-permute-start(bf16[128,768]{1,0:T(8,128)(2,1)S(1)} %get-tuple-element.82), channel_id=1, source_target_pairs={{0,16},{8,24},{16,0},{24,8},{1,17},{9,25},{17,1},{25,9},{2,18},{10... | collective-permute-start | bytes 589832 | tf_op jit(solution)/shard_map/ppermute | solution.py:806
  116.9 9.2 %collective-permute-start.18 = (bf16[128,768]{1,0:T(8,128)(2,1)S(1)}, bf16[128,768]{1,0:T(8,128)(2,1)S(1)}, u32[]{:S(2)}, u32[]{:S(2)}) collective-permute-start(bf16[128,768]{1,0:T(8,128)(2,1)S(1)} %get-tuple-element.82), channel_id=1, source_target_pairs={{0,8},{8,16},{16,24},{24,0},{1,9},{9,17},{17,25},{25,1},{2,10},{10... | collective-permute-start | bytes 589832 | tf_op jit(solution)/shard_map/ppermute | solution.py:806
  132.9 8.0 %collective-permute-start.23 = (bf16[128,768]{1,0:T(8,128)(2,1)S(1)}, bf16[128,768]{1,0:T(8,128)(2,1)S(1)}, u32[]{:S(2)}, u32[]{:S(2)}) collective-permute-start(bf16[128,768]{1,0:T(8,128)(2,1)S(1)} %get-tuple-element.98), channel_id=1, source_target_pairs={{0,8},{8,16},{16,24},{24,0},{1,9},{9,17},{17,25},{25,1},{2,10},{10... | collective-permute-start | bytes 589832 | tf_op jit(solution)/shard_map/ppermute | solution.py:806
  133.3 9.6 %collective-permute-start.22 = (bf16[128,768]{1,0:T(8,128)(2,1)S(1)}, bf16[128,768]{1,0:T(8,128)(2,1)S(1)}, u32[]{:S(2)}, u32[]{:S(2)}) collective-permute-start(bf16[128,768]{1,0:T(8,128)(2,1)S(1)} %get-tuple-element.99), channel_id=1, source_target_pairs={{0,16},{8,24},{16,0},{24,8},{1,17},{9,25},{17,1},{25,9},{2,18},{10... | collective-permute-start | bytes 589832 | tf_op jit(solution)/shard_map/ppermute | solution.py:806
  134.4 8.4 %collective-permute-start.21 = (bf16[128,768]{1,0:T(8,128)(2,1)S(1)}, bf16[128,768]{1,0:T(8,128)(2,1)}, u32[]{:S(2)}, u32[]{:S(2)}) collective-permute-start(bf16[128,768]{1,0:T(8,128)(2,1)S(1)} %get-tuple-element.97.refs_1_), channel_id=1, source_target_pairs={{0,24},{8,0},{16,8},{24,16},{1,25},{9,1},{17,9},{25,17},{2,26},{10... | collective-permute-start | bytes 589832 | tf_op jit(solution)/shard_map/ppermute | solution.py:806
  137.0 9.0 %copy-start.14 = (bf16[4,4,2,24,768]{4,3,2,1,0:T(8,128)(2,1)S(1)}, bf16[4,4,2,24,768]{4,3,2,1,0:T(8,128)(2,1)}, u32[]{:S(2)}) copy-start(bf16[4,4,2,24,768]{4,3,2,1,0:T(8,128)(2,1)} %copy-done.13) | copy-start | bytes 3538948
  149.1 13.2 %copy-start.9 = (bf16[1024,256]{1,0:T(8,128)(2,1)S(1)}, bf16[1024,256]{1,0:T(8,128)(2,1)}, u32[]{:S(2)}) copy-start(bf16[1024,256]{1,0:T(8,128)(2,1)} %get-tuple-element.54.refs_2_) | copy-start | bytes 1572868
  149.1 13.2 %copy-start.10 = (bf16[1024,192]{1,0:T(8,128)(2,1)S(1)}, bf16[1024,192]{1,0:T(8,128)(2,1)}, u32[]{:S(2)}) copy-start(bf16[1024,192]{1,0:T(8,128)(2,1)} %get-tuple-element.55.refs_3_) | copy-start | bytes 1179652
  149.1 13.2 %copy-start.11 = (f32[192,512]{1,0:T(8,128)S(1)}, f32[192,512]{1,0:T(8,128)}, u32[]{:S(2)}) copy-start(f32[192,512]{1,0:T(8,128)} %get-tuple-element.56.refs_4_) | copy-start | bytes 1179652
  149.2 5.4 %collective-permute-start.27 = (bf16[4,4,24,768]{3,2,1,0:T(8,128)(2,1)S(1)}, bf16[4,4,24,768]{3,2,1,0:T(8,128)(2,1)}, u32[]{:S(2)}, u32[]{:S(2)}) collective-permute-start(bf16[4,4,24,768]{3,2,1,0:T(8,128)(2,1)S(1)} %dynamic-slice_bitcast_fusion), channel_id=1, source_target_pairs={{0,1},{1,0},{2,3},{3,2},{4,5},{5,4},{6,7},{7,6},{8,9},{9,8},{10,11... | collective-permute-start | bytes 1769480 | tf_op jit(solution)/shard_map/ppermute | solution.py:803
  149.2 13.1 %collective-permute-start.24 = (bf16[192,128]{1,0:T(8,128)(2,1)S(1)}, bf16[192,128]{1,0:T(8,128)(2,1)S(1)}, u32[]{:S(2)}, u32[]{:S(2)}) collective-permute-start(bf16[192,128]{1,0:T(8,128)(2,1)S(1)} %get-tuple-element.106.refs_1_), channel_id=1, source_target_pairs={{0,2},{1,3},{2,4},{3,5},{4,6},{5,7},{6,0},{7,1},{8,10},{9,11},{10,... | collective-permute-start | bytes 147464 | tf_op jit(solution)/shard_map/ppermute | solution.py:800
  150.6 9.9 %collective-permute-start.26 = (bf16[192,128]{1,0:T(8,128)(2,1)S(1)}, bf16[192,128]{1,0:T(8,128)(2,1)S(1)}, u32[]{:S(2)}, u32[]{:S(2)}) collective-permute-start(bf16[192,128]{1,0:T(8,128)(2,1)S(1)} %get-tuple-element.104), channel_id=1, source_target_pairs={{0,6},{1,7},{2,0},{3,1},{4,2},{5,3},{6,4},{7,5},{8,14},{9,15},{10,... | collective-permute-start | bytes 147464 | tf_op jit(solution)/shard_map/ppermute | solution.py:800
  153.1 9.2 %collective-permute-start.25 = (bf16[192,128]{1,0:T(8,128)(2,1)S(1)}, bf16[192,128]{1,0:T(8,128)(2,1)S(1)}, u32[]{:S(2)}, u32[]{:S(2)}) collective-permute-start(bf16[192,128]{1,0:T(8,128)(2,1)S(1)} %get-tuple-element.105), channel_id=1, source_target_pairs={{0,4},{1,5},{2,6},{3,7},{4,0},{5,1},{6,2},{7,3},{8,12},{9,13},{10,... | collective-permute-start | bytes 147464 | tf_op jit(solution)/shard_map/ppermute | solution.py:800
  156.8 16.1 %all-to-all-start.3 = ((bf16[4,4,24,768]{3,2,1,0:T(8,128)(2,1)}), bf16[4,4,24,768]{3,2,1,0:T(8,128)(2,1)S(1)}, u32[]{:S(2)}, u32[]{:S(2)}) async-start(bf16[4,4,24,768]{3,2,1,0:T(8,128)(2,1)} %fusion.5.refs_10_), calls=%async_computation.3 | async-start | bytes 1179648 | tf_op jit(solution)/shard_map/all_to_all | solution.py:830
  170.2 2.7 %collective-permute-start.28 = (bf16[512,384]{1,0:T(8,128)(2,1)}, bf16[512,384]{1,0:T(8,128)(2,1)S(1)}, u32[]{:S(2)}, u32[]{:S(2)}) collective-permute-start(bf16[512,384]{1,0:T(8,128)(2,1)} %get-tuple-element.59), channel_id=1, source_target_pairs={{0,1},{1,0},{2,3},{3,2},{4,5},{5,4},{6,7},{7,6},{8,9},{9,8},{10,11... | collective-permute-start | bytes 1179656 | tf_op jit(solution)/shard_map/ppermute | solution.py:803
  179.2 6.2 %copy-start.1 = (f32[16,32,576]{2,1,0:T(8,128)S(1)}, f32[16,32,576]{2,1,0:T(8,128)}, u32[]{:S(2)}) copy-start(f32[16,32,576]{2,1,0:T(8,128)} %get-tuple-element.61.refs_1_) | copy-start | bytes 3538948
  179.3 24.7 %all-to-all-start.4 = ((bf16[4,128,768]{2,1,0:T(8,128)(2,1)}), bf16[4,128,768]{2,1,0:T(8,128)(2,1)S(1)}, u32[]{:S(2)}, u32[]{:S(2)}) async-start(bf16[4,128,768]{2,1,0:T(8,128)(2,1)} %get-tuple-element.60), calls=%async_computation.4 | async-start | bytes 1572864 | tf_op jit(solution)/shard_map/all_to_all | solution.py:827
  183.0 2.4 %collective-permute-start.29 = (bf16[16,32,576]{2,1,0:T(8,128)(2,1)}, bf16[16,32,576]{2,1,0:T(8,128)(2,1)S(1)}, u32[]{:S(2)}, u32[]{:S(2)}) collective-permute-start(bf16[16,32,576]{2,1,0:T(8,128)(2,1)} %get-tuple-element.62), channel_id=1, source_target_pairs={{0,1},{1,0},{2,3},{3,2},{4,5},{5,4},{6,7},{7,6},{8,9},{9,8},{10,11... | collective-permute-start | bytes 1769480 | tf_op jit(solution)/shard_map/ppermute | solution.py:803
  186.9 17.0 %collective-permute-start.30 = (bf16[152,768]{1,0:T(8,128)(2,1)}, bf16[152,768]{1,0:T(8,128)(2,1)S(1)}, u32[]{:S(2)}, u32[]{:S(2)}) collective-permute-start(bf16[152,768]{1,0:T(8,128)(2,1)} %get-tuple-element.63), channel_id=1, source_target_pairs={{0,8},{8,16},{16,24},{24,0},{1,9},{9,17},{17,25},{25,1},{2,10},{10... | collective-permute-start | bytes 700424 | tf_op jit(solution)/shard_map/ppermute | solution.py:806
  189.4 14.5 %collective-permute-start.31 = (bf16[152,768]{1,0:T(8,128)(2,1)}, bf16[152,768]{1,0:T(8,128)(2,1)S(1)}, u32[]{:S(2)}, u32[]{:S(2)}) collective-permute-start(bf16[152,768]{1,0:T(8,128)(2,1)} %get-tuple-element.64), channel_id=1, source_target_pairs={{0,16},{8,24},{16,0},{24,8},{1,17},{9,25},{17,1},{25,9},{2,18},{10... | collective-permute-start | bytes 700424 | tf_op jit(solution)/shard_map/ppermute | solution.py:806
  189.4 14.5 %collective-permute-start.32 = (bf16[152,768]{1,0:T(8,128)(2,1)}, bf16[152,768]{1,0:T(8,128)(2,1)S(1)}, u32[]{:S(2)}, u32[]{:S(2)}) collective-permute-start(bf16[152,768]{1,0:T(8,128)(2,1)} %get-tuple-element.65), channel_id=1, source_target_pairs={{0,24},{8,0},{16,8},{24,16},{1,25},{9,1},{17,9},{25,17},{2,26},{10... | collective-permute-start | bytes 700424 | tf_op jit(solution)/shard_map/ppermute | solution.py:806
  191.0 13.1 %copy-start.20 = (f32[128,768]{1,0:T(8,128)S(1)}, f32[128,768]{1,0:T(8,128)}, u32[]{:S(2)}) copy-start(f32[128,768]{1,0:T(8,128)} %get-tuple-element.85) | copy-start | bytes 1179652
  205.8 4.5 %copy-start.2 = (bf16[1,192,768]{2,1,0:T(8,128)(2,1)S(1)}, bf16[1,192,768]{2,1,0:T(8,128)(2,1)}, u32[]{:S(2)}) copy-start(bf16[1,192,768]{2,1,0:T(8,128)(2,1)} %reduce-scatter.2.cloned.1.call-done) | copy-start | bytes 884740
  205.8 14.2 %all-to-all-start.5 = ((bf16[4,56,768]{2,1,0:T(8,128)(2,1)}), bf16[4,56,768]{2,1,0:T(8,128)(2,1)S(1)}, u32[]{:S(2)}, u32[]{:S(2)}) async-start(bf16[4,56,768]{2,1,0:T(8,128)(2,1)} %after.16), calls=%async_computation.6 | async-start | bytes 688128 | tf_op jit(solution)/shard_map/all_to_all | solution.py:827
  (18 other events, 24.4 us)
Sparse Core Ops, SparseCore 0:
  47.7 36.8 all-gather.2
  133.0 37.9 reduce-scatter.1
